TPU v7x, 32 devices: a whole 2x2x4 slice. The times are simulated.
32 devices in a mesh: grp: 2 (over x), tile: 8 (over z, y), depth: 2 (over core).
Axes of the slice: x: 2, y: 2, z: 4, core: 2. Of those that a mesh axis runs over, the one named last changes fastest.
Arguments:
- tracer_start: float32 [16, 8, 256, 256], P('grp', 'depth', 'tile'), parts along dimension 0, may hold values from -6 to 6
- velocity: float32 [4, 8, 256, 256], P('grp', 'depth', 'tile'), parts along dimension 0, may hold values from -3 to 3
- surface: float32 [512, 256], P(('grp', 'tile')), parts along dimension 0, may hold values from -6 to 6
- mixing: float32 [16, 256, 256], P(('grp', 'depth'), 'tile'), parts along dimension 0, may hold values from 0.05 to 2
- land_mask: int32 [8, 256, 256], P('depth', 'tile'), may hold values 0 or 1
- damping: float32 [256, 256], P('tile'), may hold values from 0.002 to 0.02
- tracer_cot: float32 [16, 8, 256, 256], P('grp', 'depth', 'tile'), parts along dimension 0, may hold values from -6 to 6
- surface_cot: float32 [512, 256], P(('grp', 'tile')), parts along dimension 0, may hold values from -5 to 5
Outputs:
- adj_tracer: float32 [16, 8, 256, 256], P('grp', 'depth', 'tile'), parts along dimension 0
- adj_velocity: float32 [4, 8, 256, 256], P('grp', 'depth', 'tile'), parts along dimension 0
- adj_surface: float32 [512, 256], P(('grp', 'tile')), parts along dimension 0
There are 2 independent parts, one for each index of `grp`. A program takes and returns all parts, laid end to end along the dimension named above; an argument that names none is the same for every part. Nothing has to cross between parts.
All inputs are finite; a program needn't handle non-finite values. No bound on the sum of `land_mask` on one device may be relied on, other than what follows from the above.
Results may differ from a plain program's by a relative error of at most 0.0003.
Values sent between devices are 32-bit elements; how exact they have to be, the bound alone decides.
No kernel may reach another device: no remote copies, remote signals or barrier semaphores. Data moves between devices by JAX's collectives and lax.ppermute only.
A program may use at most 64 MiB of HBM per device.

v0:
```python
import jax
import jax.numpy as jnp
from jax import lax
from jax.sharding import PartitionSpec as P

ITERS = 6


ADVECT = 0.25
DIFFUSE = 0.1
GRAVITY = 0.5


def with_halo(block, sides, width):
    for axis, dim in sides:
        count = lax.axis_size(axis)
        forward = [(i, i + 1) for i in range(count - 1)]
        backward = [(target, source) for source, target in forward]
        low = lax.ppermute(
            lax.slice_in_dim(block, block.shape[dim] - width, None, axis=dim), axis, forward
        )
        high = lax.ppermute(lax.slice_in_dim(block, 0, width, axis=dim), axis, backward)
        block = jnp.concatenate([low, block, high], axis=dim)
    return block


def next_col(field):
    return jnp.concatenate([field[..., 1:], jnp.zeros_like(field[..., :1])], axis=-1)


def prev_col(field):
    return jnp.concatenate([jnp.zeros_like(field[..., :1]), field[..., :-1]], axis=-1)


def thomas(values, coupling):
    count = coupling.shape[0]
    ratios = []
    partial_value = []
    for level in range(count):
        if level == 0:
            divisor = 1.0 + coupling[0]
            carried = values[..., 0, :, :] / divisor
        else:
            upper_link = coupling[level - 1]
            divisor = 1.0 + coupling[level] + upper_link - upper_link * ratios[level - 1]
            carried = (values[..., level, :, :] + upper_link * partial_value[level - 1]) / divisor
        ratios.append(coupling[level] / divisor)
        partial_value.append(carried)
    solved = [None] * count
    solved[count - 1] = partial_value[count - 1]
    for level in range(count - 2, -1, -1):
        solved[level] = partial_value[level] + ratios[level] * solved[level + 1]
    return jnp.stack(solved, axis=-3)


def vertical(values, mixing):
    stacked = jnp.concatenate([values, mixing[None]], axis=0)
    columns = lax.all_to_all(stacked, "depth", split_axis=3, concat_axis=1, tiled=True)
    column_mix = columns[-1]
    coupling = jnp.concatenate([column_mix[:-1], jnp.zeros_like(column_mix[:1])], axis=0)
    solved = thomas(columns[:-1], coupling)
    return lax.all_to_all(solved, "depth", split_axis=1, concat_axis=3, tiled=True)


def surface_op(field, damping):
    padded = with_halo(field, (("tile", 0),), 1)
    beside_all = padded[2:] + padded[:-2] + next_col(field) + prev_col(field)
    return (4.0 + damping) * field - beside_all


def squares(vector):
    return lax.psum(jnp.sum(vector * vector), "tile")


def solve_tiles(source, damping):
    solution = jnp.zeros_like(source)
    norm_now = squares(source)

    def advance(turn, carry):
        solution, residual, direction, norm_now = carry
        image = surface_op(direction, damping)
        alpha = norm_now / lax.psum(jnp.sum(direction * image), "tile")
        solution = solution + alpha * direction
        residual = residual - alpha * image
        norm_next = squares(residual)
        direction = residual + norm_next / norm_now * direction
        return (solution, residual, direction, norm_next)

    solution, residual, direction, norm_now = lax.fori_loop(
        0, ITERS, advance, (solution, source, source, norm_now)
    )
    return solution


def body(tracer_start, velocity, surface, mixing, land_mask, damping, tracer_cot, surface_cot):
    tracers, levels, row_count, col_count = tracer_start.shape
    settled = vertical(tracer_start, mixing)
    weighted = land_mask.astype(jnp.float32)[None] * tracer_cot
    stacked = jnp.concatenate(
        [weighted.reshape(tracers * levels, row_count, col_count), surface[None]], axis=0
    )
    padded = with_halo(stacked, (("tile", 1),), 1)
    weight_pad = padded[:-1].reshape(tracers, levels, row_count + 2, col_count)
    surf_pad = padded[-1]
    along_x = next_col(weighted) - prev_col(weighted)
    along_y = weight_pad[..., 2:, :] - weight_pad[..., :-2, :]
    spread = (
        weight_pad[..., 2:, :]
        + weight_pad[..., :-2, :]
        + next_col(weighted)
        + prev_col(weighted)
        - 4.0 * weighted
    )
    u_eff = velocity[0] - GRAVITY * (next_col(surface) - prev_col(surface))
    v_eff = velocity[1] - GRAVITY * (surf_pad[2:] - surf_pad[:-2])
    adj_settled = weighted + ADVECT * (u_eff * along_x + v_eff * along_y) + DIFFUSE * spread
    flux_x = ADVECT * jnp.sum(settled * along_x, axis=0)
    flux_y = ADVECT * jnp.sum(settled * along_y, axis=0)
    adj_tracer = vertical(adj_settled, mixing)
    column_terms = jnp.stack([jnp.sum(flux_x, axis=0), jnp.sum(flux_y, axis=0)])
    col_sums = lax.psum(column_terms, "depth")
    col_pad = with_halo(col_sums, (("tile", 1),), 1)
    source = surface_cot + GRAVITY * (
        next_col(col_sums[0]) - prev_col(col_sums[0]) + col_pad[1, 2:] - col_pad[1, :-2]
    )
    solution = solve_tiles(source, damping)
    sol_pad = with_halo(solution, (("tile", 0),), 1)
    adj_velocity = jnp.stack(
        [
            flux_x + ADVECT * (next_col(solution) - prev_col(solution)),
            flux_y + ADVECT * (sol_pad[2:] - sol_pad[:-2]),
        ]
    )
    return (adj_tracer, adj_velocity, solution)


def solution(mesh):
    return jax.shard_map(
        body,
        mesh=mesh,
        in_specs=(
            P("grp", "depth", "tile", None),
            P("grp", "depth", "tile", None),
            P(("grp", "tile"), None),
            P(("grp", "depth"), "tile", None),
            P("depth", "tile", None),
            P("tile", None),
            P("grp", "depth", "tile", None),
            P(("grp", "tile"), None),
        ),
        out_specs=(
            P("grp", "depth", "tile", None),
            P("grp", "depth", "tile", None),
            P(("grp", "tile"), None),
        ),
        check_vma=False,
    )
```

profile of v0, /device:TPU:0, one launch (start us, length us, event | category | flops | bytes accessed | tf_op | source)
XLA Modules:
  0.0 452.6 jit_solution(10976968627692519378)
XLA Ops:
  7.2 1.4 pad_maximum_fusion.2
  8.6 7.5 %copy.39 = f32[9,4,32,256]{2,0,1,3:T(8,128)} copy(f32[9,4,32,256]{3,2,1,0:T(8,128)S(1)} %pad_maximum_fusion.2) | data formatting | bytes 2359296 | tf_op jit(solution)/shard_map/concatenate | solution.py:57
  16.0 4.8 %reshape.52 = f32[2,1,147456]{2,1,0:T(1,128)S(1)} reshape(f32[256,4,9,32]{3,2,1,0:T(8,128)} %bitcast.133) | data formatting | bytes 2359296
  20.8 4.7 %all_to_all.66 = f32[2,1,147456]{2,1,0:T(1,128)S(1)} all-to-all(f32[2,1,147456]{2,1,0:T(1,128)S(1)} %reshape.52), channel_id=1, replica_groups=mesh['grp'=2,'tile'=8,'depth'=2] {'depth'}, dimensions={0} | all-to-all | bytes 2359296 | tf_op jit(solution)/shard_map/all_to_all | solution.py:58
  26.0 4.1 reduce
  30.1 6.3 %reshape.53 = f32[256,4,9,32]{3,2,1,0:T(8,128)} reshape(f32[2,147456]{1,0:T(2,128)S(1)} %reduce) | data formatting | bytes 2359296
  36.4 7.1 %copy.48 = f32[9,4,32,2,128]{4,3,2,1,0:T(2,128)S(1)} copy(f32[9,4,32,2,128]{2,0,1,4,3:T(8,128)} %bitcast.134) | data formatting | bytes 2359296 | tf_op jit(solution)/shard_map/all_to_all | solution.py:58
  44.4 1.1 copy.43
  45.5 3.7 all-to-all-start.3
  50.1 1.3 collective-permute-start.2
  51.4 5.7 %collective-permute-start.3 = (f32[33,1,256]{2,1,0:T(1,128)S(1)}, f32[33,1,256]{2,1,0:T(1,128)S(1)}, u32[]{:S(2)}, u32[]{:S(2)}) collective-permute-start(f32[33,1,256]{2,1,0:T(1,128)S(1)} %get-tuple-element.114), channel_id=1, source_target_pairs={{0,2},{2,4},{4,6},{6,8},{8,10},{10,12},{12,14},{1,3},{3,5},{5,7},{... | collective-permute-start | bytes 101384 | tf_op jit(solution)/shard_map/ppermute | solution.py:19
  57.2 1.7 fusion.61
  58.9 1.8 copy.45
  60.7 2.1 all_to_all.61
  62.8 0.9 copy-done.8
  64.0 1.0 copy-done.1
  65.3 1.5 multiply_reduce_fusion.3
  66.9 3.6 copy.32
  70.5 4.8 %reshape.50 = f32[2,1,147456]{2,1,0:T(1,128)S(1)} reshape(f32[256,9,4,32]{3,2,1,0:T(4,128)} %bitcast.135) | data formatting | bytes 2359296
  75.3 4.7 %all_to_all.67 = f32[2,1,147456]{2,1,0:T(1,128)S(1)} all-to-all(f32[2,1,147456]{2,1,0:T(1,128)S(1)} %reshape.50), channel_id=1, replica_groups=mesh['grp'=2,'tile'=8,'depth'=2] {'depth'}, dimensions={0} | all-to-all | bytes 2359296 | tf_op jit(solution)/shard_map/all_to_all | solution.py:58
  80.0 4.1 reduce.1
  84.1 4.9 %reshape.51 = f32[256,9,4,32]{3,2,1,0:T(4,128)} reshape(f32[2,147456]{1,0:T(2,128)S(1)} %reduce.1) | data formatting | bytes 2359296
  89.0 4.9 %copy.46 = f32[9,4,32,2,128]{4,3,2,1,0:T(2,128)S(1)} copy(f32[9,4,32,2,128]{2,1,0,4,3:T(4,128)} %bitcast.136) | data formatting | bytes 2359296 | tf_op jit(solution)/shard_map/all_to_all | solution.py:58
  96.3 4.6 %all_to_all.68 = f32[8,8,32,128]{3,2,0,1:T(8,128)S(1)} all-to-all(f32[8,8,32,128]{3,2,0,1:T(8,128)S(1)} %copy.36), channel_id=1, replica_groups=mesh['grp'=2,'tile'=8,'depth'=2] {'depth'}, dimensions={1} | all-to-all | bytes 2097152 | tf_op jit(solution)/shard_map/all_to_all | solution.py:62
  101.8 1.8 all_to_all.54
  103.6 11.4 %all-reduce.12.cloned.1.call-done = f32[2,32,256]{2,1,0:T(8,128)} async-done(((f32[2,32,256]{2,1,0:T(8,128)}), f32[2,32,256]{2,1,0:T(8,128)}) %all-reduce.12.cloned.1.call-update) | async-done | bytes 65552 | tf_op jit(solution)/shard_map/psum | solution.py:121
  115.7 1.3 collective-permute-start.4
  117.0 4.5 %collective-permute-start.5 = (f32[2,1,256]{2,1,0:T(1,128)S(1)}, f32[2,1,256]{2,1,0:T(1,128)S(1)}, u32[]{:S(2)}, u32[]{:S(2)}) collective-permute-start(f32[2,1,256]{2,1,0:T(1,128)S(1)} %get-tuple-element.149), channel_id=1, source_target_pairs={{0,2},{2,4},{4,6},{6,8},{8,10},{10,12},{12,14},{1,3},{3,5},{5,7},{... | collective-permute-start | bytes 6152 | tf_op jit(solution)/shard_map/ppermute | solution.py:19
  122.9 1.5 multiply_reduce_fusion.6
  124.4 23.0 %psum.29 = f32[]{:T(128)} all-reduce(f32[]{:T(128)} %get-tuple-element.75), channel_id=1, replica_groups=mesh['grp'=2,'tile'=8,'depth'=2] {'tile'}, use_global_device_ids=true, to_apply=%region_6.0 | all-reduce | flops 1 | bytes 8 | tf_op jit(solution)/shard_map/psum | solution.py:72
  147.4 290.3 %while.17 = (s32[]{:T(128)}, f32[32,256]{1,0:T(8,128)S(1)}, f32[32,256]{1,0:T(8,128)S(1)}, f32[32,256]{1,0:T(8,128)S(1)}, f32[]{:T(128)}, /*index=5*/f32[32,256]{1,0:T(8,128)S(1)}, s32[]{:T(128)}, s32[]{:T(128)}) while((s32[]{:T(128)}, f32[32,256]{1,0:T(8,128)S(1)}, f32[32,256]{1,0:T(8,128)S(1)}, f32[32,256]{1,0:T(8,128)S(1)}, ...), condition=%wide.region_12.0_spmd.clone, body=%wide.region_7.0_spmd.clone.sunk | while | flops 155653 | bytes 570867 | solution.py:89
  147.4 1.5 collective-permute-start
  149.0 1.3 collective-permute-start.1
  151.0 3.4 collective-permute-done.1
  155.1 19.2 %psum.34 = f32[]{:T(128)} all-reduce(f32[]{:T(128)} %get-tuple-element.212), channel_id=1, replica_groups=mesh['grp'=2,'tile'=8,'depth'=2] {'tile'}, use_global_device_ids=true, to_apply=%region_9.0 | all-reduce | flops 1 | bytes 8 | tf_op jit(solution)/shard_map/while/body/eval_jaxpr/psum | solution.py:82
  175.7 18.3 %psum.35 = f32[]{:T(128)} all-reduce(f32[]{:T(128)} %get-tuple-element.214), channel_id=1, replica_groups=mesh['grp'=2,'tile'=8,'depth'=2] {'tile'}, use_global_device_ids=true, to_apply=%region_11.0 | all-reduce | flops 1 | bytes 8 | tf_op jit(solution)/shard_map/while/body/eval_jaxpr/psum | solution.py:72
  194.6 3.4 collective-permute-start
  198.0 1.3 collective-permute-start.1
  200.1 3.4 collective-permute-done.1
  204.2 18.7 %psum.34 = f32[]{:T(128)} all-reduce(f32[]{:T(128)} %get-tuple-element.212), channel_id=1, replica_groups=mesh['grp'=2,'tile'=8,'depth'=2] {'tile'}, use_global_device_ids=true, to_apply=%region_9.0 | all-reduce | flops 1 | bytes 8 | tf_op jit(solution)/shard_map/while/body/eval_jaxpr/psum | solution.py:82
  224.1 18.8 %psum.35 = f32[]{:T(128)} all-reduce(f32[]{:T(128)} %get-tuple-element.214), channel_id=1, replica_groups=mesh['grp'=2,'tile'=8,'depth'=2] {'tile'}, use_global_device_ids=true, to_apply=%region_11.0 | all-reduce | flops 1 | bytes 8 | tf_op jit(solution)/shard_map/while/body/eval_jaxpr/psum | solution.py:72
  243.7 2.9 collective-permute-start
  246.6 1.3 collective-permute-start.1
  248.6 3.4 collective-permute-done.1
  252.7 18.7 %psum.34 = f32[]{:T(128)} all-reduce(f32[]{:T(128)} %get-tuple-element.212), channel_id=1, replica_groups=mesh['grp'=2,'tile'=8,'depth'=2] {'tile'}, use_global_device_ids=true, to_apply=%region_9.0 | all-reduce | flops 1 | bytes 8 | tf_op jit(solution)/shard_map/while/body/eval_jaxpr/psum | solution.py:82
  272.7 18.8 %psum.35 = f32[]{:T(128)} all-reduce(f32[]{:T(128)} %get-tuple-element.214), channel_id=1, replica_groups=mesh['grp'=2,'tile'=8,'depth'=2] {'tile'}, use_global_device_ids=true, to_apply=%region_11.0 | all-reduce | flops 1 | bytes 8 | tf_op jit(solution)/shard_map/while/body/eval_jaxpr/psum | solution.py:72
  292.2 2.9 collective-permute-start
  295.1 1.3 collective-permute-start.1
  297.1 3.4 collective-permute-done.1
  301.2 18.7 %psum.34 = f32[]{:T(128)} all-reduce(f32[]{:T(128)} %get-tuple-element.212), channel_id=1, replica_groups=mesh['grp'=2,'tile'=8,'depth'=2] {'tile'}, use_global_device_ids=true, to_apply=%region_9.0 | all-reduce | flops 1 | bytes 8 | tf_op jit(solution)/shard_map/while/body/eval_jaxpr/psum | solution.py:82
  321.2 18.8 %psum.35 = f32[]{:T(128)} all-reduce(f32[]{:T(128)} %get-tuple-element.214), channel_id=1, replica_groups=mesh['grp'=2,'tile'=8,'depth'=2] {'tile'}, use_global_device_ids=true, to_apply=%region_11.0 | all-reduce | flops 1 | bytes 8 | tf_op jit(solution)/shard_map/while/body/eval_jaxpr/psum | solution.py:72
  340.7 2.9 collective-permute-start
  343.6 1.3 collective-permute-start.1
  345.7 3.4 collective-permute-done.1
  349.8 18.7 %psum.34 = f32[]{:T(128)} all-reduce(f32[]{:T(128)} %get-tuple-element.212), channel_id=1, replica_groups=mesh['grp'=2,'tile'=8,'depth'=2] {'tile'}, use_global_device_ids=true, to_apply=%region_9.0 | all-reduce | flops 1 | bytes 8 | tf_op jit(solution)/shard_map/while/body/eval_jaxpr/psum | solution.py:82
  369.7 18.8 %psum.35 = f32[]{:T(128)} all-reduce(f32[]{:T(128)} %get-tuple-element.214), channel_id=1, replica_groups=mesh['grp'=2,'tile'=8,'depth'=2] {'tile'}, use_global_device_ids=true, to_apply=%region_11.0 | all-reduce | flops 1 | bytes 8 | tf_op jit(solution)/shard_map/while/body/eval_jaxpr/psum | solution.py:72
  389.3 2.9 collective-permute-start
  392.1 1.3 collective-permute-start.1
  394.2 3.4 collective-permute-done.1
  398.3 18.7 %psum.34 = f32[]{:T(128)} all-reduce(f32[]{:T(128)} %get-tuple-element.212), channel_id=1, replica_groups=mesh['grp'=2,'tile'=8,'depth'=2] {'tile'}, use_global_device_ids=true, to_apply=%region_9.0 | all-reduce | flops 1 | bytes 8 | tf_op jit(solution)/shard_map/while/body/eval_jaxpr/psum | solution.py:82
  418.2 18.8 %psum.35 = f32[]{:T(128)} all-reduce(f32[]{:T(128)} %get-tuple-element.214), channel_id=1, replica_groups=mesh['grp'=2,'tile'=8,'depth'=2] {'tile'}, use_global_device_ids=true, to_apply=%region_11.0 | all-reduce | flops 1 | bytes 8 | tf_op jit(solution)/shard_map/while/body/eval_jaxpr/psum | solution.py:72
  437.9 1.3 collective-permute-start.6
  439.2 4.5 %collective-permute-start.7 = (f32[1,256]{1,0:T(1,128)S(1)}, f32[1,256]{1,0:T(1,128)S(1)}, u32[]{:S(2)}, u32[]{:S(2)}) collective-permute-start(f32[1,256]{1,0:T(1,128)S(1)} %get-tuple-element.153), channel_id=1, source_target_pairs={{0,2},{2,4},{4,6},{6,8},{8,10},{10,12},{12,14},{1,3},{3,5},{5,7},{... | collective-permute-start | bytes 3080 | tf_op jit(solution)/shard_map/ppermute | solution.py:19
  443.8 1.2 collective-permute-done.7
  (122 shorter events, 17.3 us)
Async XLA Ops:
  45.5 3.8 copy-start.9
  45.5 3.8 copy-start
  45.5 13.4 %all-to-all-start.3 = ((f32[8,8,32,128]{3,2,0,1:T(8,128)}), f32[8,8,32,128]{3,2,0,1:T(8,128)S(1)}, u32[]{:S(2)}, u32[]{:S(2)}) async-start(f32[8,8,32,128]{3,2,0,1:T(8,128)} %copy.43), calls=%async_computation.3 | async-start | bytes 2097152 | tf_op jit(solution)/shard_map/all_to_all | solution.py:62
  49.2 65.8 %all-reduce.12.cloned.1.call-start = ((), (), s32[]{:S(2)}) async-start(), calls=%async_computation.4 | async-start | bytes 131072 | tf_op jit(solution)/shard_map/psum | solution.py:121
  49.3 0.8 copy-start.5
  50.1 12.7 %collective-permute-start.2 = (f32[33,1,256]{2,1,0:T(1,128)S(1)}, f32[33,1,256]{2,1,0:T(1,128)S(1)}, u32[]{:S(2)}, u32[]{:S(2)}) collective-permute-start(f32[33,1,256]{2,1,0:T(1,128)S(1)} %get-tuple-element.115), channel_id=1, source_target_pairs={{2,0},{4,2},{6,4},{8,6},{10,8},{12,10},{14,12},{3,1},{5,3},{7,5},{... | collective-permute-start | bytes 101384 | tf_op jit(solution)/shard_map/ppermute | solution.py:22
  51.4 11.4 %collective-permute-start.3 = (f32[33,1,256]{2,1,0:T(1,128)S(1)}, f32[33,1,256]{2,1,0:T(1,128)S(1)}, u32[]{:S(2)}, u32[]{:S(2)}) collective-permute-start(f32[33,1,256]{2,1,0:T(1,128)S(1)} %get-tuple-element.114), channel_id=1, source_target_pairs={{0,2},{2,4},{4,6},{6,8},{8,10},{10,12},{12,14},{1,3},{3,5},{5,7},{... | collective-permute-start | bytes 101384 | tf_op jit(solution)/shard_map/ppermute | solution.py:19
  62.8 1.0 copy-start.8
  63.8 1.2 copy-start.1
  63.8 1.5 copy-start.2
  65.3 1.5 copy-start.7
  93.9 0.9 copy-start.4
  101.7 21.1 %copy-start.10 = (f32[32,256]{1,0:T(8,128)S(1)}, f32[32,256]{1,0:T(8,128)}, u32[]{:S(2)}) copy-start(f32[32,256]{1,0:T(8,128)} %param.17) | copy-start | bytes 98308
  101.7 45.7 %copy-start.6 = (f32[32,256]{1,0:T(8,128)S(1)}, f32[32,256]{1,0:T(8,128)}, u32[]{:S(2)}) copy-start(f32[32,256]{1,0:T(8,128)} %param.15) | copy-start | bytes 98308
  115.7 6.7 %collective-permute-start.4 = (f32[2,1,256]{2,1,0:T(1,128)S(1)}, f32[2,1,256]{2,1,0:T(1,128)S(1)}, u32[]{:S(2)}, u32[]{:S(2)}) collective-permute-start(f32[2,1,256]{2,1,0:T(1,128)S(1)} %get-tuple-element.148), channel_id=1, source_target_pairs={{2,0},{4,2},{6,4},{8,6},{10,8},{12,10},{14,12},{3,1},{5,3},{7,5},{... | collective-permute-start | bytes 6152 | tf_op jit(solution)/shard_map/ppermute | solution.py:22
  117.0 5.8 %collective-permute-start.5 = (f32[2,1,256]{2,1,0:T(1,128)S(1)}, f32[2,1,256]{2,1,0:T(1,128)S(1)}, u32[]{:S(2)}, u32[]{:S(2)}) collective-permute-start(f32[2,1,256]{2,1,0:T(1,128)S(1)} %get-tuple-element.149), channel_id=1, source_target_pairs={{0,2},{2,4},{4,6},{6,8},{8,10},{10,12},{12,14},{1,3},{3,5},{5,7},{... | collective-permute-start | bytes 6152 | tf_op jit(solution)/shard_map/ppermute | solution.py:19
  147.4 3.6 collective-permute-start
  149.0 5.5 %collective-permute-start.1 = (f32[1,256]{1,0:T(1,128)S(1)}, f32[1,256]{1,0:T(1,128)S(1)}, u32[]{:S(2)}, u32[]{:S(2)}) collective-permute-start(f32[1,256]{1,0:T(1,128)S(1)} %get-tuple-element.210), channel_id=1, source_target_pairs={{2,0},{4,2},{6,4},{8,6},{10,8},{12,10},{14,12},{3,1},{5,3},{7,5},{... | collective-permute-start | bytes 3080 | tf_op jit(solution)/shard_map/while/body/eval_jaxpr/ppermute | solution.py:22
  194.6 5.4 %collective-permute-start = (f32[1,256]{1,0:T(1,128)S(1)}, f32[1,256]{1,0:T(1,128)S(1)}, u32[]{:S(2)}, u32[]{:S(2)}) collective-permute-start(f32[1,256]{1,0:T(1,128)S(1)} %get-tuple-element.209), channel_id=1, source_target_pairs={{0,2},{2,4},{4,6},{6,8},{8,10},{10,12},{12,14},{1,3},{3,5},{5,7},{... | collective-permute-start | bytes 3080 | tf_op jit(solution)/shard_map/while/body/eval_jaxpr/ppermute | solution.py:19
  198.0 5.5 %collective-permute-start.1 = (f32[1,256]{1,0:T(1,128)S(1)}, f32[1,256]{1,0:T(1,128)S(1)}, u32[]{:S(2)}, u32[]{:S(2)}) collective-permute-start(f32[1,256]{1,0:T(1,128)S(1)} %get-tuple-element.210), channel_id=1, source_target_pairs={{2,0},{4,2},{6,4},{8,6},{10,8},{12,10},{14,12},{3,1},{5,3},{7,5},{... | collective-permute-start | bytes 3080 | tf_op jit(solution)/shard_map/while/body/eval_jaxpr/ppermute | solution.py:22
  243.7 4.9 %collective-permute-start = (f32[1,256]{1,0:T(1,128)S(1)}, f32[1,256]{1,0:T(1,128)S(1)}, u32[]{:S(2)}, u32[]{:S(2)}) collective-permute-start(f32[1,256]{1,0:T(1,128)S(1)} %get-tuple-element.209), channel_id=1, source_target_pairs={{0,2},{2,4},{4,6},{6,8},{8,10},{10,12},{12,14},{1,3},{3,5},{5,7},{... | collective-permute-start | bytes 3080 | tf_op jit(solution)/shard_map/while/body/eval_jaxpr/ppermute | solution.py:19
  246.6 5.5 %collective-permute-start.1 = (f32[1,256]{1,0:T(1,128)S(1)}, f32[1,256]{1,0:T(1,128)S(1)}, u32[]{:S(2)}, u32[]{:S(2)}) collective-permute-start(f32[1,256]{1,0:T(1,128)S(1)} %get-tuple-element.210), channel_id=1, source_target_pairs={{2,0},{4,2},{6,4},{8,6},{10,8},{12,10},{14,12},{3,1},{5,3},{7,5},{... | collective-permute-start | bytes 3080 | tf_op jit(solution)/shard_map/while/body/eval_jaxpr/ppermute | solution.py:22
  292.2 4.9 %collective-permute-start = (f32[1,256]{1,0:T(1,128)S(1)}, f32[1,256]{1,0:T(1,128)S(1)}, u32[]{:S(2)}, u32[]{:S(2)}) collective-permute-start(f32[1,256]{1,0:T(1,128)S(1)} %get-tuple-element.209), channel_id=1, source_target_pairs={{0,2},{2,4},{4,6},{6,8},{8,10},{10,12},{12,14},{1,3},{3,5},{5,7},{... | collective-permute-start | bytes 3080 | tf_op jit(solution)/shard_map/while/body/eval_jaxpr/ppermute | solution.py:19
  295.1 5.5 %collective-permute-start.1 = (f32[1,256]{1,0:T(1,128)S(1)}, f32[1,256]{1,0:T(1,128)S(1)}, u32[]{:S(2)}, u32[]{:S(2)}) collective-permute-start(f32[1,256]{1,0:T(1,128)S(1)} %get-tuple-element.210), channel_id=1, source_target_pairs={{2,0},{4,2},{6,4},{8,6},{10,8},{12,10},{14,12},{3,1},{5,3},{7,5},{... | collective-permute-start | bytes 3080 | tf_op jit(solution)/shard_map/while/body/eval_jaxpr/ppermute | solution.py:22
  340.7 4.9 %collective-permute-start = (f32[1,256]{1,0:T(1,128)S(1)}, f32[1,256]{1,0:T(1,128)S(1)}, u32[]{:S(2)}, u32[]{:S(2)}) collective-permute-start(f32[1,256]{1,0:T(1,128)S(1)} %get-tuple-element.209), channel_id=1, source_target_pairs={{0,2},{2,4},{4,6},{6,8},{8,10},{10,12},{12,14},{1,3},{3,5},{5,7},{... | collective-permute-start | bytes 3080 | tf_op jit(solution)/shard_map/while/body/eval_jaxpr/ppermute | solution.py:19
  343.6 5.5 %collective-permute-start.1 = (f32[1,256]{1,0:T(1,128)S(1)}, f32[1,256]{1,0:T(1,128)S(1)}, u32[]{:S(2)}, u32[]{:S(2)}) collective-permute-start(f32[1,256]{1,0:T(1,128)S(1)} %get-tuple-element.210), channel_id=1, source_target_pairs={{2,0},{4,2},{6,4},{8,6},{10,8},{12,10},{14,12},{3,1},{5,3},{7,5},{... | collective-permute-start | bytes 3080 | tf_op jit(solution)/shard_map/while/body/eval_jaxpr/ppermute | solution.py:22
  389.3 4.9 %collective-permute-start = (f32[1,256]{1,0:T(1,128)S(1)}, f32[1,256]{1,0:T(1,128)S(1)}, u32[]{:S(2)}, u32[]{:S(2)}) collective-permute-start(f32[1,256]{1,0:T(1,128)S(1)} %get-tuple-element.209), channel_id=1, source_target_pairs={{0,2},{2,4},{4,6},{6,8},{8,10},{10,12},{12,14},{1,3},{3,5},{5,7},{... | collective-permute-start | bytes 3080 | tf_op jit(solution)/shard_map/while/body/eval_jaxpr/ppermute | solution.py:19
  392.1 5.5 %collective-permute-start.1 = (f32[1,256]{1,0:T(1,128)S(1)}, f32[1,256]{1,0:T(1,128)S(1)}, u32[]{:S(2)}, u32[]{:S(2)}) collective-permute-start(f32[1,256]{1,0:T(1,128)S(1)} %get-tuple-element.210), channel_id=1, source_target_pairs={{2,0},{4,2},{6,4},{8,6},{10,8},{12,10},{14,12},{3,1},{5,3},{7,5},{... | collective-permute-start | bytes 3080 | tf_op jit(solution)/shard_map/while/body/eval_jaxpr/ppermute | solution.py:22
  437.8 8.0 %copy-start.3 = (f32[32,256]{1,0:T(8,128)}, f32[32,256]{1,0:T(8,128)S(1)}, u32[]{:S(2)}) copy-start(f32[32,256]{1,0:T(8,128)S(1)} %get-tuple-element.34) | copy-start | bytes 98308
  437.9 5.9 %collective-permute-start.6 = (f32[1,256]{1,0:T(1,128)S(1)}, f32[1,256]{1,0:T(1,128)S(1)}, u32[]{:S(2)}, u32[]{:S(2)}) collective-permute-start(f32[1,256]{1,0:T(1,128)S(1)} %get-tuple-element.152), channel_id=1, source_target_pairs={{2,0},{4,2},{6,4},{8,6},{10,8},{12,10},{14,12},{3,1},{5,3},{7,5},{... | collective-permute-start | bytes 3080 | tf_op jit(solution)/shard_map/ppermute | solution.py:22
  439.2 5.8 %collective-permute-start.7 = (f32[1,256]{1,0:T(1,128)S(1)}, f32[1,256]{1,0:T(1,128)S(1)}, u32[]{:S(2)}, u32[]{:S(2)}) collective-permute-start(f32[1,256]{1,0:T(1,128)S(1)} %get-tuple-element.153), channel_id=1, source_target_pairs={{0,2},{2,4},{4,6},{6,8},{8,10},{10,12},{12,14},{1,3},{3,5},{5,7},{... | collective-permute-start | bytes 3080 | tf_op jit(solution)/shard_map/ppermute | solution.py:19
Sparse Core Ops, SparseCore 0:
  95.6 19.3 all-reduce.11
where the time goes:
time: 455 us; the launch traced here: 453 us
  blocking collectives  262 us (58%)
  local copies, waits for them, and re-layouts  60.1 us (13%)
  starting transfers between devices  46.5 us (10%)
  waiting for transfers between devices  33.6 us (7%)
  other arithmetic  23.5 us (5%)
  between operations  14.6 us (3%)
  loops' own time  12.4 us (3%)
    psum x7, blocking collectives, squares(): return lax.psum(jnp.sum(vector * vector), 'tile')  136 us
    psum x6, blocking collectives, advance(): alpha = norm_now / lax.psum(jnp.sum(direction * image), 'tile')  112 us
    ppermute x9, starting transfers between devices, with_halo(): lax.ppermute(lax.slice_in_dim(block, block.shape[dim] - width, None, axis...  31.1 us
    unnamed x33, local copies, waits for them, and re-layouts  24.5 us
    ppermute x9, waiting for transfers between devices, with_halo(): lax.ppermute(lax.slice_in_dim(block, 0, width, axis=dim), axis, backward)  20.5 us
    all_to_all x3, local copies, waits for them, and re-layouts, vertical(): lax.all_to_all(stacked, 'depth', split_axis=3, concat_axis=1, tiled=True)  12.5 us
    another operation x1, loops' own time, solve_tiles(): lax.fori_loop(0, ITERS, advance, (solution, source, source, norm_now))  12.4 us
    ppermute x9, starting transfers between devices, with_halo(): lax.ppermute(lax.slice_in_dim(block, 0, width, axis=dim), axis, backward)  11.6 us
  transfers between devices with their start and end apart: 20, of which 9 were waited for; matrix products, arithmetic and copies ran while one was open for 1% of the time, Pallas kernels for 0%

commit v1 on v0

v1 whole, which is shorter than its diff:
```python
import functools

import jax
import jax.numpy as jnp
from jax import lax
from jax.experimental import pallas as pl
from jax.experimental.pallas import tpu as pltpu
from jax.sharding import PartitionSpec as P

ITERS = 6
ADVECT = 0.25
DIFFUSE = 0.1
GRAVITY = 0.5

F32 = jnp.float32
VMEM = pl.BlockSpec(memory_space=pltpu.VMEM)


def call(kernel, outs, args, scratch=(), flops=2_000_000):
    nbytes = sum(a.size * 4 for a in args) + sum(4 * functools.reduce(lambda p, q: p * q, s) for s in outs)
    return pl.pallas_call(
        kernel,
        out_shape=[jax.ShapeDtypeStruct(s, F32) for s in outs],
        in_specs=[VMEM] * len(args),
        out_specs=[VMEM] * len(outs),
        scratch_shapes=list(scratch),
        cost_estimate=pl.CostEstimate(flops=flops, bytes_accessed=nbytes, transcendentals=0),
        compiler_params=pltpu.CompilerParams(vmem_limit_bytes=40 * 1024 * 1024),
    )(*args)


def lane_shifts(f):
    lane = lax.broadcasted_iota(jnp.int32, f.shape, f.ndim - 1)
    cols = f.shape[-1]
    after = jnp.where(lane == cols - 1, 0.0, pltpu.roll(f, cols - 1, f.ndim - 1))
    before = jnp.where(lane == 0, 0.0, pltpu.roll(f, 1, f.ndim - 1))
    return after, before


def row_shifts(f, low, high):
    row = lax.broadcasted_iota(jnp.int32, f.shape, 0)
    rows = f.shape[0]
    after = jnp.where(row == rows - 1, high, pltpu.roll(f, rows - 1, 0))
    before = jnp.where(row == 0, low, pltpu.roll(f, 1, 0))
    return after, before


def chain(mix_ref, depth):
    levels = mix_ref.shape[0]
    links = [mix_ref[j + depth * (levels - 2 - 2 * j)] for j in range(levels - 1)]
    rest = jnp.ones_like(links[0])
    inverse, ratio = [], []
    for link in links:
        inv = 1.0 / (rest + link)
        inverse.append(inv)
        ratio.append(link * inv)
        rest = 1.0 + link * (rest * inv)
    return inverse, ratio, rest


def level(j, depth, levels):
    return j + depth * (levels - 1 - 2 * j)


def meet(rest, other_rest, own_mix, other_mix, depth):
    link = jnp.where(depth == 0, own_mix, other_mix)
    det = rest * other_rest + link * (rest + other_rest)
    inv = 1.0 / det
    return (other_rest + link) * inv, link * inv


def start_kernel(tracer, mix, cot, mask, surface, face, edge_a, edge_b):
    tracers, levels, rows, _ = tracer.shape
    depth = lax.axis_index("depth")
    odd = lax.rem(lax.axis_index("tile"), 2) == 1
    _, ratio, rest = chain(mix, depth)
    for tr in range(tracers):
        num = tracer[tr, level(0, depth, levels)]
        for j in range(1, levels):
            num = tracer[tr, level(j, depth, levels)] + ratio[j - 1] * num
        face[tr] = num
    face[tracers] = rest
    face[tracers + 1] = mix[levels - 1]
    for lev in range(levels):
        first_mask = mask[lev, 0:1].astype(F32)
        last_mask = mask[lev, rows - 1 : rows].astype(F32)
        for tr in range(tracers):
            first = cot[tr, lev, 0:1] * first_mask
            last = cot[tr, lev, rows - 1 : rows] * last_mask
            at = tr * levels + lev
            edge_a[at : at + 1] = jnp.where(odd, first, last)
            edge_b[at : at + 1] = jnp.where(odd, last, first)
    at = tracers * levels
    edge_a[at : at + 1] = jnp.where(odd, surface[0:1], surface[rows - 1 : rows])
    edge_b[at : at + 1] = jnp.where(odd, surface[rows - 1 : rows], surface[0:1])


def flux_kernel(tracer, mix, cot, mask, face, other, edge_a, edge_b, surface_cot, damping, flux, send):
    tracers, levels, rows, cols = tracer.shape
    depth = lax.axis_index("depth")
    odd = lax.rem(lax.axis_index("tile"), 2) == 1
    inverse, ratio, rest = chain(mix, depth)
    own_w, other_w = meet(rest, other[tracers], mix[levels - 1], other[tracers + 1], depth)
    col_x = jnp.zeros((rows, cols), F32)
    col_y = jnp.zeros((rows, cols), F32)
    flux[...] = jnp.zeros_like(flux)
    for tr in range(tracers):
        nums = [tracer[tr, level(0, depth, levels)]]
        for j in range(1, levels):
            nums.append(tracer[tr, level(j, depth, levels)] + ratio[j - 1] * nums[-1])
        value = own_w * nums[-1] + other_w * other[tr]
        for j in range(levels - 1, -1, -1):
            lev = level(j, depth, levels)
            if j < levels - 1:
                value = inverse[j] * nums[j] + ratio[j] * value
            weighted = cot[tr, lev] * mask[lev].astype(F32)
            at = tr * levels + lev
            row_a, row_b = edge_a[pl.ds(at, 1)], edge_b[pl.ds(at, 1)]
            low, high = jnp.where(odd, row_a, row_b), jnp.where(odd, row_b, row_a)
            right, left = lane_shifts(weighted)
            down, up = row_shifts(weighted, low, high)
            flux[0, lev] += ADVECT * (value * (right - left))
            flux[1, lev] += ADVECT * (value * (down - up))
    for lev in range(levels):
        col_x += flux[0, lev]
        col_y += flux[1, lev]
    right, left = lane_shifts(col_x)
    down, up = row_shifts(col_y, 0.0, 0.0)
    top = depth == 0
    source = GRAVITY * (right - left + down - up)
    send[0:rows] = source + jnp.where(top, surface_cot[...], 0.0)
    send[rows : rows + 8] = jnp.zeros((8, cols), F32)
    send[rows : rows + 1] = col_y[0:1]
    send[rows + 1 : rows + 2] = col_y[rows - 1 : rows]
    send[rows + 8 : 2 * rows + 8] = jnp.where(top, damping[...], 0.0)


def adjoint_kernel(mix, cot, mask, velocity, surface, edge_a, edge_b, nums):
    tracers, levels, rows, cols = cot.shape
    depth = lax.axis_index("depth")
    odd = lax.rem(lax.axis_index("tile"), 2) == 1
    _, ratio, _ = chain(mix, depth)
    at = tracers * levels
    row_a, row_b = edge_a[at : at + 1], edge_b[at : at + 1]
    low, high = jnp.where(odd, row_a, row_b), jnp.where(odd, row_b, row_a)
    right, left = lane_shifts(surface[...])
    down, up = row_shifts(surface[...], low, high)
    slope_x, slope_y = GRAVITY * (right - left), GRAVITY * (down - up)
    for j in range(levels):
        lev = level(j, depth, levels)
        u_eff = ADVECT * (velocity[0, lev] - slope_x)
        v_eff = ADVECT * (velocity[1, lev] - slope_y)
        wet = mask[lev].astype(F32)
        for tr in range(tracers):
            weighted = cot[tr, lev] * wet
            at = tr * levels + lev
            row_a, row_b = edge_a[pl.ds(at, 1)], edge_b[pl.ds(at, 1)]
            low, high = jnp.where(odd, row_a, row_b), jnp.where(odd, row_b, row_a)
            right, left = lane_shifts(weighted)
            down, up = row_shifts(weighted, low, high)
            out = (
                weighted
                + (u_eff * (right - left) + v_eff * (down - up))
                + DIFFUSE * (down + up + right + left - 4.0 * weighted)
            )
            if j > 0:
                out = out + ratio[j - 1] * nums[j - 1, tr]
            nums[j, tr] = out


def finish_kernel(mix, nums, face, other, other_nums, adj_tracer):
    tracers, levels, rows, cols = adj_tracer.shape
    depth = lax.axis_index("depth")
    inverse, ratio, rest = chain(mix, depth)
    own_w, other_w = meet(rest, other[tracers], mix[levels - 1], other[tracers + 1], depth)
    for tr in range(tracers):
        value = own_w * nums[levels - 1, tr] + other_w * other_nums[tr]
        adj_tracer[tr, level(levels - 1, depth, levels)] = value
        for j in range(levels - 2, -1, -1):
            value = inverse[j] * nums[j, tr] + ratio[j] * value
            adj_tracer[tr, level(j, depth, levels)] = value


def solve_kernel(tiles, partners, flux, own, *refs):
    steps = len(partners)
    got, swapped = refs[:steps], refs[steps : 2 * steps]
    adj_velocity, adj_surface, src, damp, edges, direc, image, sol = refs[2 * steps :]
    levels, rows, cols = flux.shape[1:]
    me = lax.axis_index("tile")
    depth = lax.axis_index("depth")

    edges[0:8] = jnp.zeros((8, cols), F32)
    edges[8 * (tiles + 1) : 8 * (tiles + 2)] = jnp.zeros((8, cols), F32)

    def place(ref, tile):
        at = pl.multiple_of(tile * rows, rows)
        src[pl.ds(at, rows)] = ref[0:rows]
        damp[pl.ds(at, rows)] = 4.0 + ref[rows + 8 : 2 * rows + 8]
        edges[pl.ds(pl.multiple_of((tile + 1) * 8, 8), 8)] = ref[rows : rows + 8]

    place(own, me)
    for step, (for_top, for_bottom) in enumerate(partners):
        place(got[step], partner(me, jnp.where(depth == 0, for_top, for_bottom), tiles))
        place(swapped[step], partner(me, jnp.where(depth == 0, for_bottom, for_top), tiles))

    pad = 8
    total = jnp.zeros((rows, cols), F32)
    direc[0:pad] = jnp.zeros((pad, cols), F32)
    direc[pad + tiles * rows : 2 * pad + tiles * rows] = jnp.zeros((pad, cols), F32)
    row = lax.broadcasted_iota(jnp.int32, (rows, cols), 0)
    for t in range(tiles):
        above = edges[8 * t + 1 : 8 * t + 2]
        below = edges[8 * (t + 2) : 8 * (t + 2) + 1]
        block = src[t * rows : (t + 1) * rows]
        block = block + GRAVITY * (jnp.where(row == rows - 1, below, 0.0) - jnp.where(row == 0, above, 0.0))
        src[t * rows : (t + 1) * rows] = block
        direc[pad + t * rows : pad + (t + 1) * rows] = block
        total += block * block
    norm = jnp.sum(total, keepdims=True)
    sol[...] = jnp.zeros_like(sol)
    mine = pl.ds(pl.multiple_of(me * rows, 8), rows + 2 * pad)

    def advance(turn, norm):
        total = jnp.zeros((rows, cols), F32)
        for t in range(tiles):
            at = pad + t * rows
            d = direc[at : at + rows]
            right, left = lane_shifts(d)
            beside = direc[at + 1 : at + rows + 1] + direc[at - 1 : at + rows - 1] + right + left
            im = damp[t * rows : (t + 1) * rows] * d - beside
            image[t * rows : (t + 1) * rows] = im
            total += d * im
        alpha = norm / jnp.sum(total, keepdims=True)
        sol[...] += alpha * direc[mine]
        total = jnp.zeros((rows, cols), F32)
        for t in range(tiles):
            part = slice(t * rows, (t + 1) * rows)
            r = src[part] - alpha * image[part]
            src[part] = r
            total += r * r
        fresh = jnp.sum(total, keepdims=True)
        beta = fresh / norm
        for t in range(tiles):
            at = pad + t * rows
            direc[at : at + rows] = src[t * rows : (t + 1) * rows] + beta * direc[at : at + rows]
        return fresh

    lax.fori_loop(0, ITERS, advance, norm)

    x = sol[pad : pad + rows]
    adj_surface[...] = x
    right, left = lane_shifts(x)
    slope_x = ADVECT * (right - left)
    slope_y = ADVECT * (sol[pad + 1 : pad + rows + 1] - sol[pad - 1 : pad + rows - 1])
    for lev in range(levels):
        adj_velocity[0, lev] = flux[0, lev] + slope_x
        adj_velocity[1, lev] = flux[1, lev] + slope_y


def partner(tile, offset, tiles):
    if tiles & (tiles - 1) == 0:
        return tile ^ offset
    return (offset + tiles - tile) % tiles


def partner_offsets(tiles):
    if tiles & (tiles - 1) == 0:
        others = list(range(1, tiles))
    else:
        others = list(range(tiles))
    half = (len(others) + 1) // 2
    top, bottom = others[:half], others[half:]
    if len(bottom) < half:
        bottom = bottom + [top[-1]]
    return list(zip(top, bottom))


def body(tracer_start, velocity, surface, mixing, land_mask, damping, tracer_cot, surface_cot):
    tracers, levels, rows, cols = tracer_start.shape
    tiles = lax.axis_size("tile")
    swap = [(0, 1), (1, 0)]
    plane = (rows, cols)
    edge = (tracers * levels + 1, cols)
    face, edge_a, edge_b = call(
        start_kernel,
        [(tracers + 2,) + plane, edge, edge],
        [tracer_start, mixing, tracer_cot, land_mask, surface],
    )
    pairs_a = [(i, i + 1) for i in range(0, tiles - 1, 2)]
    pairs_b = [(i, i + 1) for i in range(1, tiles - 1, 2)]
    other = lax.ppermute(face, "depth", swap)
    edge_a = lax.ppermute(edge_a, "tile", pairs_a + [(b, a) for a, b in pairs_a])
    edge_b = lax.ppermute(edge_b, "tile", pairs_b + [(b, a) for a, b in pairs_b])
    flux, part = call(
        flux_kernel,
        [(2, levels) + plane, (2 * rows + 8, cols)],
        [tracer_start, mixing, tracer_cot, land_mask, face, other, edge_a, edge_b, surface_cot, damping],
    )
    own = part + lax.ppermute(part, "depth", swap)

    partners = partner_offsets(tiles)
    got = []
    for for_top, for_bottom in partners:
        pairs = [(2 * partner(t, for_top, tiles), 2 * t) for t in range(tiles)]
        pairs += [(2 * partner(t, for_bottom, tiles) + 1, 2 * t + 1) for t in range(tiles)]
        got.append(lax.ppermute(own, ("tile", "depth"), pairs))
    swapped = [lax.ppermute(block, "depth", swap) for block in got]

    (nums,) = call(
        adjoint_kernel,
        [(levels, tracers) + plane],
        [mixing, tracer_cot, land_mask, velocity, surface, edge_a, edge_b],
        flops=20_000_000,
    )
    other_nums = lax.ppermute(nums[levels - 1], "depth", swap)
    (adj_tracer,) = call(
        finish_kernel,
        [(tracers, levels) + plane],
        [mixing, nums, face, other, other_nums],
    )
    height = tiles * rows
    adj_velocity, adj_surface = call(
        functools.partial(solve_kernel, tiles, partners),
        [(2, levels) + plane, plane],
        [flux, own] + got + swapped,
        scratch=[
            pltpu.VMEM((height, cols), F32),
            pltpu.VMEM((height, cols), F32),
            pltpu.VMEM((8 * (tiles + 2), cols), F32),
            pltpu.VMEM((height + 16, cols), F32),
            pltpu.VMEM((height, cols), F32),
            pltpu.VMEM((rows + 16, cols), F32),
        ],
    )
    return adj_tracer, adj_velocity, adj_surface


def solution(mesh):
    return jax.shard_map(
        body,
        mesh=mesh,
        in_specs=(
            P("grp", "depth", "tile", None),
            P("grp", "depth", "tile", None),
            P(("grp", "tile"), None),
            P(("grp", "depth"), "tile", None),
            P("depth", "tile", None),
            P("tile", None),
            P("grp", "depth", "tile", None),
            P(("grp", "tile"), None),
        ),
        out_specs=(
            P("grp", "depth", "tile", None),
            P("grp", "depth", "tile", None),
            P(("grp", "tile"), None),
        ),
        check_vma=False,
    )
```

time: 455 us -> 38.4 us (0.08)
  blocking collectives: 262 us -> 0 us
  local copies, waits for them, and re-layouts: 60.1 us -> 5.68 us
  waiting for transfers between devices: 33.6 us -> 2.65 us
  starting transfers between devices: 46.5 us -> 21.2 us
  other arithmetic: 23.5 us -> 0.01 us
  between operations: 14.6 us -> 0.77 us
  loops' own time: 12.4 us -> 0 us
  Pallas kernels: 0 us -> 7.64 us
    psum x13 -> x0, blocking collectives: 248 us -> none  [the longest x7 136 us: squares(): return lax.psum(jnp.sum(vector * vector), 'tile')]
    ppermute x18 -> x13, starting transfers between devices: 42.7 us -> 21.2 us  [the longest x4 10.9 us: body(): got.append(lax.ppermute(own, ('tile', 'depth'), pairs))]
    ppermute x18 -> x13, waiting for transfers between devices: 22.1 us -> 2.65 us  [the longest x1 1.37 us: body(): lax.ppermute(edge_a, 'tile', pairs_a + [(b, a) for a, b in pairs_a])]
    all_to_all x7 -> x0, local copies, waits for them, and re-layouts: 19 us -> none  [the longest x3 12.5 us: vertical(): lax.all_to_all(stacked, 'depth', split_axis=3, concat_axis=1, tiled=True)]
    unnamed x33 -> x22, local copies, waits for them, and re-layouts: 24.5 us -> 5.66 us
    all_to_all x3 -> x0, blocking collectives: 13.9 us -> none  [the longest x2 9.36 us: vertical(): lax.all_to_all(stacked, 'depth', split_axis=3, concat_axis=1, tiled=True)]
    another operation x1 -> x0, loops' own time: 12.4 us -> none  [solve_tiles(): lax.fori_loop(0, ITERS, advance, (solution, source, source, norm_now))]
    psum x1 -> x0, waiting for transfers between devices: 11.4 us -> none  [body(): col_sums = lax.psum(column_terms, 'depth')]
  transfers between devices with their start and end apart: 20 -> 13, of which waited for: 9 -> 2; matrix products, arithmetic and copies ran while one was open for 1% -> 0% of each run, Pallas kernels for 0% -> 9%
where the time goes in v1:
time: 38.4 us; the launch traced here: 38 us
  starting transfers between devices  21.2 us (55%)
  Pallas kernels  7.64 us (20%)
  local copies, waits for them, and re-layouts  5.68 us (15%)
  waiting for transfers between devices  2.65 us (7%)
  between operations  0.77 us (2%)
    ppermute x4, starting transfers between devices, body(): got.append(lax.ppermute(own, ('tile', 'depth'), pairs))  10.9 us
    pallas_call x5, Pallas kernels, call(): pl.pallas_call(kernel, out_shape=[jax.ShapeDtypeStruct(s, F32) for s in o...  7.64 us
    ppermute x4, starting transfers between devices, body(): swapped = [lax.ppermute(block, 'depth', swap) for block in got]  6.31 us
    unnamed x22, local copies, waits for them, and re-layouts  5.66 us
    ppermute x1, starting transfers between devices, body(): lax.ppermute(edge_a, 'tile', pairs_a + [(b, a) for a, b in pairs_a])  2.59 us
    ppermute x1, waiting for transfers between devices, body(): lax.ppermute(edge_a, 'tile', pairs_a + [(b, a) for a, b in pairs_a])  1.37 us
    ppermute x1, waiting for transfers between devices, body(): own = part + lax.ppermute(part, 'depth', swap)  1.25 us
    ppermute x1, starting transfers between devices, body(): lax.ppermute(edge_b, 'tile', pairs_b + [(b, a) for a, b in pairs_b])  0.78 us
  transfers between devices with their start and end apart: 13, of which 2 were waited for; matrix products, arithmetic and copies ran while one was open for 0% of the time, Pallas kernels for 9%

profile of v1, /device:TPU:0, one launch (start us, length us, event | category | flops | bytes accessed | tf_op | source)
XLA Modules:
  0.0 38.0 jit_solution(7318765200640023451)
XLA Ops:
  0.6 0.0 copy-start
  0.6 1.2 %copy-done = f32[8,4,32,256]{3,2,1,0:T(8,128)S(1)} copy-done((f32[8,4,32,256]{3,2,1,0:T(8,128)S(1)}, f32[8,4,32,256]{3,2,1,0:T(8,128)}, u32[]{:S(2)}) %copy-start) | copy-done | bytes 1048600
  1.9 0.0 copy-start.2
  1.9 1.2 %copy-done.2 = f32[8,4,32,256]{3,2,1,0:T(8,128)S(1)} copy-done((f32[8,4,32,256]{3,2,1,0:T(8,128)S(1)}, f32[8,4,32,256]{3,2,1,0:T(8,128)}, u32[]{:S(2)}) %copy-start.2) | copy-done | bytes 1048600
  3.1 0.0 copy-start.4
  3.1 0.9 %copy-done.4 = f32[4,32,256]{2,1,0:T(8,128)S(1)} copy-done((f32[4,32,256]{2,1,0:T(8,128)S(1)}, f32[4,32,256]{2,1,0:T(8,128)}, u32[]{:S(2)}) %copy-start.4) | copy-done | bytes 131096
  4.0 0.0 copy-start.5
  4.0 0.9 %copy-done.5 = s32[4,32,256]{2,1,0:T(8,128)S(1)} copy-done((s32[4,32,256]{2,1,0:T(8,128)S(1)}, s32[4,32,256]{2,1,0:T(8,128)}, u32[]{:S(2)}) %copy-start.5) | copy-done | bytes 131096
  4.9 0.0 copy-start.7
  4.9 0.8 %copy-done.7 = f32[32,256]{1,0:T(8,128)S(1)} copy-done((f32[32,256]{1,0:T(8,128)S(1)}, f32[32,256]{1,0:T(8,128)}, u32[]{:S(2)}) %copy-start.7) | copy-done | bytes 32792
  5.7 0.0 copy-start.1
  5.7 0.0 copy-start.6
  5.7 0.0 copy-start.8
  5.7 0.1 shard_map.103
  5.8 0.5 %collective-permute-start.2 = (f32[10,32,256]{2,1,0:T(8,128)S(1)}, f32[10,32,256]{2,1,0:T(8,128)S(1)}, u32[]{:S(2)}, u32[]{:S(2)}) collective-permute-start(f32[10,32,256]{2,1,0:T(8,128)S(1)} %get-tuple-element.12.face), channel_id=1, source_target_pairs={{0,1},{1,0},{2,3},{3,2},{4,5},{5,4},{6,7},{7,6},{8,9},{9,8},{10,11... | collective-permute-start | bytes 983048 | tf_op jit(solution)/shard_map/ppermute | solution.py:291
  6.3 2.6 %collective-permute-start = (f32[33,256]{1,0:T(8,128)S(1)}, f32[33,256]{1,0:T(8,128)S(1)}, u32[]{:S(2)}, u32[]{:S(2)}) collective-permute-start(f32[33,256]{1,0:T(8,128)S(1)} %get-tuple-element.10), channel_id=1, source_target_pairs={{0,2},{4,6},{8,10},{12,14},{2,0},{6,4},{10,8},{14,12},{1,3},{5,7},... | collective-permute-start | bytes 101384 | tf_op jit(solution)/shard_map/ppermute | solution.py:292
  8.9 0.0 copy-start.3
  8.9 0.8 %collective-permute-start.1 = (f32[33,256]{1,0:T(8,128)S(1)}, f32[33,256]{1,0:T(8,128)S(1)}, u32[]{:S(2)}, u32[]{:S(2)}) collective-permute-start(f32[33,256]{1,0:T(8,128)S(1)} %get-tuple-element.11), channel_id=1, source_target_pairs={{2,4},{6,8},{10,12},{4,2},{8,6},{12,10},{3,5},{7,9},{11,13},{5,3},... | collective-permute-start | bytes 101384 | tf_op jit(solution)/shard_map/ppermute | solution.py:293
  9.7 1.4 %collective-permute-done.edge_a = f32[33,256]{1,0:T(8,128)S(1)} collective-permute-done((f32[33,256]{1,0:T(8,128)S(1)}, f32[33,256]{1,0:T(8,128)S(1)}, u32[]{:S(2)}, u32[]{:S(2)}) %collective-permute-start) | collective-permute-done | bytes 33824 | tf_op jit(solution)/shard_map/ppermute | solution.py:292
  11.0 0.0 collective-permute-done.1.edge_b
  11.0 0.0 copy-done.1
  11.1 0.0 copy-done.6
  11.1 0.0 copy-done.8
  11.1 1.0 %shard_map.104.nums = f32[4,8,32,256]{3,2,1,0:T(8,128)S(1)} custom-call(f32[4,32,256]{2,1,0:T(8,128)S(1)} %copy-done.4, f32[8,4,32,256]{3,2,1,0:T(8,128)S(1)} %copy-done.1, s32[4,32,256]{2,1,0:T(8,128)S(1)} %copy-done.5, f32[2,4,32,256]{3,2,1,0:T(8,128)S(1)} %copy-done.6, f32[32,256]{1,0:T(8,128)S(1)} %copy-done.8, ...), custom_call_target="tpu_custom_call" | custom-call | flops 20000000 | bytes 2721792 | tf_op jit(solution)/shard_map/pallas_call | solution.py:21
  12.1 0.0 copy-start.9
  12.1 0.0 copy-start.10
  12.1 0.1 collective-permute-start.3
  12.2 0.0 collective-permute-done.2.other
  12.2 0.0 copy-done.3
  12.2 0.6 %copy-done.9 = f32[32,256]{1,0:T(8,128)S(1)} copy-done((f32[32,256]{1,0:T(8,128)S(1)}, f32[32,256]{1,0:T(8,128)}, u32[]{:S(2)}) %copy-start.9) | copy-done | bytes 32792
  12.8 0.0 copy-done.10
  12.8 1.1 %shard_map.106 = (f32[2,4,32,256]{3,2,1,0:T(8,128)S(1)}, f32[72,256]{1,0:T(8,128)S(1)}) custom-call(f32[8,4,32,256]{3,2,1,0:T(8,128)S(1)} %copy-done.3, f32[4,32,256]{2,1,0:T(8,128)S(1)} %copy-done.4, f32[8,4,32,256]{3,2,1,0:T(8,128)S(1)} %copy-done.1, s32[4,32,256]{2,1,0:T(8,128)S(1)} %copy-done.5, f32[10,32,256]{2,1,0:T(8,128)S(1)} %get-tuple-element.12.face, ...), custom_call_target="tpu_custom_call" | custom-call | flops 2000000 | bytes 3483648 | tf_op jit(solution)/shard_map/pallas_call | solution.py:21
  14.0 0.1 collective-permute-start.4
  14.1 1.3 %collective-permute-done.4 = f32[72,256]{1,0:T(8,128)S(1)} collective-permute-done((f32[72,256]{1,0:T(8,128)S(1)}, f32[72,256]{1,0:T(8,128)S(1)}, u32[]{:S(2)}, u32[]{:S(2)}) %collective-permute-start.4) | collective-permute-done | bytes 73760 | tf_op jit(solution)/shard_map/ppermute | solution.py:299
  15.3 4.9 %collective-permute-start.5 = (f32[72,256]{1,0:T(8,128)S(1)}, f32[72,256]{1,0:T(8,128)S(1)}, u32[]{:S(2)}, u32[]{:S(2)}) collective-permute-start(f32[72,256]{1,0:T(8,128)S(1)} %add.3.own), channel_id=1, source_target_pairs={{2,0},{0,2},{6,4},{4,6},{10,8},{8,10},{14,12},{12,14},{11,1},{9,3}... | collective-permute-start | bytes 221192 | tf_op jit(solution)/shard_map/ppermute | solution.py:306
  20.3 2.0 %collective-permute-start.6 = (f32[72,256]{1,0:T(8,128)S(1)}, f32[72,256]{1,0:T(8,128)S(1)}, u32[]{:S(2)}, u32[]{:S(2)}) collective-permute-start(f32[72,256]{1,0:T(8,128)S(1)} %add.3.own), channel_id=1, source_target_pairs={{4,0},{6,2},{0,4},{2,6},{12,8},{14,10},{8,12},{10,14},{13,1},{15,3... | collective-permute-start | bytes 221192 | tf_op jit(solution)/shard_map/ppermute | solution.py:306
  22.2 1.0 %collective-permute-start.7 = (f32[72,256]{1,0:T(8,128)S(1)}, f32[72,256]{1,0:T(8,128)S(1)}, u32[]{:S(2)}, u32[]{:S(2)}) collective-permute-start(f32[72,256]{1,0:T(8,128)S(1)} %add.3.own), channel_id=1, source_target_pairs={{6,0},{4,2},{2,4},{0,6},{14,8},{12,10},{10,12},{8,14},{15,1},{13,3... | collective-permute-start | bytes 221192 | tf_op jit(solution)/shard_map/ppermute | solution.py:306
  23.2 3.0 %collective-permute-start.8 = (f32[72,256]{1,0:T(8,128)S(1)}, f32[72,256]{1,0:T(8,128)S(1)}, u32[]{:S(2)}, u32[]{:S(2)}) collective-permute-start(f32[72,256]{1,0:T(8,128)S(1)} %add.3.own), channel_id=1, source_target_pairs={{8,0},{10,2},{12,4},{14,6},{0,8},{2,10},{4,12},{6,14},{9,1},{11,3}... | collective-permute-start | bytes 221192 | tf_op jit(solution)/shard_map/ppermute | solution.py:306
  26.2 0.0 collective-permute-done.5.refs_0_
  26.2 0.6 %collective-permute-start.9 = (f32[72,256]{1,0:T(8,128)S(1)}, f32[72,256]{1,0:T(8,128)S(1)}, u32[]{:S(2)}, u32[]{:S(2)}) collective-permute-start(f32[72,256]{1,0:T(8,128)S(1)} %collective-permute-done.5.refs_0_), channel_id=1, source_target_pairs={{0,1},{1,0},{2,3},{3,2},{4,5},{5,4},{6,7},{7,6},{8,9},{9,8},{10,11... | collective-permute-start | bytes 221192 | tf_op jit(solution)/shard_map/ppermute | solution.py:307
  26.8 0.0 collective-permute-done.6.refs_1_
  26.8 1.0 %collective-permute-start.10 = (f32[72,256]{1,0:T(8,128)S(1)}, f32[72,256]{1,0:T(8,128)S(1)}, u32[]{:S(2)}, u32[]{:S(2)}) collective-permute-start(f32[72,256]{1,0:T(8,128)S(1)} %collective-permute-done.6.refs_1_), channel_id=1, source_target_pairs={{0,1},{1,0},{2,3},{3,2},{4,5},{5,4},{6,7},{7,6},{8,9},{9,8},{10,11... | collective-permute-start | bytes 221192 | tf_op jit(solution)/shard_map/ppermute | solution.py:307
  27.7 0.0 collective-permute-done.7.refs_2_
  27.7 2.9 %collective-permute-start.11 = (f32[72,256]{1,0:T(8,128)S(1)}, f32[72,256]{1,0:T(8,128)S(1)}, u32[]{:S(2)}, u32[]{:S(2)}) collective-permute-start(f32[72,256]{1,0:T(8,128)S(1)} %collective-permute-done.7.refs_2_), channel_id=1, source_target_pairs={{0,1},{1,0},{2,3},{3,2},{4,5},{5,4},{6,7},{7,6},{8,9},{9,8},{10,11... | collective-permute-start | bytes 221192 | tf_op jit(solution)/shard_map/ppermute | solution.py:307
  30.7 0.0 collective-permute-done.8.refs_3_
  30.7 1.9 %collective-permute-start.12 = (f32[72,256]{1,0:T(8,128)S(1)}, f32[72,256]{1,0:T(8,128)S(1)}, u32[]{:S(2)}, u32[]{:S(2)}) collective-permute-start(f32[72,256]{1,0:T(8,128)S(1)} %collective-permute-done.8.refs_3_), channel_id=1, source_target_pairs={{0,1},{1,0},{2,3},{3,2},{4,5},{5,4},{6,7},{7,6},{8,9},{9,8},{10,11... | collective-permute-start | bytes 221192 | tf_op jit(solution)/shard_map/ppermute | solution.py:307
  32.5 0.0 collective-permute-done.3.other_nums
  32.6 1.2 %shard_map.105 = f32[8,4,32,256]{3,2,1,0:T(8,128)} custom-call(f32[4,32,256]{2,1,0:T(8,128)S(1)} %copy-done.4, f32[4,8,32,256]{3,2,1,0:T(8,128)S(1)} %shard_map.104.nums, f32[10,32,256]{2,1,0:T(8,128)S(1)} %get-tuple-element.12.face, f32[10,32,256]{2,1,0:T(8,128)S(1)} %collective-permute-done.2.other, f32[8,32,256]{2,1,0:T(8,128)S(1)} %collective-permute-done.3.other_nums), custom_call_target="tpu_custom_call" | custom-call | flops 2000000 | bytes 3145728 | tf_op jit(solution)/shard_map/pallas_call | solution.py:21
  33.7 0.0 collective-permute-done.9.refs_4_
  33.7 0.0 collective-permute-done.10.refs_5_
  33.7 0.0 collective-permute-done.11.refs_6_
  33.7 0.0 collective-permute-done.12.refs_7_
  33.7 4.2 %shard_map.107 = (f32[2,4,32,256]{3,2,1,0:T(8,128)}, f32[32,256]{1,0:T(8,128)}) custom-call(f32[2,4,32,256]{3,2,1,0:T(8,128)S(1)} %get-tuple-element.13.flux, f32[72,256]{1,0:T(8,128)S(1)} %add.3.own, f32[72,256]{1,0:T(8,128)S(1)} %collective-permute-done.5.refs_0_, f32[72,256]{1,0:T(8,128)S(1)} %collective-permute-done.6.refs_1_, ...), custom_call_target="tpu_custom_call" | custom-call | flops 2000000 | bytes 1220608 | tf_op jit(solution)/shard_map/pallas_call | solution.py:21
  (2 shorter events, 0.0 us)
Async XLA Ops:
  0.6 1.2 %copy-start = (f32[8,4,32,256]{3,2,1,0:T(8,128)S(1)}, f32[8,4,32,256]{3,2,1,0:T(8,128)}, u32[]{:S(2)}) copy-start(f32[8,4,32,256]{3,2,1,0:T(8,128)} %cot.5) | copy-start | bytes 3145732
  1.9 1.2 %copy-start.2 = (f32[8,4,32,256]{3,2,1,0:T(8,128)S(1)}, f32[8,4,32,256]{3,2,1,0:T(8,128)}, u32[]{:S(2)}) copy-start(f32[8,4,32,256]{3,2,1,0:T(8,128)} %tracer.3) | copy-start | bytes 3145732
  3.1 0.9 %copy-start.4 = (f32[4,32,256]{2,1,0:T(8,128)S(1)}, f32[4,32,256]{2,1,0:T(8,128)}, u32[]{:S(2)}) copy-start(f32[4,32,256]{2,1,0:T(8,128)} %mix.7) | copy-start | bytes 393220
  4.0 0.9 %copy-start.5 = (s32[4,32,256]{2,1,0:T(8,128)S(1)}, s32[4,32,256]{2,1,0:T(8,128)}, u32[]{:S(2)}) copy-start(s32[4,32,256]{2,1,0:T(8,128)} %mask.5) | copy-start | bytes 393220
  4.9 0.8 %copy-start.7 = (f32[32,256]{1,0:T(8,128)S(1)}, f32[32,256]{1,0:T(8,128)}, u32[]{:S(2)}) copy-start(f32[32,256]{1,0:T(8,128)} %surface.3) | copy-start | bytes 98308
  5.7 5.4 %copy-start.1 = (f32[8,4,32,256]{3,2,1,0:T(8,128)S(1)}, f32[8,4,32,256]{3,2,1,0:T(8,128)}, u32[]{:S(2)}) copy-start(f32[8,4,32,256]{3,2,1,0:T(8,128)} %cot.5) | copy-start | bytes 3145732
  5.7 5.4 %copy-start.6 = (f32[2,4,32,256]{3,2,1,0:T(8,128)S(1)}, f32[2,4,32,256]{3,2,1,0:T(8,128)}, u32[]{:S(2)}) copy-start(f32[2,4,32,256]{3,2,1,0:T(8,128)} %velocity.1) | copy-start | bytes 786436
  5.7 5.4 %copy-start.8 = (f32[32,256]{1,0:T(8,128)S(1)}, f32[32,256]{1,0:T(8,128)}, u32[]{:S(2)}) copy-start(f32[32,256]{1,0:T(8,128)} %surface.3) | copy-start | bytes 98308
  5.8 6.4 %collective-permute-start.2 = (f32[10,32,256]{2,1,0:T(8,128)S(1)}, f32[10,32,256]{2,1,0:T(8,128)S(1)}, u32[]{:S(2)}, u32[]{:S(2)}) collective-permute-start(f32[10,32,256]{2,1,0:T(8,128)S(1)} %get-tuple-element.12.face), channel_id=1, source_target_pairs={{0,1},{1,0},{2,3},{3,2},{4,5},{5,4},{6,7},{7,6},{8,9},{9,8},{10,11... | collective-permute-start | bytes 983048 | tf_op jit(solution)/shard_map/ppermute | solution.py:291
  6.3 4.8 %collective-permute-start = (f32[33,256]{1,0:T(8,128)S(1)}, f32[33,256]{1,0:T(8,128)S(1)}, u32[]{:S(2)}, u32[]{:S(2)}) collective-permute-start(f32[33,256]{1,0:T(8,128)S(1)} %get-tuple-element.10), channel_id=1, source_target_pairs={{0,2},{4,6},{8,10},{12,14},{2,0},{6,4},{10,8},{14,12},{1,3},{5,7},... | collective-permute-start | bytes 101384 | tf_op jit(solution)/shard_map/ppermute | solution.py:292
  8.9 3.3 %copy-start.3 = (f32[8,4,32,256]{3,2,1,0:T(8,128)S(1)}, f32[8,4,32,256]{3,2,1,0:T(8,128)}, u32[]{:S(2)}) copy-start(f32[8,4,32,256]{3,2,1,0:T(8,128)} %tracer.3) | copy-start | bytes 3145732
  8.9 2.2 %collective-permute-start.1 = (f32[33,256]{1,0:T(8,128)S(1)}, f32[33,256]{1,0:T(8,128)S(1)}, u32[]{:S(2)}, u32[]{:S(2)}) collective-permute-start(f32[33,256]{1,0:T(8,128)S(1)} %get-tuple-element.11), channel_id=1, source_target_pairs={{2,4},{6,8},{10,12},{4,2},{8,6},{12,10},{3,5},{7,9},{11,13},{5,3},... | collective-permute-start | bytes 101384 | tf_op jit(solution)/shard_map/ppermute | solution.py:293
  12.1 0.8 %copy-start.9 = (f32[32,256]{1,0:T(8,128)S(1)}, f32[32,256]{1,0:T(8,128)}, u32[]{:S(2)}) copy-start(f32[32,256]{1,0:T(8,128)} %surface_cot.1) | copy-start | bytes 98308
  12.1 0.8 %copy-start.10 = (f32[32,256]{1,0:T(8,128)S(1)}, f32[32,256]{1,0:T(8,128)}, u32[]{:S(2)}) copy-start(f32[32,256]{1,0:T(8,128)} %damping.1) | copy-start | bytes 98308
  12.1 20.4 %collective-permute-start.3 = (f32[8,32,256]{2,1,0:T(8,128)S(1)}, f32[8,32,256]{2,1,0:T(8,128)S(1)}, u32[]{:S(2)}, u32[]{:S(2)}) collective-permute-start(f32[8,32,256]{2,1,0:T(8,128)S(1)} %slice_bitcast_fusion), channel_id=1, source_target_pairs={{0,1},{1,0},{2,3},{3,2},{4,5},{5,4},{6,7},{7,6},{8,9},{9,8},{10,11... | collective-permute-start | bytes 786440 | tf_op jit(solution)/shard_map/ppermute | solution.py:315
  14.0 1.3 %collective-permute-start.4 = (f32[72,256]{1,0:T(8,128)S(1)}, f32[72,256]{1,0:T(8,128)S(1)}, u32[]{:S(2)}, u32[]{:S(2)}) collective-permute-start(f32[72,256]{1,0:T(8,128)S(1)} %get-tuple-element.14), channel_id=1, source_target_pairs={{0,1},{1,0},{2,3},{3,2},{4,5},{5,4},{6,7},{7,6},{8,9},{9,8},{10,11... | collective-permute-start | bytes 221192 | tf_op jit(solution)/shard_map/ppermute | solution.py:299
  15.3 10.9 %collective-permute-start.5 = (f32[72,256]{1,0:T(8,128)S(1)}, f32[72,256]{1,0:T(8,128)S(1)}, u32[]{:S(2)}, u32[]{:S(2)}) collective-permute-start(f32[72,256]{1,0:T(8,128)S(1)} %add.3.own), channel_id=1, source_target_pairs={{2,0},{0,2},{6,4},{4,6},{10,8},{8,10},{14,12},{12,14},{11,1},{9,3}... | collective-permute-start | bytes 221192 | tf_op jit(solution)/shard_map/ppermute | solution.py:306
  20.3 6.5 %collective-permute-start.6 = (f32[72,256]{1,0:T(8,128)S(1)}, f32[72,256]{1,0:T(8,128)S(1)}, u32[]{:S(2)}, u32[]{:S(2)}) collective-permute-start(f32[72,256]{1,0:T(8,128)S(1)} %add.3.own), channel_id=1, source_target_pairs={{4,0},{6,2},{0,4},{2,6},{12,8},{14,10},{8,12},{10,14},{13,1},{15,3... | collective-permute-start | bytes 221192 | tf_op jit(solution)/shard_map/ppermute | solution.py:306
  22.2 5.5 %collective-permute-start.7 = (f32[72,256]{1,0:T(8,128)S(1)}, f32[72,256]{1,0:T(8,128)S(1)}, u32[]{:S(2)}, u32[]{:S(2)}) collective-permute-start(f32[72,256]{1,0:T(8,128)S(1)} %add.3.own), channel_id=1, source_target_pairs={{6,0},{4,2},{2,4},{0,6},{14,8},{12,10},{10,12},{8,14},{15,1},{13,3... | collective-permute-start | bytes 221192 | tf_op jit(solution)/shard_map/ppermute | solution.py:306
  23.2 7.5 %collective-permute-start.8 = (f32[72,256]{1,0:T(8,128)S(1)}, f32[72,256]{1,0:T(8,128)S(1)}, u32[]{:S(2)}, u32[]{:S(2)}) collective-permute-start(f32[72,256]{1,0:T(8,128)S(1)} %add.3.own), channel_id=1, source_target_pairs={{8,0},{10,2},{12,4},{14,6},{0,8},{2,10},{4,12},{6,14},{9,1},{11,3}... | collective-permute-start | bytes 221192 | tf_op jit(solution)/shard_map/ppermute | solution.py:306
  26.2 7.5 %collective-permute-start.9 = (f32[72,256]{1,0:T(8,128)S(1)}, f32[72,256]{1,0:T(8,128)S(1)}, u32[]{:S(2)}, u32[]{:S(2)}) collective-permute-start(f32[72,256]{1,0:T(8,128)S(1)} %collective-permute-done.5.refs_0_), channel_id=1, source_target_pairs={{0,1},{1,0},{2,3},{3,2},{4,5},{5,4},{6,7},{7,6},{8,9},{9,8},{10,11... | collective-permute-start | bytes 221192 | tf_op jit(solution)/shard_map/ppermute | solution.py:307
  26.8 6.9 %collective-permute-start.10 = (f32[72,256]{1,0:T(8,128)S(1)}, f32[72,256]{1,0:T(8,128)S(1)}, u32[]{:S(2)}, u32[]{:S(2)}) collective-permute-start(f32[72,256]{1,0:T(8,128)S(1)} %collective-permute-done.6.refs_1_), channel_id=1, source_target_pairs={{0,1},{1,0},{2,3},{3,2},{4,5},{5,4},{6,7},{7,6},{8,9},{9,8},{10,11... | collective-permute-start | bytes 221192 | tf_op jit(solution)/shard_map/ppermute | solution.py:307
  27.7 6.0 %collective-permute-start.11 = (f32[72,256]{1,0:T(8,128)S(1)}, f32[72,256]{1,0:T(8,128)S(1)}, u32[]{:S(2)}, u32[]{:S(2)}) collective-permute-start(f32[72,256]{1,0:T(8,128)S(1)} %collective-permute-done.7.refs_2_), channel_id=1, source_target_pairs={{0,1},{1,0},{2,3},{3,2},{4,5},{5,4},{6,7},{7,6},{8,9},{9,8},{10,11... | collective-permute-start | bytes 221192 | tf_op jit(solution)/shard_map/ppermute | solution.py:307
  30.7 3.0 %collective-permute-start.12 = (f32[72,256]{1,0:T(8,128)S(1)}, f32[72,256]{1,0:T(8,128)S(1)}, u32[]{:S(2)}, u32[]{:S(2)}) collective-permute-start(f32[72,256]{1,0:T(8,128)S(1)} %collective-permute-done.8.refs_3_), channel_id=1, source_target_pairs={{0,1},{1,0},{2,3},{3,2},{4,5},{5,4},{6,7},{7,6},{8,9},{9,8},{10,11... | collective-permute-start | bytes 221192 | tf_op jit(solution)/shard_map/ppermute | solution.py:307

commit v2 on v1

--- a/solution.py
+++ b/solution.py
@@ -14,15 +14,16 @@
 
 F32 = jnp.float32
 VMEM = pl.BlockSpec(memory_space=pltpu.VMEM)
-
-
-def call(kernel, outs, args, scratch=(), flops=2_000_000):
+HBM = pl.BlockSpec(memory_space=pltpu.HBM)
+
+
+def call(kernel, outs, args, scratch=(), flops=2_000_000, hbm_in=(), hbm_out=()):
     nbytes = sum(a.size * 4 for a in args) + sum(4 * functools.reduce(lambda p, q: p * q, s) for s in outs)
     return pl.pallas_call(
         kernel,
         out_shape=[jax.ShapeDtypeStruct(s, F32) for s in outs],
-        in_specs=[VMEM] * len(args),
-        out_specs=[VMEM] * len(outs),
+        in_specs=[HBM if i in hbm_in else VMEM for i in range(len(args))],
+        out_specs=[HBM if i in hbm_out else VMEM for i in range(len(outs))],
         scratch_shapes=list(scratch),
         cost_estimate=pl.CostEstimate(flops=flops, bytes_accessed=nbytes, transcendentals=0),
         compiler_params=pltpu.CompilerParams(vmem_limit_bytes=40 * 1024 * 1024),
@@ -69,10 +70,16 @@
     return (other_rest + link) * inv, link * inv
 
 
-def start_kernel(tracer, mix, cot, mask, surface, face, edge_a, edge_b):
+def start_kernel(tracer_in, mix_in, cot_in, mask_in, surface_in, tracer, mix, weighted, surface, face, edge_a, edge_b, cot, mask, sems):
     tracers, levels, rows, _ = tracer.shape
     depth = lax.axis_index("depth")
     odd = lax.rem(lax.axis_index("tile"), 2) == 1
+    moves = [(mix_in, mix), (tracer_in, tracer), (surface_in, surface), (mask_in, mask), (cot_in, cot)]
+    copies = [pltpu.make_async_copy(src, dst, sems.at[i]) for i, (src, dst) in enumerate(moves)]
+    for copy in copies:
+        copy.start()
+    copies[0].wait()
+    copies[1].wait()
     _, ratio, rest = chain(mix, depth)
     for tr in range(tracers):
         num = tracer[tr, level(0, depth, levels)]
@@ -81,28 +88,29 @@
         face[tr] = num
     face[tracers] = rest
     face[tracers + 1] = mix[levels - 1]
+    for copy in copies[2:]:
+        copy.wait()
     for lev in range(levels):
-        first_mask = mask[lev, 0:1].astype(F32)
-        last_mask = mask[lev, rows - 1 : rows].astype(F32)
+        wet = mask[lev].astype(F32)
         for tr in range(tracers):
-            first = cot[tr, lev, 0:1] * first_mask
-            last = cot[tr, lev, rows - 1 : rows] * last_mask
+            block = cot[tr, lev] * wet
+            weighted[tr, lev] = block
+            first, last = block[0:1], block[rows - 1 : rows]
             at = tr * levels + lev
             edge_a[at : at + 1] = jnp.where(odd, first, last)
             edge_b[at : at + 1] = jnp.where(odd, last, first)
     at = tracers * levels
+    edge_a[at : at + 8] = jnp.zeros_like(edge_a[at : at + 8])
+    edge_b[at : at + 8] = jnp.zeros_like(edge_b[at : at + 8])
     edge_a[at : at + 1] = jnp.where(odd, surface[0:1], surface[rows - 1 : rows])
     edge_b[at : at + 1] = jnp.where(odd, surface[rows - 1 : rows], surface[0:1])
 
 
-def flux_kernel(tracer, mix, cot, mask, face, other, edge_a, edge_b, surface_cot, damping, flux, send):
+def flux_kernel(tracer, mix, weighted, face, other, flux, firsts, lasts):
     tracers, levels, rows, cols = tracer.shape
     depth = lax.axis_index("depth")
-    odd = lax.rem(lax.axis_index("tile"), 2) == 1
     inverse, ratio, rest = chain(mix, depth)
     own_w, other_w = meet(rest, other[tracers], mix[levels - 1], other[tracers + 1], depth)
-    col_x = jnp.zeros((rows, cols), F32)
-    col_y = jnp.zeros((rows, cols), F32)
     flux[...] = jnp.zeros_like(flux)
     for tr in range(tracers):
         nums = [tracer[tr, level(0, depth, levels)]]
@@ -113,30 +121,53 @@
             lev = level(j, depth, levels)
             if j < levels - 1:
                 value = inverse[j] * nums[j] + ratio[j] * value
-            weighted = cot[tr, lev] * mask[lev].astype(F32)
-            at = tr * levels + lev
-            row_a, row_b = edge_a[pl.ds(at, 1)], edge_b[pl.ds(at, 1)]
-            low, high = jnp.where(odd, row_a, row_b), jnp.where(odd, row_b, row_a)
-            right, left = lane_shifts(weighted)
-            down, up = row_shifts(weighted, low, high)
+            block = weighted[tr, lev]
+            right, left = lane_shifts(block)
+            down, up = row_shifts(block, 0.0, 0.0)
             flux[0, lev] += ADVECT * (value * (right - left))
             flux[1, lev] += ADVECT * (value * (down - up))
+            at = tr * levels + lev
+            firsts[pl.ds(at, 1)] = value[0:1]
+            lasts[pl.ds(at, 1)] = value[rows - 1 : rows]
+
+
+def column_kernel(flux_in, firsts, lasts, edge_a, edge_b, surface_cot, damping, flux, send):
+    levels, rows, cols = flux.shape[1:]
+    planes = firsts.shape[0]
+    depth = lax.axis_index("depth")
+    odd = lax.rem(lax.axis_index("tile"), 2) == 1
+    row_a, row_b = edge_a[0:planes], edge_b[0:planes]
+    low = ADVECT * (firsts[...] * jnp.where(odd, row_a, row_b))
+    high = ADVECT * (lasts[...] * jnp.where(odd, row_b, row_a))
+    row = lax.broadcasted_iota(jnp.int32, (rows, cols), 0)
+    kind = lax.broadcasted_iota(jnp.int32, (8, cols), 0)
+    def by_level(terms):
+        return sum(terms[8 * i : 8 * (i + 1)] for i in range(planes // 8))
+
+    low, high = by_level(low), by_level(high)
+    col_x = jnp.zeros((rows, cols), F32)
+    col_y = jnp.zeros((rows, cols), F32)
     for lev in range(levels):
-        col_x += flux[0, lev]
-        col_y += flux[1, lev]
+        at_level = lax.rem(kind, levels) == lev
+        minus = jnp.sum(jnp.where(at_level, low, 0.0), axis=0, keepdims=True)
+        plus = jnp.sum(jnp.where(at_level, high, 0.0), axis=0, keepdims=True)
+        flux_x = flux_in[0, lev]
+        flux_y = flux_in[1, lev] + (jnp.where(row == rows - 1, plus, 0.0) - jnp.where(row == 0, minus, 0.0))
+        flux[0, lev] = flux_x
+        flux[1, lev] = flux_y
+        col_x += flux_x
+        col_y += flux_y
     right, left = lane_shifts(col_x)
     down, up = row_shifts(col_y, 0.0, 0.0)
     top = depth == 0
     source = GRAVITY * (right - left + down - up)
     send[0:rows] = source + jnp.where(top, surface_cot[...], 0.0)
-    send[rows : rows + 8] = jnp.zeros((8, cols), F32)
-    send[rows : rows + 1] = col_y[0:1]
-    send[rows + 1 : rows + 2] = col_y[rows - 1 : rows]
+    send[rows : rows + 8] = jnp.where(kind == 0, col_y[0:1], jnp.where(kind == 1, col_y[rows - 1 : rows], 0.0))
     send[rows + 8 : 2 * rows + 8] = jnp.where(top, damping[...], 0.0)
 
 
-def adjoint_kernel(mix, cot, mask, velocity, surface, edge_a, edge_b, nums):
-    tracers, levels, rows, cols = cot.shape
+def adjoint_kernel(mix, weighted_in, velocity, surface, edge_a, edge_b, after, nums, last):
+    tracers, levels, rows, cols = weighted_in.shape
     depth = lax.axis_index("depth")
     odd = lax.rem(lax.axis_index("tile"), 2) == 1
     _, ratio, _ = chain(mix, depth)
@@ -150,9 +181,8 @@
         lev = level(j, depth, levels)
         u_eff = ADVECT * (velocity[0, lev] - slope_x)
         v_eff = ADVECT * (velocity[1, lev] - slope_y)
-        wet = mask[lev].astype(F32)
         for tr in range(tracers):
-            weighted = cot[tr, lev] * wet
+            weighted = weighted_in[tr, lev]
             at = tr * levels + lev
             row_a, row_b = edge_a[pl.ds(at, 1)], edge_b[pl.ds(at, 1)]
             low, high = jnp.where(odd, row_a, row_b), jnp.where(odd, row_b, row_a)
@@ -165,29 +195,32 @@
             )
             if j > 0:
                 out = out + ratio[j - 1] * nums[j - 1, tr]
-            nums[j, tr] = out
-
-
-def finish_kernel(mix, nums, face, other, other_nums, adj_tracer):
-    tracers, levels, rows, cols = adj_tracer.shape
-    depth = lax.axis_index("depth")
+            if j < levels - 1:
+                nums[j, tr] = out
+            else:
+                last[tr] = out
+
+
+def solve_kernel(tiles, partners, flux, mix, nums, last, face, other, other_last, own, *refs):
+    steps = len(partners)
+    got, swapped = refs[:steps], refs[steps : 2 * steps]
+    adj_tracer_out, adj_velocity, adj_surface = refs[2 * steps : 2 * steps + 3]
+    src, damp, edges, direc, image, sol, adj_tracer, sem = refs[2 * steps + 3 :]
+    levels, rows, cols = flux.shape[1:]
+    me = lax.axis_index("tile")
+    depth = lax.axis_index("depth")
+
+    tracers = last.shape[0]
     inverse, ratio, rest = chain(mix, depth)
     own_w, other_w = meet(rest, other[tracers], mix[levels - 1], other[tracers + 1], depth)
     for tr in range(tracers):
-        value = own_w * nums[levels - 1, tr] + other_w * other_nums[tr]
+        value = own_w * last[tr] + other_w * other_last[tr]
         adj_tracer[tr, level(levels - 1, depth, levels)] = value
         for j in range(levels - 2, -1, -1):
             value = inverse[j] * nums[j, tr] + ratio[j] * value
             adj_tracer[tr, level(j, depth, levels)] = value
-
-
-def solve_kernel(tiles, partners, flux, own, *refs):
-    steps = len(partners)
-    got, swapped = refs[:steps], refs[steps : 2 * steps]
-    adj_velocity, adj_surface, src, damp, edges, direc, image, sol = refs[2 * steps :]
-    levels, rows, cols = flux.shape[1:]
-    me = lax.axis_index("tile")
-    depth = lax.axis_index("depth")
+    copy_out = pltpu.make_async_copy(adj_tracer, adj_tracer_out, sem)
+    copy_out.start()
 
     edges[0:8] = jnp.zeros((8, cols), F32)
     edges[8 * (tiles + 1) : 8 * (tiles + 2)] = jnp.zeros((8, cols), F32)
@@ -255,6 +288,7 @@
     for lev in range(levels):
         adj_velocity[0, lev] = flux[0, lev] + slope_x
         adj_velocity[1, lev] = flux[1, lev] + slope_y
+    copy_out.wait()
 
 
 def partner(tile, offset, tiles):
@@ -268,11 +302,10 @@
         others = list(range(1, tiles))
     else:
         others = list(range(tiles))
-    half = (len(others) + 1) // 2
-    top, bottom = others[:half], others[half:]
-    if len(bottom) < half:
-        bottom = bottom + [top[-1]]
-    return list(zip(top, bottom))
+    if len(others) % 2 == 1:
+        others = others[:1] + others
+    pairs = [(others[i], others[i + 1]) for i in range(0, len(others), 2)]
+    return [pair if i % 2 == 0 else pair[::-1] for i, pair in enumerate(pairs)]
 
 
 def body(tracer_start, velocity, surface, mixing, land_mask, damping, tracer_cot, surface_cot):
@@ -280,21 +313,29 @@
     tiles = lax.axis_size("tile")
     swap = [(0, 1), (1, 0)]
     plane = (rows, cols)
-    edge = (tracers * levels + 1, cols)
-    face, edge_a, edge_b = call(
+    block = (tracers, levels) + plane
+    edge = (tracers * levels + 8, cols)
+    tracer, mix, weighted, surface_in, face, edge_a, edge_b = call(
         start_kernel,
-        [(tracers + 2,) + plane, edge, edge],
+        [block, (levels,) + plane, block, plane, (tracers + 2,) + plane, edge, edge],
         [tracer_start, mixing, tracer_cot, land_mask, surface],
+        scratch=[pltpu.VMEM(block, F32), pltpu.VMEM((levels,) + plane, jnp.int32), pltpu.SemaphoreType.DMA((5,))],
+        hbm_in=range(5),
     )
     pairs_a = [(i, i + 1) for i in range(0, tiles - 1, 2)]
     pairs_b = [(i, i + 1) for i in range(1, tiles - 1, 2)]
     other = lax.ppermute(face, "depth", swap)
+    edge_b = lax.ppermute(edge_b, "tile", pairs_b + [(b, a) for a, b in pairs_b])
     edge_a = lax.ppermute(edge_a, "tile", pairs_a + [(b, a) for a, b in pairs_a])
-    edge_b = lax.ppermute(edge_b, "tile", pairs_b + [(b, a) for a, b in pairs_b])
+    flux, firsts, lasts = call(
+        flux_kernel,
+        [(2, levels) + plane, (tracers * levels, cols), (tracers * levels, cols)],
+        [tracer, mix, weighted, face, other],
+    )
     flux, part = call(
-        flux_kernel,
+        column_kernel,
         [(2, levels) + plane, (2 * rows + 8, cols)],
-        [tracer_start, mixing, tracer_cot, land_mask, face, other, edge_a, edge_b, surface_cot, damping],
+        [flux, firsts, lasts, edge_a, edge_b, surface_cot, damping],
     )
     own = part + lax.ppermute(part, "depth", swap)
 
@@ -304,25 +345,19 @@
         pairs = [(2 * partner(t, for_top, tiles), 2 * t) for t in range(tiles)]
         pairs += [(2 * partner(t, for_bottom, tiles) + 1, 2 * t + 1) for t in range(tiles)]
         got.append(lax.ppermute(own, ("tile", "depth"), pairs))
-    swapped = [lax.ppermute(block, "depth", swap) for block in got]
-
-    (nums,) = call(
+    swapped = [lax.ppermute(piece, "depth", swap) for piece in got]
+
+    nums, last = call(
         adjoint_kernel,
-        [(levels, tracers) + plane],
-        [mixing, tracer_cot, land_mask, velocity, surface, edge_a, edge_b],
-        flops=20_000_000,
-    )
-    other_nums = lax.ppermute(nums[levels - 1], "depth", swap)
-    (adj_tracer,) = call(
-        finish_kernel,
-        [(tracers, levels) + plane],
-        [mixing, nums, face, other, other_nums],
-    )
+        [(levels - 1, tracers) + plane, (tracers,) + plane],
+        [mix, weighted, velocity, surface_in, edge_a, edge_b, own],
+    )
+    other_last = lax.ppermute(last, "depth", swap)
     height = tiles * rows
-    adj_velocity, adj_surface = call(
+    return call(
         functools.partial(solve_kernel, tiles, partners),
-        [(2, levels) + plane, plane],
-        [flux, own] + got + swapped,
+        [block, (2, levels) + plane, plane],
+        [flux, mix, nums, last, face, other, other_last, own] + got + swapped,
         scratch=[
             pltpu.VMEM((height, cols), F32),
             pltpu.VMEM((height, cols), F32),
@@ -330,9 +365,11 @@
             pltpu.VMEM((height + 16, cols), F32),
             pltpu.VMEM((height, cols), F32),
             pltpu.VMEM((rows + 16, cols), F32),
+            pltpu.VMEM(block, F32),
+            pltpu.SemaphoreType.DMA(()),
         ],
-    )
-    return adj_tracer, adj_velocity, adj_surface
+        hbm_out=(0,),
+    )
 
 
 def solution(mesh):

time: 38.4 us -> 35.6 us (0.927)
  starting transfers between devices: 21.2 us -> 15.2 us
  waiting for transfers between devices: 2.65 us -> 7.42 us
  Pallas kernels: 7.64 us -> 6.92 us
  local copies, waits for them, and re-layouts: 5.68 us -> 5.03 us
    ppermute x5, starting transfers between devices: 6.38 us -> 1.14 us  [the longest x4 0.91 us: body(): swapped = [lax.ppermute(piece, 'depth', swap) for piece in got]]
    ppermute x4, waiting for transfers between devices: 0.01 us -> 4.38 us  [body(): got.append(lax.ppermute(own, ('tile', 'depth'), pairs))]
    ppermute x5, waiting for transfers between devices: 0.01 us -> 1.2 us  [the longest x4 1.19 us: body(): swapped = [lax.ppermute(piece, 'depth', swap) for piece in got]]
    ppermute x1, waiting for transfers between devices: 1.37 us -> 0.58 us  [body(): lax.ppermute(edge_a, 'tile', pairs_a + [(b, a) for a, b in pairs_a])]
    pallas_call x5, Pallas kernels: 7.64 us -> 6.92 us  [call(): pl.pallas_call(kernel, out_shape=[jax.ShapeDtypeStruct(s, F32) for s in o...]
    ppermute x4, starting transfers between devices: 10.9 us -> 10.2 us  [body(): got.append(lax.ppermute(own, ('tile', 'depth'), pairs))]
    unnamed x22 -> x16, local copies, waits for them, and re-layouts: 5.66 us -> 5.03 us
  transfers between devices with their start and end apart: 13 -> 13, of which waited for: 2 -> 6; matrix products, arithmetic and copies ran while one was open for 0% -> 0% of each run, Pallas kernels for 9% -> 2%
where the time goes in v2:
time: 35.6 us; the launch traced here: 35.3 us
  starting transfers between devices  15.2 us (43%)
  waiting for transfers between devices  7.42 us (21%)
  Pallas kernels  6.92 us (19%)
  local copies, waits for them, and re-layouts  5.03 us (14%)
  between operations  0.75 us (2%)
    ppermute x4, starting transfers between devices, body(): got.append(lax.ppermute(own, ('tile', 'depth'), pairs))  10.2 us
    pallas_call x5, Pallas kernels, call(): pl.pallas_call(kernel, out_shape=[jax.ShapeDtypeStruct(s, F32) for s in o...  6.92 us
    unnamed x16, local copies, waits for them, and re-layouts  5.03 us
    ppermute x4, waiting for transfers between devices, body(): got.append(lax.ppermute(own, ('tile', 'depth'), pairs))  4.38 us
    ppermute x1, starting transfers between devices, body(): lax.ppermute(edge_a, 'tile', pairs_a + [(b, a) for a, b in pairs_a])  2.59 us
    ppermute x1, waiting for transfers between devices, body(): own = part + lax.ppermute(part, 'depth', swap)  1.25 us
    ppermute x4, waiting for transfers between devices, body(): swapped = [lax.ppermute(piece, 'depth', swap) for piece in got]  1.19 us
    ppermute x4, starting transfers between devices, body(): swapped = [lax.ppermute(piece, 'depth', swap) for piece in got]  0.91 us
  transfers between devices with their start and end apart: 13, of which 6 were waited for; matrix products, arithmetic and copies ran while one was open for 0% of the time, Pallas kernels for 2%

profile of v2, /device:TPU:0, one launch (start us, length us, event | category | flops | bytes accessed | tf_op | source)
XLA Modules:
  0.0 35.3 jit_solution(16719587637505906049)
XLA Ops:
  0.6 0.0 copy-start
  0.6 1.2 %copy-done = f32[8,4,32,256]{3,2,1,0:T(8,128)S(1)} copy-done((f32[8,4,32,256]{3,2,1,0:T(8,128)S(1)}, f32[8,4,32,256]{3,2,1,0:T(8,128)}, u32[]{:S(2)}) %copy-start) | copy-done | bytes 1048600
  1.9 0.0 copy-start.1
  1.9 1.2 %copy-done.1 = f32[8,4,32,256]{3,2,1,0:T(8,128)S(1)} copy-done((f32[8,4,32,256]{3,2,1,0:T(8,128)S(1)}, f32[8,4,32,256]{3,2,1,0:T(8,128)}, u32[]{:S(2)}) %copy-start.1) | copy-done | bytes 1048600
  3.1 0.0 copy-start.3
  3.1 0.9 %copy-done.3 = f32[4,32,256]{2,1,0:T(8,128)S(1)} copy-done((f32[4,32,256]{2,1,0:T(8,128)S(1)}, f32[4,32,256]{2,1,0:T(8,128)}, u32[]{:S(2)}) %copy-start.3) | copy-done | bytes 131096
  4.0 0.0 copy-start.4
  4.0 0.9 %copy-done.4 = s32[4,32,256]{2,1,0:T(8,128)S(1)} copy-done((s32[4,32,256]{2,1,0:T(8,128)S(1)}, s32[4,32,256]{2,1,0:T(8,128)}, u32[]{:S(2)}) %copy-start.4) | copy-done | bytes 131096
  4.9 0.0 copy-start.5
  4.9 0.8 %copy-done.5 = f32[32,256]{1,0:T(8,128)S(1)} copy-done((f32[32,256]{1,0:T(8,128)S(1)}, f32[32,256]{1,0:T(8,128)}, u32[]{:S(2)}) %copy-start.5) | copy-done | bytes 32792
  5.7 0.7 %shard_map.103 = (f32[8,4,32,256]{3,2,1,0:T(8,128)S(1)}, f32[4,32,256]{2,1,0:T(8,128)S(1)}, f32[8,4,32,256]{3,2,1,0:T(8,128)S(1)}, f32[32,256]{1,0:T(8,128)S(1)}...) custom-call(f32[8,4,32,256]{3,2,1,0:T(8,128)S(1)} %copy-done, ...), custom_call_target="tpu_custom_call" | custom-call | flops 2000000 | bytes 5062656 | tf_op jit(solution)/shard_map/pallas_call | solution.py:22
  6.4 0.5 %collective-permute-start = (f32[10,32,256]{2,1,0:T(8,128)S(1)}, f32[10,32,256]{2,1,0:T(8,128)S(1)}, u32[]{:S(2)}, u32[]{:S(2)}) collective-permute-start(f32[10,32,256]{2,1,0:T(8,128)S(1)} %get-tuple-element.20.face), channel_id=1, source_target_pairs={{0,1},{1,0},{2,3},{3,2},{4,5},{5,4},{6,7},{7,6},{8,9},{9,8},{10,11... | collective-permute-start | bytes 983048 | tf_op jit(solution)/shard_map/ppermute | solution.py:327
  6.9 2.6 %collective-permute-start.1 = (f32[40,256]{1,0:T(8,128)S(1)}, f32[40,256]{1,0:T(8,128)S(1)}, u32[]{:S(2)}, u32[]{:S(2)}) collective-permute-start(f32[40,256]{1,0:T(8,128)S(1)} %get-tuple-element.24), channel_id=1, source_target_pairs={{0,2},{4,6},{8,10},{12,14},{2,0},{6,4},{10,8},{14,12},{1,3},{5,7},... | collective-permute-start | bytes 122888 | tf_op jit(solution)/shard_map/ppermute | solution.py:329
  9.5 0.7 %collective-permute-start.2 = (f32[40,256]{1,0:T(8,128)S(1)}, f32[40,256]{1,0:T(8,128)S(1)}, u32[]{:S(2)}, u32[]{:S(2)}) collective-permute-start(f32[40,256]{1,0:T(8,128)S(1)} %get-tuple-element.25), channel_id=1, source_target_pairs={{2,4},{6,8},{10,12},{4,2},{8,6},{12,10},{3,5},{7,9},{11,13},{5,3},... | collective-permute-start | bytes 122888 | tf_op jit(solution)/shard_map/ppermute | solution.py:328
  10.2 0.0 collective-permute-done.other
  10.2 0.0 copy-start.6
  10.2 0.0 copy-start.7
  10.2 0.9 %shard_map.104 = (f32[2,4,32,256]{3,2,1,0:T(8,128)S(1)}, f32[32,256]{1,0:T(8,128)S(1)}, f32[32,256]{1,0:T(8,128)S(1)}) custom-call(f32[8,4,32,256]{3,2,1,0:T(8,128)S(1)} %get-tuple-element.17.tracer, f32[4,32,256]{2,1,0:T(8,128)S(1)} %get-tuple-element.18.mix, f32[8,4,32,256]{3,2,1,0:T(8,128)S(1)} %get-tuple-element.19.weighted.weighted_in, ...), custom_call_target="tpu_custom_call" | custom-call | flops 2000000 | bytes 3211264 | tf_op jit(solution)/shard_map/pallas_call | solution.py:22
  11.1 0.6 %collective-permute-done.1.edge_a = f32[40,256]{1,0:T(8,128)S(1)} collective-permute-done((f32[40,256]{1,0:T(8,128)S(1)}, f32[40,256]{1,0:T(8,128)S(1)}, u32[]{:S(2)}, u32[]{:S(2)}) %collective-permute-start.1) | collective-permute-done | bytes 40992 | tf_op jit(solution)/shard_map/ppermute | solution.py:329
  11.7 0.0 collective-permute-done.2.edge_b
  11.7 0.0 copy-done.6
  11.7 0.0 copy-done.7
  11.7 0.0 copy-start.2
  11.7 0.1 shard_map.105
  11.8 0.1 collective-permute-start.3
  11.9 1.3 %collective-permute-done.3 = f32[72,256]{1,0:T(8,128)S(1)} collective-permute-done((f32[72,256]{1,0:T(8,128)S(1)}, f32[72,256]{1,0:T(8,128)S(1)}, u32[]{:S(2)}, u32[]{:S(2)}) %collective-permute-start.3) | collective-permute-done | bytes 73760 | tf_op jit(solution)/shard_map/ppermute | solution.py:340
  13.1 0.0 copy-done.2
  13.2 0.9 %shard_map.106 = (f32[3,8,32,256]{3,2,1,0:T(8,128)S(1)}, f32[8,32,256]{2,1,0:T(8,128)S(1)}) custom-call(f32[4,32,256]{2,1,0:T(8,128)S(1)} %get-tuple-element.18.mix, f32[8,4,32,256]{3,2,1,0:T(8,128)S(1)} %get-tuple-element.19.weighted.weighted_in, f32[2,4,32,256]{3,2,1,0:T(8,128)S(1)} %copy-done.2, f32[32,256]{1,0:T(8,128)S(1)} %get-tuple-element.27.surface, ...), custom_call_target="tpu_custom_call" | custom-call | flops 2000000 | bytes 2678784 | tf_op jit(solution)/shard_map/pallas_call | solution.py:22
  14.1 0.2 collective-permute-start.4
  14.3 4.9 %collective-permute-start.8 = (f32[72,256]{1,0:T(8,128)S(1)}, f32[72,256]{1,0:T(8,128)S(1)}, u32[]{:S(2)}, u32[]{:S(2)}) collective-permute-start(f32[72,256]{1,0:T(8,128)S(1)} %add.3.after.own), channel_id=1, source_target_pairs={{14,0},{12,2},{10,4},{8,6},{6,8},{4,10},{2,12},{0,14},{13,1},{15,3... | collective-permute-start | bytes 221192 | tf_op jit(solution)/shard_map/ppermute | solution.py:347
  19.2 2.7 %collective-permute-start.7 = (f32[72,256]{1,0:T(8,128)S(1)}, f32[72,256]{1,0:T(8,128)S(1)}, u32[]{:S(2)}, u32[]{:S(2)}) collective-permute-start(f32[72,256]{1,0:T(8,128)S(1)} %add.3.after.own), channel_id=1, source_target_pairs={{8,0},{10,2},{12,4},{14,6},{0,8},{2,10},{4,12},{6,14},{11,1},{9,3}... | collective-permute-start | bytes 221192 | tf_op jit(solution)/shard_map/ppermute | solution.py:347
  21.9 1.1 %collective-permute-start.6 = (f32[72,256]{1,0:T(8,128)S(1)}, f32[72,256]{1,0:T(8,128)S(1)}, u32[]{:S(2)}, u32[]{:S(2)}) collective-permute-start(f32[72,256]{1,0:T(8,128)S(1)} %add.3.after.own), channel_id=1, source_target_pairs={{6,0},{4,2},{2,4},{0,6},{14,8},{12,10},{10,12},{8,14},{5,1},{7,3},... | collective-permute-start | bytes 221192 | tf_op jit(solution)/shard_map/ppermute | solution.py:347
  22.9 1.6 %collective-permute-start.5 = (f32[72,256]{1,0:T(8,128)S(1)}, f32[72,256]{1,0:T(8,128)S(1)}, u32[]{:S(2)}, u32[]{:S(2)}) collective-permute-start(f32[72,256]{1,0:T(8,128)S(1)} %add.3.after.own), channel_id=1, source_target_pairs={{2,0},{0,2},{6,4},{4,6},{10,8},{8,10},{14,12},{12,14},{3,1},{1,3},... | collective-permute-start | bytes 221192 | tf_op jit(solution)/shard_map/ppermute | solution.py:347
  24.5 0.0 collective-permute-done.8.refs_3_
  24.5 0.3 collective-permute-start.12
  24.9 4.4 %collective-permute-done.7.refs_2_ = f32[72,256]{1,0:T(8,128)S(1)} collective-permute-done((f32[72,256]{1,0:T(8,128)S(1)}, f32[72,256]{1,0:T(8,128)S(1)}, u32[]{:S(2)}, u32[]{:S(2)}) %collective-permute-start.7) | collective-permute-done | bytes 73760 | tf_op jit(solution)/shard_map/ppermute | solution.py:347
  29.2 0.0 collective-permute-start.11
  29.2 0.0 collective-permute-done.6.refs_1_
  29.2 0.5 %collective-permute-start.10 = (f32[72,256]{1,0:T(8,128)S(1)}, f32[72,256]{1,0:T(8,128)S(1)}, u32[]{:S(2)}, u32[]{:S(2)}) collective-permute-start(f32[72,256]{1,0:T(8,128)S(1)} %collective-permute-done.6.refs_1_), channel_id=1, source_target_pairs={{0,1},{1,0},{2,3},{3,2},{4,5},{5,4},{6,7},{7,6},{8,9},{9,8},{10,11... | collective-permute-start | bytes 221192 | tf_op jit(solution)/shard_map/ppermute | solution.py:348
  29.7 0.0 collective-permute-done.5.refs_0_
  29.8 0.1 collective-permute-start.9
  29.8 0.0 collective-permute-done.12.refs_7_
  29.8 0.7 %collective-permute-done.11.refs_6_ = f32[72,256]{1,0:T(8,128)S(1)} collective-permute-done((f32[72,256]{1,0:T(8,128)S(1)}, f32[72,256]{1,0:T(8,128)S(1)}, u32[]{:S(2)}, u32[]{:S(2)}) %collective-permute-start.11) | collective-permute-done | bytes 73760 | tf_op jit(solution)/shard_map/ppermute | solution.py:348
  30.5 0.2 collective-permute-done.10.refs_5_
  30.7 0.4 %collective-permute-done.9.refs_4_ = f32[72,256]{1,0:T(8,128)S(1)} collective-permute-done((f32[72,256]{1,0:T(8,128)S(1)}, f32[72,256]{1,0:T(8,128)S(1)}, u32[]{:S(2)}, u32[]{:S(2)}) %collective-permute-start.9) | collective-permute-done | bytes 73760 | tf_op jit(solution)/shard_map/ppermute | solution.py:348
  31.0 0.0 collective-permute-done.4.other_last
  31.0 4.3 %shard_map.107 = (f32[8,4,32,256]{3,2,1,0:T(8,128)}, f32[2,4,32,256]{3,2,1,0:T(8,128)}, f32[32,256]{1,0:T(8,128)}) custom-call(f32[2,4,32,256]{3,2,1,0:T(8,128)S(1)} %get-tuple-element.26.flux, f32[4,32,256]{2,1,0:T(8,128)S(1)} %get-tuple-element.18.mix, f32[3,8,32,256]{3,2,1,0:T(8,128)S(1)} %get-tuple-element.29.nums, ...), custom_call_target="tpu_custom_call" | custom-call | flops 2000000 | bytes 4366336 | tf_op jit(solution)/shard_map/pallas_call | solution.py:22
  (1 shorter events, 0.0 us)
Async XLA Ops:
  0.6 1.2 %copy-start = (f32[8,4,32,256]{3,2,1,0:T(8,128)S(1)}, f32[8,4,32,256]{3,2,1,0:T(8,128)}, u32[]{:S(2)}) copy-start(f32[8,4,32,256]{3,2,1,0:T(8,128)} %tracer_in.1) | copy-start | bytes 3145732
  1.9 1.2 %copy-start.1 = (f32[8,4,32,256]{3,2,1,0:T(8,128)S(1)}, f32[8,4,32,256]{3,2,1,0:T(8,128)}, u32[]{:S(2)}) copy-start(f32[8,4,32,256]{3,2,1,0:T(8,128)} %cot_in.1) | copy-start | bytes 3145732
  3.1 0.9 %copy-start.3 = (f32[4,32,256]{2,1,0:T(8,128)S(1)}, f32[4,32,256]{2,1,0:T(8,128)}, u32[]{:S(2)}) copy-start(f32[4,32,256]{2,1,0:T(8,128)} %mix_in.1) | copy-start | bytes 393220
  4.0 0.9 %copy-start.4 = (s32[4,32,256]{2,1,0:T(8,128)S(1)}, s32[4,32,256]{2,1,0:T(8,128)}, u32[]{:S(2)}) copy-start(s32[4,32,256]{2,1,0:T(8,128)} %mask_in.1) | copy-start | bytes 393220
  4.9 0.8 %copy-start.5 = (f32[32,256]{1,0:T(8,128)S(1)}, f32[32,256]{1,0:T(8,128)}, u32[]{:S(2)}) copy-start(f32[32,256]{1,0:T(8,128)} %surface_in.1) | copy-start | bytes 98308
  6.4 3.8 %collective-permute-start = (f32[10,32,256]{2,1,0:T(8,128)S(1)}, f32[10,32,256]{2,1,0:T(8,128)S(1)}, u32[]{:S(2)}, u32[]{:S(2)}) collective-permute-start(f32[10,32,256]{2,1,0:T(8,128)S(1)} %get-tuple-element.20.face), channel_id=1, source_target_pairs={{0,1},{1,0},{2,3},{3,2},{4,5},{5,4},{6,7},{7,6},{8,9},{9,8},{10,11... | collective-permute-start | bytes 983048 | tf_op jit(solution)/shard_map/ppermute | solution.py:327
  6.9 4.8 %collective-permute-start.1 = (f32[40,256]{1,0:T(8,128)S(1)}, f32[40,256]{1,0:T(8,128)S(1)}, u32[]{:S(2)}, u32[]{:S(2)}) collective-permute-start(f32[40,256]{1,0:T(8,128)S(1)} %get-tuple-element.24), channel_id=1, source_target_pairs={{0,2},{4,6},{8,10},{12,14},{2,0},{6,4},{10,8},{14,12},{1,3},{5,7},... | collective-permute-start | bytes 122888 | tf_op jit(solution)/shard_map/ppermute | solution.py:329
  9.5 2.2 %collective-permute-start.2 = (f32[40,256]{1,0:T(8,128)S(1)}, f32[40,256]{1,0:T(8,128)S(1)}, u32[]{:S(2)}, u32[]{:S(2)}) collective-permute-start(f32[40,256]{1,0:T(8,128)S(1)} %get-tuple-element.25), channel_id=1, source_target_pairs={{2,4},{6,8},{10,12},{4,2},{8,6},{12,10},{3,5},{7,9},{11,13},{5,3},... | collective-permute-start | bytes 122888 | tf_op jit(solution)/shard_map/ppermute | solution.py:328
  10.2 1.5 %copy-start.6 = (f32[32,256]{1,0:T(8,128)S(1)}, f32[32,256]{1,0:T(8,128)}, u32[]{:S(2)}) copy-start(f32[32,256]{1,0:T(8,128)} %surface_cot.1) | copy-start | bytes 98308
  10.2 1.5 %copy-start.7 = (f32[32,256]{1,0:T(8,128)S(1)}, f32[32,256]{1,0:T(8,128)}, u32[]{:S(2)}) copy-start(f32[32,256]{1,0:T(8,128)} %damping.1) | copy-start | bytes 98308
  11.7 1.5 %copy-start.2 = (f32[2,4,32,256]{3,2,1,0:T(8,128)S(1)}, f32[2,4,32,256]{3,2,1,0:T(8,128)}, u32[]{:S(2)}) copy-start(f32[2,4,32,256]{3,2,1,0:T(8,128)} %velocity.1) | copy-start | bytes 786436
  11.8 1.3 %collective-permute-start.3 = (f32[72,256]{1,0:T(8,128)S(1)}, f32[72,256]{1,0:T(8,128)S(1)}, u32[]{:S(2)}, u32[]{:S(2)}) collective-permute-start(f32[72,256]{1,0:T(8,128)S(1)} %get-tuple-element.28), channel_id=1, source_target_pairs={{0,1},{1,0},{2,3},{3,2},{4,5},{5,4},{6,7},{7,6},{8,9},{9,8},{10,11... | collective-permute-start | bytes 221192 | tf_op jit(solution)/shard_map/ppermute | solution.py:340
  14.1 17.0 %collective-permute-start.4 = (f32[8,32,256]{2,1,0:T(8,128)S(1)}, f32[8,32,256]{2,1,0:T(8,128)S(1)}, u32[]{:S(2)}, u32[]{:S(2)}) collective-permute-start(f32[8,32,256]{2,1,0:T(8,128)S(1)} %get-tuple-element.30.last), channel_id=1, source_target_pairs={{0,1},{1,0},{2,3},{3,2},{4,5},{5,4},{6,7},{7,6},{8,9},{9,8},{10,11... | collective-permute-start | bytes 786440 | tf_op jit(solution)/shard_map/ppermute | solution.py:355
  14.3 10.2 %collective-permute-start.8 = (f32[72,256]{1,0:T(8,128)S(1)}, f32[72,256]{1,0:T(8,128)S(1)}, u32[]{:S(2)}, u32[]{:S(2)}) collective-permute-start(f32[72,256]{1,0:T(8,128)S(1)} %add.3.after.own), channel_id=1, source_target_pairs={{14,0},{12,2},{10,4},{8,6},{6,8},{4,10},{2,12},{0,14},{13,1},{15,3... | collective-permute-start | bytes 221192 | tf_op jit(solution)/shard_map/ppermute | solution.py:347
  19.2 10.1 %collective-permute-start.7 = (f32[72,256]{1,0:T(8,128)S(1)}, f32[72,256]{1,0:T(8,128)S(1)}, u32[]{:S(2)}, u32[]{:S(2)}) collective-permute-start(f32[72,256]{1,0:T(8,128)S(1)} %add.3.after.own), channel_id=1, source_target_pairs={{8,0},{10,2},{12,4},{14,6},{0,8},{2,10},{4,12},{6,14},{11,1},{9,3}... | collective-permute-start | bytes 221192 | tf_op jit(solution)/shard_map/ppermute | solution.py:347
  21.9 7.4 %collective-permute-start.6 = (f32[72,256]{1,0:T(8,128)S(1)}, f32[72,256]{1,0:T(8,128)S(1)}, u32[]{:S(2)}, u32[]{:S(2)}) collective-permute-start(f32[72,256]{1,0:T(8,128)S(1)} %add.3.after.own), channel_id=1, source_target_pairs={{6,0},{4,2},{2,4},{0,6},{14,8},{12,10},{10,12},{8,14},{5,1},{7,3},... | collective-permute-start | bytes 221192 | tf_op jit(solution)/shard_map/ppermute | solution.py:347
  22.9 6.8 %collective-permute-start.5 = (f32[72,256]{1,0:T(8,128)S(1)}, f32[72,256]{1,0:T(8,128)S(1)}, u32[]{:S(2)}, u32[]{:S(2)}) collective-permute-start(f32[72,256]{1,0:T(8,128)S(1)} %add.3.after.own), channel_id=1, source_target_pairs={{2,0},{0,2},{6,4},{4,6},{10,8},{8,10},{14,12},{12,14},{3,1},{1,3},... | collective-permute-start | bytes 221192 | tf_op jit(solution)/shard_map/ppermute | solution.py:347
  24.5 5.3 %collective-permute-start.12 = (f32[72,256]{1,0:T(8,128)S(1)}, f32[72,256]{1,0:T(8,128)S(1)}, u32[]{:S(2)}, u32[]{:S(2)}) collective-permute-start(f32[72,256]{1,0:T(8,128)S(1)} %collective-permute-done.8.refs_3_), channel_id=1, source_target_pairs={{0,1},{1,0},{2,3},{3,2},{4,5},{5,4},{6,7},{7,6},{8,9},{9,8},{10,11... | collective-permute-start | bytes 221192 | tf_op jit(solution)/shard_map/ppermute | solution.py:348
  29.2 1.3 %collective-permute-start.11 = (f32[72,256]{1,0:T(8,128)S(1)}, f32[72,256]{1,0:T(8,128)S(1)}, u32[]{:S(2)}, u32[]{:S(2)}) collective-permute-start(f32[72,256]{1,0:T(8,128)S(1)} %collective-permute-done.7.refs_2_), channel_id=1, source_target_pairs={{0,1},{1,0},{2,3},{3,2},{4,5},{5,4},{6,7},{7,6},{8,9},{9,8},{10,11... | collective-permute-start | bytes 221192 | tf_op jit(solution)/shard_map/ppermute | solution.py:348
  29.2 1.4 %collective-permute-start.10 = (f32[72,256]{1,0:T(8,128)S(1)}, f32[72,256]{1,0:T(8,128)S(1)}, u32[]{:S(2)}, u32[]{:S(2)}) collective-permute-start(f32[72,256]{1,0:T(8,128)S(1)} %collective-permute-done.6.refs_1_), channel_id=1, source_target_pairs={{0,1},{1,0},{2,3},{3,2},{4,5},{5,4},{6,7},{7,6},{8,9},{9,8},{10,11... | collective-permute-start | bytes 221192 | tf_op jit(solution)/shard_map/ppermute | solution.py:348
  29.8 1.3 %collective-permute-start.9 = (f32[72,256]{1,0:T(8,128)S(1)}, f32[72,256]{1,0:T(8,128)S(1)}, u32[]{:S(2)}, u32[]{:S(2)}) collective-permute-start(f32[72,256]{1,0:T(8,128)S(1)} %collective-permute-done.5.refs_0_), channel_id=1, source_target_pairs={{0,1},{1,0},{2,3},{3,2},{4,5},{5,4},{6,7},{7,6},{8,9},{9,8},{10,11... | collective-permute-start | bytes 221192 | tf_op jit(solution)/shard_map/ppermute | solution.py:348

commit v3 on v2

--- a/solution.py
+++ b/solution.py
@@ -17,7 +17,7 @@
 HBM = pl.BlockSpec(memory_space=pltpu.HBM)
 
 
-def call(kernel, outs, args, scratch=(), flops=2_000_000, hbm_in=(), hbm_out=()):
+def call(kernel, outs, args, scratch=(), flops=2_000_000, hbm_in=(), hbm_out=(), vmem=40):
     nbytes = sum(a.size * 4 for a in args) + sum(4 * functools.reduce(lambda p, q: p * q, s) for s in outs)
     return pl.pallas_call(
         kernel,
@@ -26,7 +26,7 @@
         out_specs=[HBM if i in hbm_out else VMEM for i in range(len(outs))],
         scratch_shapes=list(scratch),
         cost_estimate=pl.CostEstimate(flops=flops, bytes_accessed=nbytes, transcendentals=0),
-        compiler_params=pltpu.CompilerParams(vmem_limit_bytes=40 * 1024 * 1024),
+        compiler_params=pltpu.CompilerParams(vmem_limit_bytes=int(vmem * 1024 * 1024)),
     )(*args)
 
 
@@ -70,11 +70,12 @@
     return (other_rest + link) * inv, link * inv
 
 
-def start_kernel(tracer_in, mix_in, cot_in, mask_in, surface_in, tracer, mix, weighted, surface, face, edge_a, edge_b, cot, mask, sems):
+def start_kernel(tracer_in, mix_in, cot_in, mask_in, surface_in, face, edge_b, edge_a, tracer, mix, surface, cot, mask, sems):
     tracers, levels, rows, _ = tracer.shape
     depth = lax.axis_index("depth")
     odd = lax.rem(lax.axis_index("tile"), 2) == 1
-    moves = [(mix_in, mix), (tracer_in, tracer), (surface_in, surface), (mask_in, mask), (cot_in, cot)]
+    moves = [(mix_in, mix), (tracer_in, tracer), (surface_in, surface), (mask_in, mask)]
+    moves += [(cot_in.at[:, :, 0:8], cot.at[0]), (cot_in.at[:, :, rows - 8 : rows], cot.at[1])]
     copies = [pltpu.make_async_copy(src, dst, sems.at[i]) for i, (src, dst) in enumerate(moves)]
     for copy in copies:
         copy.start()
@@ -91,12 +92,12 @@
     for copy in copies[2:]:
         copy.wait()
     for lev in range(levels):
-        wet = mask[lev].astype(F32)
+        first_wet = mask[lev, 0:1].astype(F32)
+        last_wet = mask[lev, rows - 1 : rows].astype(F32)
         for tr in range(tracers):
-            block = cot[tr, lev] * wet
-            weighted[tr, lev] = block
-            first, last = block[0:1], block[rows - 1 : rows]
-            at = tr * levels + lev
+            first = cot[0, tr, lev, 0:1] * first_wet
+            last = cot[1, tr, lev, 7:8] * last_wet
+            at = lev * tracers + tr
             edge_a[at : at + 1] = jnp.where(odd, first, last)
             edge_b[at : at + 1] = jnp.where(odd, last, first)
     at = tracers * levels
@@ -106,51 +107,77 @@
     edge_b[at : at + 1] = jnp.where(odd, surface[rows - 1 : rows], surface[0:1])
 
 
-def flux_kernel(tracer, mix, weighted, face, other, flux, firsts, lasts):
+def interior_kernel(tracer, mix, cot, mask, velocity, surface, other, flux, nums, last, packed, lines, speed):
     tracers, levels, rows, cols = tracer.shape
     depth = lax.axis_index("depth")
     inverse, ratio, rest = chain(mix, depth)
     own_w, other_w = meet(rest, other[tracers], mix[levels - 1], other[tracers + 1], depth)
+    right, left = lane_shifts(surface[...])
+    down, up = row_shifts(surface[...], 0.0, 0.0)
+    for lev in range(levels):
+        speed[0, lev] = ADVECT * (velocity[0, lev] - GRAVITY * (right - left))
+        along = ADVECT * (velocity[1, lev] - GRAVITY * (down - up))
+        speed[1, lev] = along
+        lines[lev : lev + 1] = along[0:1]
+        lines[levels + lev : levels + lev + 1] = along[rows - 1 : rows]
+    lines[2 * levels : 4 * levels] = jnp.zeros((2 * levels, cols), F32)
+    for j in range(levels - 1):
+        at = 2 * levels + j
+        lines[at : at + 1] = ratio[j][0:1]
+        lines[at + levels : at + levels + 1] = ratio[j][rows - 1 : rows]
     flux[...] = jnp.zeros_like(flux)
     for tr in range(tracers):
-        nums = [tracer[tr, level(0, depth, levels)]]
+        held = [tracer[tr, level(0, depth, levels)]]
         for j in range(1, levels):
-            nums.append(tracer[tr, level(j, depth, levels)] + ratio[j - 1] * nums[-1])
-        value = own_w * nums[-1] + other_w * other[tr]
+            held.append(tracer[tr, level(j, depth, levels)] + ratio[j - 1] * held[-1])
+        value = own_w * held[-1] + other_w * other[tr]
+        outs = [None] * levels
         for j in range(levels - 1, -1, -1):
             lev = level(j, depth, levels)
             if j < levels - 1:
-                value = inverse[j] * nums[j] + ratio[j] * value
-            block = weighted[tr, lev]
+                value = inverse[j] * held[j] + ratio[j] * value
+            block = cot[tr, lev] * mask[lev].astype(F32)
             right, left = lane_shifts(block)
             down, up = row_shifts(block, 0.0, 0.0)
-            flux[0, lev] += ADVECT * (value * (right - left))
-            flux[1, lev] += ADVECT * (value * (down - up))
-            at = tr * levels + lev
-            firsts[pl.ds(at, 1)] = value[0:1]
-            lasts[pl.ds(at, 1)] = value[rows - 1 : rows]
-
-
-def column_kernel(flux_in, firsts, lasts, edge_a, edge_b, surface_cot, damping, flux, send):
+            across, along = right - left, down - up
+            flux[0, lev] += ADVECT * (value * across)
+            flux[1, lev] += ADVECT * (value * along)
+            outs[j] = (
+                block
+                + (speed[0, lev] * across + speed[1, lev] * along)
+                + DIFFUSE * (down + up + right + left - 4.0 * block)
+            )
+            at = lev * tracers + tr
+            packed[0, pl.ds(at, 1)] = value[0:1]
+            packed[1, pl.ds(at, 1)] = value[rows - 1 : rows]
+            packed[2, pl.ds(at, 1)] = block[1:2]
+            packed[3, pl.ds(at, 1)] = block[rows - 2 : rows - 1]
+        num = outs[0]
+        for j in range(1, levels):
+            nums[j - 1, tr] = num
+            num = outs[j] + ratio[j - 1] * num
+        last[tr] = num
+
+
+def column_kernel(flux_in, packed, lines, edge_b, edge_a, surface_cot, damping, flux, delta, send):
     levels, rows, cols = flux.shape[1:]
-    planes = firsts.shape[0]
+    tracers = delta.shape[2]
     depth = lax.axis_index("depth")
     odd = lax.rem(lax.axis_index("tile"), 2) == 1
-    row_a, row_b = edge_a[0:planes], edge_b[0:planes]
-    low = ADVECT * (firsts[...] * jnp.where(odd, row_a, row_b))
-    high = ADVECT * (lasts[...] * jnp.where(odd, row_b, row_a))
     row = lax.broadcasted_iota(jnp.int32, (rows, cols), 0)
     kind = lax.broadcasted_iota(jnp.int32, (8, cols), 0)
-    def by_level(terms):
-        return sum(terms[8 * i : 8 * (i + 1)] for i in range(planes // 8))
-
-    low, high = by_level(low), by_level(high)
+
+    def halo(at, size):
+        from_a, from_b = edge_a[pl.ds(at, size)], edge_b[pl.ds(at, size)]
+        return jnp.where(odd, from_a, from_b), jnp.where(odd, from_b, from_a)
+
     col_x = jnp.zeros((rows, cols), F32)
     col_y = jnp.zeros((rows, cols), F32)
     for lev in range(levels):
-        at_level = lax.rem(kind, levels) == lev
-        minus = jnp.sum(jnp.where(at_level, low, 0.0), axis=0, keepdims=True)
-        plus = jnp.sum(jnp.where(at_level, high, 0.0), axis=0, keepdims=True)
+        low, high = halo(lev * tracers, tracers)
+        at = slice(lev * tracers, (lev + 1) * tracers)
+        minus = ADVECT * jnp.sum(packed[0, at] * low, axis=0, keepdims=True)
+        plus = ADVECT * jnp.sum(packed[1, at] * high, axis=0, keepdims=True)
         flux_x = flux_in[0, lev]
         flux_y = flux_in[1, lev] + (jnp.where(row == rows - 1, plus, 0.0) - jnp.where(row == 0, minus, 0.0))
         flux[0, lev] = flux_x
@@ -165,43 +192,24 @@
     send[rows : rows + 8] = jnp.where(kind == 0, col_y[0:1], jnp.where(kind == 1, col_y[rows - 1 : rows], 0.0))
     send[rows + 8 : 2 * rows + 8] = jnp.where(top, damping[...], 0.0)
 
-
-def adjoint_kernel(mix, weighted_in, velocity, surface, edge_a, edge_b, after, nums, last):
-    tracers, levels, rows, cols = weighted_in.shape
-    depth = lax.axis_index("depth")
-    odd = lax.rem(lax.axis_index("tile"), 2) == 1
-    _, ratio, _ = chain(mix, depth)
-    at = tracers * levels
-    row_a, row_b = edge_a[at : at + 1], edge_b[at : at + 1]
-    low, high = jnp.where(odd, row_a, row_b), jnp.where(odd, row_b, row_a)
-    right, left = lane_shifts(surface[...])
-    down, up = row_shifts(surface[...], low, high)
-    slope_x, slope_y = GRAVITY * (right - left), GRAVITY * (down - up)
+    low_s, high_s = halo(levels * tracers, 8)
+    low_s, high_s = ADVECT * GRAVITY * low_s[0:1], ADVECT * GRAVITY * high_s[0:1]
     for j in range(levels):
         lev = level(j, depth, levels)
-        u_eff = ADVECT * (velocity[0, lev] - slope_x)
-        v_eff = ADVECT * (velocity[1, lev] - slope_y)
-        for tr in range(tracers):
-            weighted = weighted_in[tr, lev]
-            at = tr * levels + lev
-            row_a, row_b = edge_a[pl.ds(at, 1)], edge_b[pl.ds(at, 1)]
-            low, high = jnp.where(odd, row_a, row_b), jnp.where(odd, row_b, row_a)
-            right, left = lane_shifts(weighted)
-            down, up = row_shifts(weighted, low, high)
-            out = (
-                weighted
-                + (u_eff * (right - left) + v_eff * (down - up))
-                + DIFFUSE * (down + up + right + left - 4.0 * weighted)
-            )
-            if j > 0:
-                out = out + ratio[j - 1] * nums[j - 1, tr]
-            if j < levels - 1:
-                nums[j, tr] = out
-            else:
-                last[tr] = out
-
-
-def solve_kernel(tiles, partners, flux, mix, nums, last, face, other, other_last, own, *refs):
+        at = pl.multiple_of(lev * tracers, tracers)
+        low, high = halo(at, tracers)
+        first = low_s * packed[2, pl.ds(at, tracers)] + (DIFFUSE - (lines[pl.ds(lev, 1)] + low_s)) * low
+        final = high_s * packed[3, pl.ds(at, tracers)] + (DIFFUSE + (lines[pl.ds(levels + lev, 1)] - high_s)) * high
+        if j > 0:
+            first = first + lines[2 * levels + j - 1 : 2 * levels + j] * delta[0, j - 1]
+            final = final + lines[3 * levels + j - 1 : 3 * levels + j] * delta[1, j - 1]
+        delta[0, j] = first
+        delta[1, j] = final
+    send[2 * rows + 8 : 2 * rows + 8 + tracers] = delta[0, levels - 1]
+    send[2 * rows + 8 + tracers : 2 * rows + 8 + 2 * tracers] = delta[1, levels - 1]
+
+
+def solve_kernel(tiles, partners, flux, mix, nums, last, delta, other, other_last, swept, own, *refs):
     steps = len(partners)
     got, swapped = refs[:steps], refs[steps : 2 * steps]
     adj_tracer_out, adj_velocity, adj_surface = refs[2 * steps : 2 * steps + 3]
@@ -213,11 +221,21 @@
     tracers = last.shape[0]
     inverse, ratio, rest = chain(mix, depth)
     own_w, other_w = meet(rest, other[tracers], mix[levels - 1], other[tracers + 1], depth)
+    row = lax.broadcasted_iota(jnp.int32, (rows, cols), 0)
+    far = 2 * rows + 8
+
+    def with_rows(block, first, final):
+        return block + (jnp.where(row == 0, first, 0.0) + jnp.where(row == rows - 1, final, 0.0))
+
     for tr in range(tracers):
-        value = own_w * last[tr] + other_w * other_last[tr]
+        num = with_rows(last[tr], delta[0, levels - 1, tr : tr + 1], delta[1, levels - 1, tr : tr + 1])
+        at = far + tr
+        other_num = with_rows(other_last[tr], swept[at : at + 1], swept[at + tracers : at + tracers + 1])
+        value = own_w * num + other_w * other_num
         adj_tracer[tr, level(levels - 1, depth, levels)] = value
         for j in range(levels - 2, -1, -1):
-            value = inverse[j] * nums[j, tr] + ratio[j] * value
+            num = with_rows(nums[j, tr], delta[0, j, tr : tr + 1], delta[1, j, tr : tr + 1])
+            value = inverse[j] * num + ratio[j] * value
             adj_tracer[tr, level(j, depth, levels)] = value
     copy_out = pltpu.make_async_copy(adj_tracer, adj_tracer_out, sem)
     copy_out.start()
@@ -240,7 +258,6 @@
     total = jnp.zeros((rows, cols), F32)
     direc[0:pad] = jnp.zeros((pad, cols), F32)
     direc[pad + tiles * rows : 2 * pad + tiles * rows] = jnp.zeros((pad, cols), F32)
-    row = lax.broadcasted_iota(jnp.int32, (rows, cols), 0)
     for t in range(tiles):
         above = edges[8 * t + 1 : 8 * t + 2]
         below = edges[8 * (t + 2) : 8 * (t + 2) + 1]
@@ -315,29 +332,41 @@
     plane = (rows, cols)
     block = (tracers, levels) + plane
     edge = (tracers * levels + 8, cols)
-    tracer, mix, weighted, surface_in, face, edge_a, edge_b = call(
+    face, edge_b, edge_a = call(
         start_kernel,
-        [block, (levels,) + plane, block, plane, (tracers + 2,) + plane, edge, edge],
+        [(tracers + 2,) + plane, edge, edge],
         [tracer_start, mixing, tracer_cot, land_mask, surface],
-        scratch=[pltpu.VMEM(block, F32), pltpu.VMEM((levels,) + plane, jnp.int32), pltpu.SemaphoreType.DMA((5,))],
+        scratch=[
+            pltpu.VMEM(block, F32),
+            pltpu.VMEM((levels,) + plane, F32),
+            pltpu.VMEM(plane, F32),
+            pltpu.VMEM((2, tracers, levels, 8, cols), F32),
+            pltpu.VMEM((levels,) + plane, jnp.int32),
+            pltpu.SemaphoreType.DMA((6,)),
+        ],
         hbm_in=range(5),
+        vmem=56,
     )
     pairs_a = [(i, i + 1) for i in range(0, tiles - 1, 2)]
     pairs_b = [(i, i + 1) for i in range(1, tiles - 1, 2)]
     other = lax.ppermute(face, "depth", swap)
     edge_b = lax.ppermute(edge_b, "tile", pairs_b + [(b, a) for a, b in pairs_b])
     edge_a = lax.ppermute(edge_a, "tile", pairs_a + [(b, a) for a, b in pairs_a])
-    flux, firsts, lasts = call(
-        flux_kernel,
-        [(2, levels) + plane, (tracers * levels, cols), (tracers * levels, cols)],
-        [tracer, mix, weighted, face, other],
+    planes = tracers * levels
+    flux, nums, last, packed, lines = call(
+        interior_kernel,
+        [(2, levels) + plane, (levels - 1, tracers) + plane, (tracers,) + plane, (4, planes, cols), (4 * levels, cols)],
+        [tracer_start, mixing, tracer_cot, land_mask, velocity, surface, other],
+        scratch=[pltpu.VMEM((2, levels) + plane, F32)],
     )
-    flux, part = call(
+    other_last = lax.ppermute(last, "depth", swap)
+    flux, delta, part = call(
         column_kernel,
-        [(2, levels) + plane, (2 * rows + 8, cols)],
-        [flux, firsts, lasts, edge_a, edge_b, surface_cot, damping],
+        [(2, levels) + plane, (2, levels, tracers, cols), (2 * rows + 8 + 2 * tracers, cols)],
+        [flux, packed, lines, edge_b, edge_a, surface_cot, damping],
     )
-    own = part + lax.ppermute(part, "depth", swap)
+    swept = lax.ppermute(part, "depth", swap)
+    own = part[: 2 * rows + 8] + swept[: 2 * rows + 8]
 
     partners = partner_offsets(tiles)
     got = []
@@ -347,17 +376,11 @@
         got.append(lax.ppermute(own, ("tile", "depth"), pairs))
     swapped = [lax.ppermute(piece, "depth", swap) for piece in got]
 
-    nums, last = call(
-        adjoint_kernel,
-        [(levels - 1, tracers) + plane, (tracers,) + plane],
-        [mix, weighted, velocity, surface_in, edge_a, edge_b, own],
-    )
-    other_last = lax.ppermute(last, "depth", swap)
     height = tiles * rows
     return call(
         functools.partial(solve_kernel, tiles, partners),
         [block, (2, levels) + plane, plane],
-        [flux, mix, nums, last, face, other, other_last, own] + got + swapped,
+        [flux, mixing, nums, last, delta, other, other_last, swept, own] + got + swapped,
         scratch=[
             pltpu.VMEM((height, cols), F32),
             pltpu.VMEM((height, cols), F32),

time: 35.6 us -> 30.6 us (0.86)
  local copies, waits for them, and re-layouts: 5.03 us -> 0.97 us
  waiting for transfers between devices: 7.42 us -> 5.5 us
  Pallas kernels: 6.92 us -> 8.25 us
    unnamed x16, local copies, waits for them, and re-layouts: 5.03 us -> 0.97 us
    ppermute x4, starting transfers between devices: 10.2 us -> 7.26 us  [body(): got.append(lax.ppermute(own, ('tile', 'depth'), pairs))]
    ppermute x1, starting transfers between devices: 2.59 us -> 5.37 us  [body(): lax.ppermute(edge_a, 'tile', pairs_a + [(b, a) for a, b in pairs_a])]
    pallas_call x5 -> x4, Pallas kernels: 6.92 us -> 8.25 us  [call(): pl.pallas_call(kernel, out_shape=[jax.ShapeDtypeStruct(s, F32) for s in o...]
    ppermute x4, waiting for transfers between devices: 4.38 us -> 3.5 us  [body(): got.append(lax.ppermute(own, ('tile', 'depth'), pairs))]
    ppermute x1, waiting for transfers between devices: 0.58 us -> 0.01 us  [body(): lax.ppermute(edge_a, 'tile', pairs_a + [(b, a) for a, b in pairs_a])]
    ppermute x1, waiting for transfers between devices: 1.25 us -> 0.78 us  [body(): swept = lax.ppermute(part, 'depth', swap)]
  transfers between devices with their start and end apart: 13 -> 13, of which waited for: 6 -> 6; matrix products, arithmetic and copies ran while one was open for 0% -> 0% of each run, Pallas kernels for 2% -> 5%
where the time goes in v3:
time: 30.6 us; the launch traced here: 30.5 us
  starting transfers between devices  14.9 us (49%)
  Pallas kernels  8.25 us (27%)
  waiting for transfers between devices  5.5 us (18%)
  local copies, waits for them, and re-layouts  0.97 us (3%)
  between operations  0.79 us (3%)
    pallas_call x4, Pallas kernels, call(): pl.pallas_call(kernel, out_shape=[jax.ShapeDtypeStruct(s, F32) for s in o...  8.25 us
    ppermute x4, starting transfers between devices, body(): got.append(lax.ppermute(own, ('tile', 'depth'), pairs))  7.26 us
    ppermute x1, starting transfers between devices, body(): lax.ppermute(edge_a, 'tile', pairs_a + [(b, a) for a, b in pairs_a])  5.37 us
    ppermute x4, waiting for transfers between devices, body(): got.append(lax.ppermute(own, ('tile', 'depth'), pairs))  3.5 us
    ppermute x4, waiting for transfers between devices, body(): swapped = [lax.ppermute(piece, 'depth', swap) for piece in got]  1.21 us
    unnamed x16, local copies, waits for them, and re-layouts  0.97 us
    ppermute x1, waiting for transfers between devices, body(): swept = lax.ppermute(part, 'depth', swap)  0.78 us
    ppermute x1, starting transfers between devices, body(): lax.ppermute(edge_b, 'tile', pairs_b + [(b, a) for a, b in pairs_b])  0.65 us
  transfers between devices with their start and end apart: 13, of which 6 were waited for; matrix products, arithmetic and copies ran while one was open for 0% of the time, Pallas kernels for 5%

profile of v3, /device:TPU:0, one launch (start us, length us, event | category | flops | bytes accessed | tf_op | source)
XLA Modules:
  0.0 30.5 jit_solution(11198355142816203348)
XLA Ops:
  0.6 0.0 copy-start.2
  0.6 0.0 copy-start.1
  0.7 0.0 copy-start.3
  0.7 0.0 copy-start.5
  0.7 0.0 copy-start
  0.7 2.4 %shard_map.103 = (f32[10,32,256]{2,1,0:T(8,128)}, f32[40,256]{1,0:T(8,128)}, f32[40,256]{1,0:T(8,128)}) custom-call(f32[8,4,32,256]{3,2,1,0:T(8,128)} %tracer.1, f32[4,32,256]{2,1,0:T(8,128)} %mix.3, f32[8,4,32,256]{3,2,1,0:T(8,128)} %cot.1, s32[4,32,256]{2,1,0:T(8,128)} %mask.1, f32[32,256]{1,0:T(8,128)} %surface.1), custom_call_target="tpu_custom_call" | custom-call | flops 2000000 | bytes 2801664 | tf_op jit(solution)/shard_map/pallas_call | solution.py:22
  3.1 0.5 %collective-permute-start = (f32[10,32,256]{2,1,0:T(8,128)}, f32[10,32,256]{2,1,0:T(8,128)S(1)}, u32[]{:S(2)}, u32[]{:S(2)}) collective-permute-start(f32[10,32,256]{2,1,0:T(8,128)} %get-tuple-element.14), channel_id=1, source_target_pairs={{0,1},{1,0},{2,3},{3,2},{4,5},{5,4},{6,7},{7,6},{8,9},{9,8},{10,11... | collective-permute-start | bytes 983048 | tf_op jit(solution)/shard_map/ppermute | solution.py:352
  3.6 0.7 %collective-permute-start.1 = (f32[40,256]{1,0:T(8,128)}, f32[40,256]{1,0:T(8,128)S(1)}, u32[]{:S(2)}, u32[]{:S(2)}) collective-permute-start(f32[40,256]{1,0:T(8,128)} %get-tuple-element.18), channel_id=1, source_target_pairs={{2,4},{6,8},{10,12},{4,2},{8,6},{12,10},{3,5},{7,9},{11,13},{5,3},... | collective-permute-start | bytes 122888 | tf_op jit(solution)/shard_map/ppermute | solution.py:353
  4.3 5.4 %collective-permute-start.2 = (f32[40,256]{1,0:T(8,128)}, f32[40,256]{1,0:T(8,128)S(1)}, u32[]{:S(2)}, u32[]{:S(2)}) collective-permute-start(f32[40,256]{1,0:T(8,128)} %get-tuple-element.19), channel_id=1, source_target_pairs={{0,2},{4,6},{8,10},{12,14},{2,0},{6,4},{10,8},{14,12},{1,3},{5,7},... | collective-permute-start | bytes 122888 | tf_op jit(solution)/shard_map/ppermute | solution.py:354
  9.6 0.0 collective-permute-done.other
  9.6 0.0 copy-done.2
  9.6 0.0 copy-done.1
  9.7 0.0 copy-done.3
  9.7 0.0 copy-done.5
  9.7 0.0 copy-done
  9.7 0.0 copy-start.4
  9.7 0.9 %copy-done.4 = f32[2,4,32,256]{3,2,1,0:T(8,128)S(1)} copy-done((f32[2,4,32,256]{3,2,1,0:T(8,128)S(1)}, f32[2,4,32,256]{3,2,1,0:T(8,128)}, u32[]{:S(2)}) %copy-start.4) | copy-done | bytes 262168
  10.6 0.0 copy-start.6
  10.6 0.0 copy-start.7
  10.6 1.4 %shard_map.104 = (f32[2,4,32,256]{3,2,1,0:T(8,128)S(1)}, f32[3,8,32,256]{3,2,1,0:T(8,128)S(1)}, f32[8,32,256]{2,1,0:T(8,128)S(1)}, f32[4,32,256]{2,1,0:T(8,128)S(1)}, f32[16,256]{1,0:T(8,128)S(1)}) custom-call(f32[8,4,32,256]{3,2,1,0:T(8,128)S(1)} %copy-done, f32[4,32,256]{2,1,0:T(8,128)S(1)} %copy-done.2, f32[8,4,32,256]{3,2,1,0:T(8,128)S(1)} %copy-done.1, ...), custom_call_target="tpu_custom_call" | custom-call | flops 2000000 | bytes 4440064 | tf_op jit(solution)/shard_map/pallas_call | solution.py:22
  12.0 0.0 collective-permute-done.1.edge_b
  12.0 0.0 collective-permute-done.2.edge_a
  12.1 0.0 copy-done.6
  12.1 0.0 copy-done.7
  12.1 0.1 shard_map.105
  12.2 0.1 collective-permute-start.4
  12.3 0.5 %collective-permute-start.3 = (f32[8,32,256]{2,1,0:T(8,128)S(1)}, f32[8,32,256]{2,1,0:T(8,128)S(1)}, u32[]{:S(2)}, u32[]{:S(2)}) collective-permute-start(f32[8,32,256]{2,1,0:T(8,128)S(1)} %get-tuple-element.22.last), channel_id=1, source_target_pairs={{0,1},{1,0},{2,3},{3,2},{4,5},{5,4},{6,7},{7,6},{8,9},{9,8},{10,11... | collective-permute-start | bytes 786440 | tf_op jit(solution)/shard_map/ppermute | solution.py:362
  12.8 0.8 %collective-permute-done.4.swept = f32[88,256]{1,0:T(8,128)S(1)} collective-permute-done((f32[88,256]{1,0:T(8,128)S(1)}, f32[88,256]{1,0:T(8,128)S(1)}, u32[]{:S(2)}, u32[]{:S(2)}) %collective-permute-start.4) | collective-permute-done | bytes 90144 | tf_op jit(solution)/shard_map/ppermute | solution.py:368
  13.5 3.5 %collective-permute-start.8 = (f32[72,256]{1,0:T(8,128)S(1)}, f32[72,256]{1,0:T(8,128)S(1)}, u32[]{:S(2)}, u32[]{:S(2)}) collective-permute-start(f32[72,256]{1,0:T(8,128)S(1)} %slice_add_fusion.own), channel_id=1, source_target_pairs={{14,0},{12,2},{10,4},{8,6},{6,8},{4,10},{2,12},{0,14},{13,1},{15,3... | collective-permute-start | bytes 221192 | tf_op jit(solution)/shard_map/ppermute | solution.py:376
  17.0 1.0 %collective-permute-start.7 = (f32[72,256]{1,0:T(8,128)S(1)}, f32[72,256]{1,0:T(8,128)S(1)}, u32[]{:S(2)}, u32[]{:S(2)}) collective-permute-start(f32[72,256]{1,0:T(8,128)S(1)} %slice_add_fusion.own), channel_id=1, source_target_pairs={{8,0},{10,2},{12,4},{14,6},{0,8},{2,10},{4,12},{6,14},{11,1},{9,3}... | collective-permute-start | bytes 221192 | tf_op jit(solution)/shard_map/ppermute | solution.py:376
  18.0 0.9 %collective-permute-start.6 = (f32[72,256]{1,0:T(8,128)S(1)}, f32[72,256]{1,0:T(8,128)S(1)}, u32[]{:S(2)}, u32[]{:S(2)}) collective-permute-start(f32[72,256]{1,0:T(8,128)S(1)} %slice_add_fusion.own), channel_id=1, source_target_pairs={{6,0},{4,2},{2,4},{0,6},{14,8},{12,10},{10,12},{8,14},{5,1},{7,3},... | collective-permute-start | bytes 221192 | tf_op jit(solution)/shard_map/ppermute | solution.py:376
  18.9 1.9 %collective-permute-start.5 = (f32[72,256]{1,0:T(8,128)S(1)}, f32[72,256]{1,0:T(8,128)S(1)}, u32[]{:S(2)}, u32[]{:S(2)}) collective-permute-start(f32[72,256]{1,0:T(8,128)S(1)} %slice_add_fusion.own), channel_id=1, source_target_pairs={{2,0},{0,2},{6,4},{4,6},{10,8},{8,10},{14,12},{12,14},{3,1},{1,3},... | collective-permute-start | bytes 221192 | tf_op jit(solution)/shard_map/ppermute | solution.py:376
  20.8 0.7 %collective-permute-done.8.refs_3_ = f32[72,256]{1,0:T(8,128)S(1)} collective-permute-done((f32[72,256]{1,0:T(8,128)S(1)}, f32[72,256]{1,0:T(8,128)S(1)}, u32[]{:S(2)}, u32[]{:S(2)}) %collective-permute-start.8) | collective-permute-done | bytes 73760 | tf_op jit(solution)/shard_map/ppermute | solution.py:376
  21.5 0.0 collective-permute-start.12
  21.5 2.8 %collective-permute-done.7.refs_2_ = f32[72,256]{1,0:T(8,128)S(1)} collective-permute-done((f32[72,256]{1,0:T(8,128)S(1)}, f32[72,256]{1,0:T(8,128)S(1)}, u32[]{:S(2)}, u32[]{:S(2)}) %collective-permute-start.7) | collective-permute-done | bytes 73760 | tf_op jit(solution)/shard_map/ppermute | solution.py:376
  24.3 0.0 collective-permute-start.11
  24.3 0.0 collective-permute-done.6.refs_1_
  24.3 0.5 %collective-permute-start.10 = (f32[72,256]{1,0:T(8,128)S(1)}, f32[72,256]{1,0:T(8,128)S(1)}, u32[]{:S(2)}, u32[]{:S(2)}) collective-permute-start(f32[72,256]{1,0:T(8,128)S(1)} %collective-permute-done.6.refs_1_), channel_id=1, source_target_pairs={{0,1},{1,0},{2,3},{3,2},{4,5},{5,4},{6,7},{7,6},{8,9},{9,8},{10,11... | collective-permute-start | bytes 221192 | tf_op jit(solution)/shard_map/ppermute | solution.py:377
  24.8 0.0 collective-permute-done.5.refs_0_
  24.8 0.1 collective-permute-start.9
  24.9 0.0 collective-permute-done.12.refs_7_
  24.9 0.7 %collective-permute-done.11.refs_6_ = f32[72,256]{1,0:T(8,128)S(1)} collective-permute-done((f32[72,256]{1,0:T(8,128)S(1)}, f32[72,256]{1,0:T(8,128)S(1)}, u32[]{:S(2)}, u32[]{:S(2)}) %collective-permute-start.11) | collective-permute-done | bytes 73760 | tf_op jit(solution)/shard_map/ppermute | solution.py:377
  25.6 0.2 collective-permute-done.10.refs_5_
  25.7 0.4 %collective-permute-done.9.refs_4_ = f32[72,256]{1,0:T(8,128)S(1)} collective-permute-done((f32[72,256]{1,0:T(8,128)S(1)}, f32[72,256]{1,0:T(8,128)S(1)}, u32[]{:S(2)}, u32[]{:S(2)}) %collective-permute-start.9) | collective-permute-done | bytes 73760 | tf_op jit(solution)/shard_map/ppermute | solution.py:377
  26.1 0.0 collective-permute-done.3.other_last
  26.1 4.4 %shard_map.106 = (f32[8,4,32,256]{3,2,1,0:T(8,128)}, f32[2,4,32,256]{3,2,1,0:T(8,128)}, f32[32,256]{1,0:T(8,128)}) custom-call(f32[2,4,32,256]{3,2,1,0:T(8,128)S(1)} %get-tuple-element.20.flux, f32[4,32,256]{2,1,0:T(8,128)S(1)} %copy-done.2, f32[3,8,32,256]{3,2,1,0:T(8,128)S(1)} %get-tuple-element.21.nums, f32[8,32,256]{2,1,0:T(8,128)S(1)} %get-tuple-element.22.last, ...), custom_call_target="tpu_custom_call" | custom-call | flops 2000000 | bytes 4194304 | tf_op jit(solution)/shard_map/pallas_call | solution.py:22
  (1 shorter events, 0.0 us)
Async XLA Ops:
  0.6 9.0 %copy-start.2 = (f32[4,32,256]{2,1,0:T(8,128)S(1)}, f32[4,32,256]{2,1,0:T(8,128)}, u32[]{:S(2)}) copy-start(f32[4,32,256]{2,1,0:T(8,128)} %mix.3) | copy-start | bytes 393220
  0.6 9.0 %copy-start.1 = (f32[8,4,32,256]{3,2,1,0:T(8,128)S(1)}, f32[8,4,32,256]{3,2,1,0:T(8,128)}, u32[]{:S(2)}) copy-start(f32[8,4,32,256]{3,2,1,0:T(8,128)} %cot.1) | copy-start | bytes 3145732
  0.7 9.0 %copy-start.3 = (s32[4,32,256]{2,1,0:T(8,128)S(1)}, s32[4,32,256]{2,1,0:T(8,128)}, u32[]{:S(2)}) copy-start(s32[4,32,256]{2,1,0:T(8,128)} %mask.1) | copy-start | bytes 393220
  0.7 9.0 %copy-start.5 = (f32[32,256]{1,0:T(8,128)S(1)}, f32[32,256]{1,0:T(8,128)}, u32[]{:S(2)}) copy-start(f32[32,256]{1,0:T(8,128)} %surface.1) | copy-start | bytes 98308
  0.7 9.0 %copy-start = (f32[8,4,32,256]{3,2,1,0:T(8,128)S(1)}, f32[8,4,32,256]{3,2,1,0:T(8,128)}, u32[]{:S(2)}) copy-start(f32[8,4,32,256]{3,2,1,0:T(8,128)} %tracer.1) | copy-start | bytes 3145732
  3.1 6.5 %collective-permute-start = (f32[10,32,256]{2,1,0:T(8,128)}, f32[10,32,256]{2,1,0:T(8,128)S(1)}, u32[]{:S(2)}, u32[]{:S(2)}) collective-permute-start(f32[10,32,256]{2,1,0:T(8,128)} %get-tuple-element.14), channel_id=1, source_target_pairs={{0,1},{1,0},{2,3},{3,2},{4,5},{5,4},{6,7},{7,6},{8,9},{9,8},{10,11... | collective-permute-start | bytes 983048 | tf_op jit(solution)/shard_map/ppermute | solution.py:352
  3.6 8.4 %collective-permute-start.1 = (f32[40,256]{1,0:T(8,128)}, f32[40,256]{1,0:T(8,128)S(1)}, u32[]{:S(2)}, u32[]{:S(2)}) collective-permute-start(f32[40,256]{1,0:T(8,128)} %get-tuple-element.18), channel_id=1, source_target_pairs={{2,4},{6,8},{10,12},{4,2},{8,6},{12,10},{3,5},{7,9},{11,13},{5,3},... | collective-permute-start | bytes 122888 | tf_op jit(solution)/shard_map/ppermute | solution.py:353
  4.3 7.8 %collective-permute-start.2 = (f32[40,256]{1,0:T(8,128)}, f32[40,256]{1,0:T(8,128)S(1)}, u32[]{:S(2)}, u32[]{:S(2)}) collective-permute-start(f32[40,256]{1,0:T(8,128)} %get-tuple-element.19), channel_id=1, source_target_pairs={{0,2},{4,6},{8,10},{12,14},{2,0},{6,4},{10,8},{14,12},{1,3},{5,7},... | collective-permute-start | bytes 122888 | tf_op jit(solution)/shard_map/ppermute | solution.py:354
  9.7 1.0 %copy-start.4 = (f32[2,4,32,256]{3,2,1,0:T(8,128)S(1)}, f32[2,4,32,256]{3,2,1,0:T(8,128)}, u32[]{:S(2)}) copy-start(f32[2,4,32,256]{3,2,1,0:T(8,128)} %velocity.1) | copy-start | bytes 786436
  10.6 1.4 %copy-start.6 = (f32[32,256]{1,0:T(8,128)S(1)}, f32[32,256]{1,0:T(8,128)}, u32[]{:S(2)}) copy-start(f32[32,256]{1,0:T(8,128)} %surface_cot.1) | copy-start | bytes 98308
  10.6 1.4 %copy-start.7 = (f32[32,256]{1,0:T(8,128)S(1)}, f32[32,256]{1,0:T(8,128)}, u32[]{:S(2)}) copy-start(f32[32,256]{1,0:T(8,128)} %damping.1) | copy-start | bytes 98308
  12.2 1.4 %collective-permute-start.4 = (f32[88,256]{1,0:T(8,128)S(1)}, f32[88,256]{1,0:T(8,128)S(1)}, u32[]{:S(2)}, u32[]{:S(2)}) collective-permute-start(f32[88,256]{1,0:T(8,128)S(1)} %get-tuple-element.24), channel_id=1, source_target_pairs={{0,1},{1,0},{2,3},{3,2},{4,5},{5,4},{6,7},{7,6},{8,9},{9,8},{10,11... | collective-permute-start | bytes 270344 | tf_op jit(solution)/shard_map/ppermute | solution.py:368
  12.3 13.8 %collective-permute-start.3 = (f32[8,32,256]{2,1,0:T(8,128)S(1)}, f32[8,32,256]{2,1,0:T(8,128)S(1)}, u32[]{:S(2)}, u32[]{:S(2)}) collective-permute-start(f32[8,32,256]{2,1,0:T(8,128)S(1)} %get-tuple-element.22.last), channel_id=1, source_target_pairs={{0,1},{1,0},{2,3},{3,2},{4,5},{5,4},{6,7},{7,6},{8,9},{9,8},{10,11... | collective-permute-start | bytes 786440 | tf_op jit(solution)/shard_map/ppermute | solution.py:362
  13.5 7.9 %collective-permute-start.8 = (f32[72,256]{1,0:T(8,128)S(1)}, f32[72,256]{1,0:T(8,128)S(1)}, u32[]{:S(2)}, u32[]{:S(2)}) collective-permute-start(f32[72,256]{1,0:T(8,128)S(1)} %slice_add_fusion.own), channel_id=1, source_target_pairs={{14,0},{12,2},{10,4},{8,6},{6,8},{4,10},{2,12},{0,14},{13,1},{15,3... | collective-permute-start | bytes 221192 | tf_op jit(solution)/shard_map/ppermute | solution.py:376
  17.0 7.3 %collective-permute-start.7 = (f32[72,256]{1,0:T(8,128)S(1)}, f32[72,256]{1,0:T(8,128)S(1)}, u32[]{:S(2)}, u32[]{:S(2)}) collective-permute-start(f32[72,256]{1,0:T(8,128)S(1)} %slice_add_fusion.own), channel_id=1, source_target_pairs={{8,0},{10,2},{12,4},{14,6},{0,8},{2,10},{4,12},{6,14},{11,1},{9,3}... | collective-permute-start | bytes 221192 | tf_op jit(solution)/shard_map/ppermute | solution.py:376
  18.0 6.3 %collective-permute-start.6 = (f32[72,256]{1,0:T(8,128)S(1)}, f32[72,256]{1,0:T(8,128)S(1)}, u32[]{:S(2)}, u32[]{:S(2)}) collective-permute-start(f32[72,256]{1,0:T(8,128)S(1)} %slice_add_fusion.own), channel_id=1, source_target_pairs={{6,0},{4,2},{2,4},{0,6},{14,8},{12,10},{10,12},{8,14},{5,1},{7,3},... | collective-permute-start | bytes 221192 | tf_op jit(solution)/shard_map/ppermute | solution.py:376
  18.9 5.9 %collective-permute-start.5 = (f32[72,256]{1,0:T(8,128)S(1)}, f32[72,256]{1,0:T(8,128)S(1)}, u32[]{:S(2)}, u32[]{:S(2)}) collective-permute-start(f32[72,256]{1,0:T(8,128)S(1)} %slice_add_fusion.own), channel_id=1, source_target_pairs={{2,0},{0,2},{6,4},{4,6},{10,8},{8,10},{14,12},{12,14},{3,1},{1,3},... | collective-permute-start | bytes 221192 | tf_op jit(solution)/shard_map/ppermute | solution.py:376
  21.5 3.4 %collective-permute-start.12 = (f32[72,256]{1,0:T(8,128)S(1)}, f32[72,256]{1,0:T(8,128)S(1)}, u32[]{:S(2)}, u32[]{:S(2)}) collective-permute-start(f32[72,256]{1,0:T(8,128)S(1)} %collective-permute-done.8.refs_3_), channel_id=1, source_target_pairs={{0,1},{1,0},{2,3},{3,2},{4,5},{5,4},{6,7},{7,6},{8,9},{9,8},{10,11... | collective-permute-start | bytes 221192 | tf_op jit(solution)/shard_map/ppermute | solution.py:377
  24.3 1.3 %collective-permute-start.11 = (f32[72,256]{1,0:T(8,128)S(1)}, f32[72,256]{1,0:T(8,128)S(1)}, u32[]{:S(2)}, u32[]{:S(2)}) collective-permute-start(f32[72,256]{1,0:T(8,128)S(1)} %collective-permute-done.7.refs_2_), channel_id=1, source_target_pairs={{0,1},{1,0},{2,3},{3,2},{4,5},{5,4},{6,7},{7,6},{8,9},{9,8},{10,11... | collective-permute-start | bytes 221192 | tf_op jit(solution)/shard_map/ppermute | solution.py:377
  24.3 1.4 %collective-permute-start.10 = (f32[72,256]{1,0:T(8,128)S(1)}, f32[72,256]{1,0:T(8,128)S(1)}, u32[]{:S(2)}, u32[]{:S(2)}) collective-permute-start(f32[72,256]{1,0:T(8,128)S(1)} %collective-permute-done.6.refs_1_), channel_id=1, source_target_pairs={{0,1},{1,0},{2,3},{3,2},{4,5},{5,4},{6,7},{7,6},{8,9},{9,8},{10,11... | collective-permute-start | bytes 221192 | tf_op jit(solution)/shard_map/ppermute | solution.py:377
  24.8 1.3 %collective-permute-start.9 = (f32[72,256]{1,0:T(8,128)S(1)}, f32[72,256]{1,0:T(8,128)S(1)}, u32[]{:S(2)}, u32[]{:S(2)}) collective-permute-start(f32[72,256]{1,0:T(8,128)S(1)} %collective-permute-done.5.refs_0_), channel_id=1, source_target_pairs={{0,1},{1,0},{2,3},{3,2},{4,5},{5,4},{6,7},{7,6},{8,9},{9,8},{10,11... | collective-permute-start | bytes 221192 | tf_op jit(solution)/shard_map/ppermute | solution.py:377

commit v4 on v3

--- a/solution.py
+++ b/solution.py
@@ -213,7 +213,7 @@
     steps = len(partners)
     got, swapped = refs[:steps], refs[steps : 2 * steps]
     adj_tracer_out, adj_velocity, adj_surface = refs[2 * steps : 2 * steps + 3]
-    src, damp, edges, direc, image, sol, adj_tracer, sem = refs[2 * steps + 3 :]
+    resid, image, moved, damp, firsts, finals, direc, sol, adj_tracer, sem = refs[2 * steps + 3 :]
     levels, rows, cols = flux.shape[1:]
     me = lax.axis_index("tile")
     depth = lax.axis_index("depth")
@@ -240,72 +240,127 @@
     copy_out = pltpu.make_async_copy(adj_tracer, adj_tracer_out, sem)
     copy_out.start()
 
-    edges[0:8] = jnp.zeros((8, cols), F32)
-    edges[8 * (tiles + 1) : 8 * (tiles + 2)] = jnp.zeros((8, cols), F32)
+    parts = cols // 128
+    lanes = [slice(128 * h, 128 * (h + 1)) for h in range(parts)]
 
     def place(ref, tile):
-        at = pl.multiple_of(tile * rows, rows)
-        src[pl.ds(at, rows)] = ref[0:rows]
-        damp[pl.ds(at, rows)] = 4.0 + ref[rows + 8 : 2 * rows + 8]
-        edges[pl.ds(pl.multiple_of((tile + 1) * 8, 8), 8)] = ref[rows : rows + 8]
+        for h, lane in enumerate(lanes):
+            resid[h, pl.ds(tiles + tile, rows, stride=tiles)] = ref[0:rows, lane]
+            damp[h, pl.ds(tile, rows, stride=tiles)] = 4.0 + ref[rows + 8 : 2 * rows + 8, lane]
+            firsts[h, pl.ds(tile, 1)] = ref[rows : rows + 1, lane]
+            finals[h, pl.ds(tile, 1)] = ref[rows + 1 : rows + 2, lane]
 
     place(own, me)
     for step, (for_top, for_bottom) in enumerate(partners):
         place(got[step], partner(me, jnp.where(depth == 0, for_top, for_bottom), tiles))
         place(swapped[step], partner(me, jnp.where(depth == 0, for_bottom, for_top), tiles))
 
-    pad = 8
-    total = jnp.zeros((rows, cols), F32)
-    direc[0:pad] = jnp.zeros((pad, cols), F32)
-    direc[pad + tiles * rows : 2 * pad + tiles * rows] = jnp.zeros((pad, cols), F32)
-    for t in range(tiles):
-        above = edges[8 * t + 1 : 8 * t + 2]
-        below = edges[8 * (t + 2) : 8 * (t + 2) + 1]
-        block = src[t * rows : (t + 1) * rows]
-        block = block + GRAVITY * (jnp.where(row == rows - 1, below, 0.0) - jnp.where(row == 0, above, 0.0))
-        src[t * rows : (t + 1) * rows] = block
-        direc[pad + t * rows : pad + (t + 1) * rows] = block
-        total += block * block
-    norm = jnp.sum(total, keepdims=True)
+    column = lax.broadcasted_iota(jnp.int32, (tiles, 128), 1)
+
+    def group(ref, g):
+        return [ref[h, g * tiles : (g + 1) * tiles] for h in range(parts)]
+
+    def keep(ref, g, values):
+        for h, value in enumerate(values):
+            ref[h, g * tiles : (g + 1) * tiles] = value
+
+    def beside(values):
+        left = [pltpu.roll(v, 1, 1) for v in values]
+        right = [pltpu.roll(v, 127, 1) for v in values]
+        left = [jnp.where(column == 0, left[h - 1] if h > 0 else 0.0, left[h]) for h in range(parts)]
+        right = [jnp.where(column == 127, right[h + 1] if h < parts - 1 else 0.0, right[h]) for h in range(parts)]
+        return [p + q for p, q in zip(left, right)]
+
+    for h in range(parts):
+        next_first, _ = row_shifts(firsts[h], 0.0, 0.0)
+        _, last_final = row_shifts(finals[h], 0.0, 0.0)
+        resid[h, rows * tiles : (rows + 1) * tiles] += GRAVITY * next_first
+        resid[h, tiles : 2 * tiles] -= GRAVITY * last_final
+
+    def sweep(fresh):
+        final, first = fresh(rows - 1), fresh(0)
+        above = [row_shifts(v, 0.0, 0.0)[1] for v in final]
+        after = [row_shifts(v, 0.0, 0.0)[0] for v in first]
+        keep(resid, 0, above)
+        keep(resid, rows + 1, after)
+        norms = [jnp.zeros((tiles, 128), F32)] * parts
+        dots = [jnp.zeros((tiles, 128), F32)] * parts
+        here = first
+        for b in range(rows):
+            below = fresh(b + 1) if b + 1 < rows - 1 else final if b + 1 == rows - 1 else after
+            side, weight = beside(here), group(damp, b)
+            made = [weight[h] * here[h] - ((above[h] + below[h]) + side[h]) for h in range(parts)]
+            keep(image, b, made)
+            norms = [norms[h] + here[h] * here[h] for h in range(parts)]
+            dots = [dots[h] + here[h] * made[h] for h in range(parts)]
+            above, here = here, below
+        return jnp.sum(sum(norms), keepdims=True), jnp.sum(sum(dots), keepdims=True)
+
+    def step_own(alpha, beta):
+        for h in range(parts):
+            d = resid[h, pl.ds(me, rows + 2, stride=tiles)] + beta * direc[h]
+            direc[h] = d
+            sol[h] += alpha * d
+
+    direc[...] = jnp.zeros_like(direc)
     sol[...] = jnp.zeros_like(sol)
-    mine = pl.ds(pl.multiple_of(me * rows, 8), rows + 2 * pad)
-
-    def advance(turn, norm):
-        total = jnp.zeros((rows, cols), F32)
-        for t in range(tiles):
-            at = pad + t * rows
-            d = direc[at : at + rows]
-            right, left = lane_shifts(d)
-            beside = direc[at + 1 : at + rows + 1] + direc[at - 1 : at + rows - 1] + right + left
-            im = damp[t * rows : (t + 1) * rows] * d - beside
-            image[t * rows : (t + 1) * rows] = im
-            total += d * im
-        alpha = norm / jnp.sum(total, keepdims=True)
-        sol[...] += alpha * direc[mine]
-        total = jnp.zeros((rows, cols), F32)
-        for t in range(tiles):
-            part = slice(t * rows, (t + 1) * rows)
-            r = src[part] - alpha * image[part]
-            src[part] = r
-            total += r * r
-        fresh = jnp.sum(total, keepdims=True)
-        beta = fresh / norm
-        for t in range(tiles):
-            at = pad + t * rows
-            direc[at : at + rows] = src[t * rows : (t + 1) * rows] + beta * direc[at : at + rows]
-        return fresh
-
-    lax.fori_loop(0, ITERS, advance, norm)
-
-    x = sol[pad : pad + rows]
+    moved[...] = jnp.zeros_like(moved)
+    norm, dot = sweep(lambda b: group(resid, b + 1))
+
+    def advance(turn, carry):
+        norm, alpha, beta = carry
+        step_own(alpha, beta)
+
+        def fresh(b):
+            old, made, kept = group(resid, b + 1), group(image, b), group(moved, b)
+            kept = [made[h] + beta * kept[h] for h in range(parts)]
+            new = [old[h] - alpha * kept[h] for h in range(parts)]
+            keep(moved, b, kept)
+            keep(resid, b + 1, new)
+            return new
+
+        norm_now, dot = sweep(fresh)
+        beta = norm_now / norm
+        return norm_now, norm_now / (dot - beta * norm_now / alpha), beta
+
+    _, alpha, beta = lax.fori_loop(0, ITERS - 1, advance, (norm, norm / dot, jnp.zeros_like(norm)))
+    step_own(alpha, beta)
+
+    x = jnp.concatenate([sol[h, 1 : rows + 1] for h in range(parts)], axis=1)
     adj_surface[...] = x
     right, left = lane_shifts(x)
     slope_x = ADVECT * (right - left)
-    slope_y = ADVECT * (sol[pad + 1 : pad + rows + 1] - sol[pad - 1 : pad + rows - 1])
+    slope_y = jnp.concatenate([ADVECT * (sol[h, 2 : rows + 2] - sol[h, 0:rows]) for h in range(parts)], axis=1)
     for lev in range(levels):
         adj_velocity[0, lev] = flux[0, lev] + slope_x
         adj_velocity[1, lev] = flux[1, lev] + slope_y
     copy_out.wait()
+
+
+def solve_call(partners, args, tiles):
+    flux, last = args[0], args[3]
+    tracers = last.shape[0]
+    levels, rows, cols = flux.shape[1:]
+    plane, height, parts = (rows, cols), tiles * rows, cols // 128
+    block = (tracers, levels) + plane
+    return call(
+        functools.partial(solve_kernel, tiles, partners),
+        [block, (2, levels) + plane, plane],
+        args,
+        scratch=[
+            pltpu.VMEM((parts, height + 2 * tiles, 128), F32),
+            pltpu.VMEM((parts, height, 128), F32),
+            pltpu.VMEM((parts, height, 128), F32),
+            pltpu.VMEM((parts, height, 128), F32),
+            pltpu.VMEM((parts, tiles, 128), F32),
+            pltpu.VMEM((parts, tiles, 128), F32),
+            pltpu.VMEM((parts, rows + 2, 128), F32),
+            pltpu.VMEM((parts, rows + 2, 128), F32),
+            pltpu.VMEM(block, F32),
+            pltpu.SemaphoreType.DMA(()),
+        ],
+        hbm_out=(0,),
+    )
 
 
 def partner(tile, offset, tiles):
@@ -376,22 +431,10 @@
         got.append(lax.ppermute(own, ("tile", "depth"), pairs))
     swapped = [lax.ppermute(piece, "depth", swap) for piece in got]
 
-    height = tiles * rows
-    return call(
-        functools.partial(solve_kernel, tiles, partners),
-        [block, (2, levels) + plane, plane],
+    return solve_call(
+        partners,
         [flux, mixing, nums, last, delta, other, other_last, swept, own] + got + swapped,
-        scratch=[
-            pltpu.VMEM((height, cols), F32),
-            pltpu.VMEM((height, cols), F32),
-            pltpu.VMEM((8 * (tiles + 2), cols), F32),
-            pltpu.VMEM((height + 16, cols), F32),
-            pltpu.VMEM((height, cols), F32),
-            pltpu.VMEM((rows + 16, cols), F32),
-            pltpu.VMEM(block, F32),
-            pltpu.SemaphoreType.DMA(()),
-        ],
-        hbm_out=(0,),
+        tiles,
     )
 
 

time: 30.6 us -> 29.4 us (0.961)
  Pallas kernels: 8.25 us -> 7.06 us
    pallas_call x4, Pallas kernels: 8.25 us -> 7.06 us  [call(): pl.pallas_call(kernel, out_shape=[jax.ShapeDtypeStruct(s, F32) for s in o...]
where the time goes in v4:
time: 29.4 us; the launch traced here: 29.3 us
  starting transfers between devices  14.9 us (51%)
  Pallas kernels  7.06 us (24%)
  waiting for transfers between devices  5.5 us (19%)
  local copies, waits for them, and re-layouts  0.97 us (3%)
  between operations  0.79 us (3%)
    ppermute x4, starting transfers between devices, body(): got.append(lax.ppermute(own, ('tile', 'depth'), pairs))  7.26 us
    pallas_call x4, Pallas kernels, call(): pl.pallas_call(kernel, out_shape=[jax.ShapeDtypeStruct(s, F32) for s in o...  7.06 us
    ppermute x1, starting transfers between devices, body(): lax.ppermute(edge_a, 'tile', pairs_a + [(b, a) for a, b in pairs_a])  5.37 us
    ppermute x4, waiting for transfers between devices, body(): got.append(lax.ppermute(own, ('tile', 'depth'), pairs))  3.5 us
    ppermute x4, waiting for transfers between devices, body(): swapped = [lax.ppermute(piece, 'depth', swap) for piece in got]  1.21 us
    unnamed x16, local copies, waits for them, and re-layouts  0.97 us
    ppermute x1, waiting for transfers between devices, body(): swept = lax.ppermute(part, 'depth', swap)  0.78 us
    ppermute x1, starting transfers between devices, body(): lax.ppermute(edge_b, 'tile', pairs_b + [(b, a) for a, b in pairs_b])  0.65 us
  transfers between devices with their start and end apart: 13, of which 6 were waited for; matrix products, arithmetic and copies ran while one was open for 0% of the time, Pallas kernels for 5%

profile of v4, /device:TPU:0, one launch (start us, length us, event | category | flops | bytes accessed | tf_op | source)
XLA Modules:
  0.0 29.3 jit_solution(7479872456922810062)
XLA Ops:
  0.6 0.0 copy-start.2
  0.6 0.0 copy-start.1
  0.7 0.0 copy-start.3
  0.7 0.0 copy-start.5
  0.7 0.0 copy-start
  0.7 2.4 %shard_map.103 = (f32[10,32,256]{2,1,0:T(8,128)}, f32[40,256]{1,0:T(8,128)}, f32[40,256]{1,0:T(8,128)}) custom-call(f32[8,4,32,256]{3,2,1,0:T(8,128)} %tracer.1, f32[4,32,256]{2,1,0:T(8,128)} %mix.3, f32[8,4,32,256]{3,2,1,0:T(8,128)} %cot.1, s32[4,32,256]{2,1,0:T(8,128)} %mask.1, f32[32,256]{1,0:T(8,128)} %surface.1), custom_call_target="tpu_custom_call" | custom-call | flops 2000000 | bytes 2801664 | tf_op jit(solution)/shard_map/pallas_call | solution.py:22
  3.1 0.5 %collective-permute-start = (f32[10,32,256]{2,1,0:T(8,128)}, f32[10,32,256]{2,1,0:T(8,128)S(1)}, u32[]{:S(2)}, u32[]{:S(2)}) collective-permute-start(f32[10,32,256]{2,1,0:T(8,128)} %get-tuple-element.14), channel_id=1, source_target_pairs={{0,1},{1,0},{2,3},{3,2},{4,5},{5,4},{6,7},{7,6},{8,9},{9,8},{10,11... | collective-permute-start | bytes 983048 | tf_op jit(solution)/shard_map/ppermute | solution.py:407
  3.6 0.7 %collective-permute-start.1 = (f32[40,256]{1,0:T(8,128)}, f32[40,256]{1,0:T(8,128)S(1)}, u32[]{:S(2)}, u32[]{:S(2)}) collective-permute-start(f32[40,256]{1,0:T(8,128)} %get-tuple-element.18), channel_id=1, source_target_pairs={{2,4},{6,8},{10,12},{4,2},{8,6},{12,10},{3,5},{7,9},{11,13},{5,3},... | collective-permute-start | bytes 122888 | tf_op jit(solution)/shard_map/ppermute | solution.py:408
  4.3 5.4 %collective-permute-start.2 = (f32[40,256]{1,0:T(8,128)}, f32[40,256]{1,0:T(8,128)S(1)}, u32[]{:S(2)}, u32[]{:S(2)}) collective-permute-start(f32[40,256]{1,0:T(8,128)} %get-tuple-element.19), channel_id=1, source_target_pairs={{0,2},{4,6},{8,10},{12,14},{2,0},{6,4},{10,8},{14,12},{1,3},{5,7},... | collective-permute-start | bytes 122888 | tf_op jit(solution)/shard_map/ppermute | solution.py:409
  9.6 0.0 collective-permute-done.other
  9.6 0.0 copy-done.2
  9.6 0.0 copy-done.1
  9.7 0.0 copy-done.3
  9.7 0.0 copy-done.5
  9.7 0.0 copy-done
  9.7 0.0 copy-start.4
  9.7 0.9 %copy-done.4 = f32[2,4,32,256]{3,2,1,0:T(8,128)S(1)} copy-done((f32[2,4,32,256]{3,2,1,0:T(8,128)S(1)}, f32[2,4,32,256]{3,2,1,0:T(8,128)}, u32[]{:S(2)}) %copy-start.4) | copy-done | bytes 262168
  10.6 0.0 copy-start.6
  10.6 0.0 copy-start.7
  10.6 1.4 %shard_map.104 = (f32[2,4,32,256]{3,2,1,0:T(8,128)S(1)}, f32[3,8,32,256]{3,2,1,0:T(8,128)S(1)}, f32[8,32,256]{2,1,0:T(8,128)S(1)}, f32[4,32,256]{2,1,0:T(8,128)S(1)}, f32[16,256]{1,0:T(8,128)S(1)}) custom-call(f32[8,4,32,256]{3,2,1,0:T(8,128)S(1)} %copy-done, f32[4,32,256]{2,1,0:T(8,128)S(1)} %copy-done.2, f32[8,4,32,256]{3,2,1,0:T(8,128)S(1)} %copy-done.1, ...), custom_call_target="tpu_custom_call" | custom-call | flops 2000000 | bytes 4440064 | tf_op jit(solution)/shard_map/pallas_call | solution.py:22
  12.0 0.0 collective-permute-done.1.edge_b
  12.0 0.0 collective-permute-done.2.edge_a
  12.1 0.0 copy-done.6
  12.1 0.0 copy-done.7
  12.1 0.1 shard_map.105
  12.2 0.1 collective-permute-start.4
  12.3 0.5 %collective-permute-start.3 = (f32[8,32,256]{2,1,0:T(8,128)S(1)}, f32[8,32,256]{2,1,0:T(8,128)S(1)}, u32[]{:S(2)}, u32[]{:S(2)}) collective-permute-start(f32[8,32,256]{2,1,0:T(8,128)S(1)} %get-tuple-element.22.last), channel_id=1, source_target_pairs={{0,1},{1,0},{2,3},{3,2},{4,5},{5,4},{6,7},{7,6},{8,9},{9,8},{10,11... | collective-permute-start | bytes 786440 | tf_op jit(solution)/shard_map/ppermute | solution.py:417
  12.8 0.8 %collective-permute-done.4.swept = f32[88,256]{1,0:T(8,128)S(1)} collective-permute-done((f32[88,256]{1,0:T(8,128)S(1)}, f32[88,256]{1,0:T(8,128)S(1)}, u32[]{:S(2)}, u32[]{:S(2)}) %collective-permute-start.4) | collective-permute-done | bytes 90144 | tf_op jit(solution)/shard_map/ppermute | solution.py:423
  13.5 3.5 %collective-permute-start.8 = (f32[72,256]{1,0:T(8,128)S(1)}, f32[72,256]{1,0:T(8,128)S(1)}, u32[]{:S(2)}, u32[]{:S(2)}) collective-permute-start(f32[72,256]{1,0:T(8,128)S(1)} %slice_add_fusion.own), channel_id=1, source_target_pairs={{14,0},{12,2},{10,4},{8,6},{6,8},{4,10},{2,12},{0,14},{13,1},{15,3... | collective-permute-start | bytes 221192 | tf_op jit(solution)/shard_map/ppermute | solution.py:431
  17.0 1.0 %collective-permute-start.7 = (f32[72,256]{1,0:T(8,128)S(1)}, f32[72,256]{1,0:T(8,128)S(1)}, u32[]{:S(2)}, u32[]{:S(2)}) collective-permute-start(f32[72,256]{1,0:T(8,128)S(1)} %slice_add_fusion.own), channel_id=1, source_target_pairs={{8,0},{10,2},{12,4},{14,6},{0,8},{2,10},{4,12},{6,14},{11,1},{9,3}... | collective-permute-start | bytes 221192 | tf_op jit(solution)/shard_map/ppermute | solution.py:431
  18.0 0.9 %collective-permute-start.6 = (f32[72,256]{1,0:T(8,128)S(1)}, f32[72,256]{1,0:T(8,128)S(1)}, u32[]{:S(2)}, u32[]{:S(2)}) collective-permute-start(f32[72,256]{1,0:T(8,128)S(1)} %slice_add_fusion.own), channel_id=1, source_target_pairs={{6,0},{4,2},{2,4},{0,6},{14,8},{12,10},{10,12},{8,14},{5,1},{7,3},... | collective-permute-start | bytes 221192 | tf_op jit(solution)/shard_map/ppermute | solution.py:431
  18.9 1.9 %collective-permute-start.5 = (f32[72,256]{1,0:T(8,128)S(1)}, f32[72,256]{1,0:T(8,128)S(1)}, u32[]{:S(2)}, u32[]{:S(2)}) collective-permute-start(f32[72,256]{1,0:T(8,128)S(1)} %slice_add_fusion.own), channel_id=1, source_target_pairs={{2,0},{0,2},{6,4},{4,6},{10,8},{8,10},{14,12},{12,14},{3,1},{1,3},... | collective-permute-start | bytes 221192 | tf_op jit(solution)/shard_map/ppermute | solution.py:431
  20.8 0.7 %collective-permute-done.8.refs_3_ = f32[72,256]{1,0:T(8,128)S(1)} collective-permute-done((f32[72,256]{1,0:T(8,128)S(1)}, f32[72,256]{1,0:T(8,128)S(1)}, u32[]{:S(2)}, u32[]{:S(2)}) %collective-permute-start.8) | collective-permute-done | bytes 73760 | tf_op jit(solution)/shard_map/ppermute | solution.py:431
  21.5 0.0 collective-permute-start.12
  21.5 2.8 %collective-permute-done.7.refs_2_ = f32[72,256]{1,0:T(8,128)S(1)} collective-permute-done((f32[72,256]{1,0:T(8,128)S(1)}, f32[72,256]{1,0:T(8,128)S(1)}, u32[]{:S(2)}, u32[]{:S(2)}) %collective-permute-start.7) | collective-permute-done | bytes 73760 | tf_op jit(solution)/shard_map/ppermute | solution.py:431
  24.3 0.0 collective-permute-start.11
  24.3 0.0 collective-permute-done.6.refs_1_
  24.3 0.5 %collective-permute-start.10 = (f32[72,256]{1,0:T(8,128)S(1)}, f32[72,256]{1,0:T(8,128)S(1)}, u32[]{:S(2)}, u32[]{:S(2)}) collective-permute-start(f32[72,256]{1,0:T(8,128)S(1)} %collective-permute-done.6.refs_1_), channel_id=1, source_target_pairs={{0,1},{1,0},{2,3},{3,2},{4,5},{5,4},{6,7},{7,6},{8,9},{9,8},{10,11... | collective-permute-start | bytes 221192 | tf_op jit(solution)/shard_map/ppermute | solution.py:432
  24.8 0.0 collective-permute-done.5.refs_0_
  24.8 0.1 collective-permute-start.9
  24.9 0.0 collective-permute-done.12.refs_7_
  24.9 0.7 %collective-permute-done.11.refs_6_ = f32[72,256]{1,0:T(8,128)S(1)} collective-permute-done((f32[72,256]{1,0:T(8,128)S(1)}, f32[72,256]{1,0:T(8,128)S(1)}, u32[]{:S(2)}, u32[]{:S(2)}) %collective-permute-start.11) | collective-permute-done | bytes 73760 | tf_op jit(solution)/shard_map/ppermute | solution.py:432
  25.6 0.2 collective-permute-done.10.refs_5_
  25.7 0.4 %collective-permute-done.9.refs_4_ = f32[72,256]{1,0:T(8,128)S(1)} collective-permute-done((f32[72,256]{1,0:T(8,128)S(1)}, f32[72,256]{1,0:T(8,128)S(1)}, u32[]{:S(2)}, u32[]{:S(2)}) %collective-permute-start.9) | collective-permute-done | bytes 73760 | tf_op jit(solution)/shard_map/ppermute | solution.py:432
  26.1 0.0 collective-permute-done.3.other_last
  26.1 3.2 %shard_map.106 = (f32[8,4,32,256]{3,2,1,0:T(8,128)}, f32[2,4,32,256]{3,2,1,0:T(8,128)}, f32[32,256]{1,0:T(8,128)}) custom-call(f32[2,4,32,256]{3,2,1,0:T(8,128)S(1)} %get-tuple-element.20.flux, f32[4,32,256]{2,1,0:T(8,128)S(1)} %copy-done.2, f32[3,8,32,256]{3,2,1,0:T(8,128)S(1)} %get-tuple-element.21.nums, f32[8,32,256]{2,1,0:T(8,128)S(1)} %get-tuple-element.22.last, ...), custom_call_target="tpu_custom_call" | custom-call | flops 2000000 | bytes 4194304 | tf_op jit(solution)/shard_map/pallas_call | solution.py:22
  (1 shorter events, 0.0 us)
Async XLA Ops:
  0.6 9.0 %copy-start.2 = (f32[4,32,256]{2,1,0:T(8,128)S(1)}, f32[4,32,256]{2,1,0:T(8,128)}, u32[]{:S(2)}) copy-start(f32[4,32,256]{2,1,0:T(8,128)} %mix.3) | copy-start | bytes 393220
  0.6 9.0 %copy-start.1 = (f32[8,4,32,256]{3,2,1,0:T(8,128)S(1)}, f32[8,4,32,256]{3,2,1,0:T(8,128)}, u32[]{:S(2)}) copy-start(f32[8,4,32,256]{3,2,1,0:T(8,128)} %cot.1) | copy-start | bytes 3145732
  0.7 9.0 %copy-start.3 = (s32[4,32,256]{2,1,0:T(8,128)S(1)}, s32[4,32,256]{2,1,0:T(8,128)}, u32[]{:S(2)}) copy-start(s32[4,32,256]{2,1,0:T(8,128)} %mask.1) | copy-start | bytes 393220
  0.7 9.0 %copy-start.5 = (f32[32,256]{1,0:T(8,128)S(1)}, f32[32,256]{1,0:T(8,128)}, u32[]{:S(2)}) copy-start(f32[32,256]{1,0:T(8,128)} %surface.1) | copy-start | bytes 98308
  0.7 9.0 %copy-start = (f32[8,4,32,256]{3,2,1,0:T(8,128)S(1)}, f32[8,4,32,256]{3,2,1,0:T(8,128)}, u32[]{:S(2)}) copy-start(f32[8,4,32,256]{3,2,1,0:T(8,128)} %tracer.1) | copy-start | bytes 3145732
  3.1 6.5 %collective-permute-start = (f32[10,32,256]{2,1,0:T(8,128)}, f32[10,32,256]{2,1,0:T(8,128)S(1)}, u32[]{:S(2)}, u32[]{:S(2)}) collective-permute-start(f32[10,32,256]{2,1,0:T(8,128)} %get-tuple-element.14), channel_id=1, source_target_pairs={{0,1},{1,0},{2,3},{3,2},{4,5},{5,4},{6,7},{7,6},{8,9},{9,8},{10,11... | collective-permute-start | bytes 983048 | tf_op jit(solution)/shard_map/ppermute | solution.py:407
  3.6 8.4 %collective-permute-start.1 = (f32[40,256]{1,0:T(8,128)}, f32[40,256]{1,0:T(8,128)S(1)}, u32[]{:S(2)}, u32[]{:S(2)}) collective-permute-start(f32[40,256]{1,0:T(8,128)} %get-tuple-element.18), channel_id=1, source_target_pairs={{2,4},{6,8},{10,12},{4,2},{8,6},{12,10},{3,5},{7,9},{11,13},{5,3},... | collective-permute-start | bytes 122888 | tf_op jit(solution)/shard_map/ppermute | solution.py:408
  4.3 7.8 %collective-permute-start.2 = (f32[40,256]{1,0:T(8,128)}, f32[40,256]{1,0:T(8,128)S(1)}, u32[]{:S(2)}, u32[]{:S(2)}) collective-permute-start(f32[40,256]{1,0:T(8,128)} %get-tuple-element.19), channel_id=1, source_target_pairs={{0,2},{4,6},{8,10},{12,14},{2,0},{6,4},{10,8},{14,12},{1,3},{5,7},... | collective-permute-start | bytes 122888 | tf_op jit(solution)/shard_map/ppermute | solution.py:409
  9.7 1.0 %copy-start.4 = (f32[2,4,32,256]{3,2,1,0:T(8,128)S(1)}, f32[2,4,32,256]{3,2,1,0:T(8,128)}, u32[]{:S(2)}) copy-start(f32[2,4,32,256]{3,2,1,0:T(8,128)} %velocity.1) | copy-start | bytes 786436
  10.6 1.4 %copy-start.6 = (f32[32,256]{1,0:T(8,128)S(1)}, f32[32,256]{1,0:T(8,128)}, u32[]{:S(2)}) copy-start(f32[32,256]{1,0:T(8,128)} %surface_cot.1) | copy-start | bytes 98308
  10.6 1.4 %copy-start.7 = (f32[32,256]{1,0:T(8,128)S(1)}, f32[32,256]{1,0:T(8,128)}, u32[]{:S(2)}) copy-start(f32[32,256]{1,0:T(8,128)} %damping.1) | copy-start | bytes 98308
  12.2 1.4 %collective-permute-start.4 = (f32[88,256]{1,0:T(8,128)S(1)}, f32[88,256]{1,0:T(8,128)S(1)}, u32[]{:S(2)}, u32[]{:S(2)}) collective-permute-start(f32[88,256]{1,0:T(8,128)S(1)} %get-tuple-element.24), channel_id=1, source_target_pairs={{0,1},{1,0},{2,3},{3,2},{4,5},{5,4},{6,7},{7,6},{8,9},{9,8},{10,11... | collective-permute-start | bytes 270344 | tf_op jit(solution)/shard_map/ppermute | solution.py:423
  12.3 13.8 %collective-permute-start.3 = (f32[8,32,256]{2,1,0:T(8,128)S(1)}, f32[8,32,256]{2,1,0:T(8,128)S(1)}, u32[]{:S(2)}, u32[]{:S(2)}) collective-permute-start(f32[8,32,256]{2,1,0:T(8,128)S(1)} %get-tuple-element.22.last), channel_id=1, source_target_pairs={{0,1},{1,0},{2,3},{3,2},{4,5},{5,4},{6,7},{7,6},{8,9},{9,8},{10,11... | collective-permute-start | bytes 786440 | tf_op jit(solution)/shard_map/ppermute | solution.py:417
  13.5 7.9 %collective-permute-start.8 = (f32[72,256]{1,0:T(8,128)S(1)}, f32[72,256]{1,0:T(8,128)S(1)}, u32[]{:S(2)}, u32[]{:S(2)}) collective-permute-start(f32[72,256]{1,0:T(8,128)S(1)} %slice_add_fusion.own), channel_id=1, source_target_pairs={{14,0},{12,2},{10,4},{8,6},{6,8},{4,10},{2,12},{0,14},{13,1},{15,3... | collective-permute-start | bytes 221192 | tf_op jit(solution)/shard_map/ppermute | solution.py:431
  17.0 7.3 %collective-permute-start.7 = (f32[72,256]{1,0:T(8,128)S(1)}, f32[72,256]{1,0:T(8,128)S(1)}, u32[]{:S(2)}, u32[]{:S(2)}) collective-permute-start(f32[72,256]{1,0:T(8,128)S(1)} %slice_add_fusion.own), channel_id=1, source_target_pairs={{8,0},{10,2},{12,4},{14,6},{0,8},{2,10},{4,12},{6,14},{11,1},{9,3}... | collective-permute-start | bytes 221192 | tf_op jit(solution)/shard_map/ppermute | solution.py:431
  18.0 6.3 %collective-permute-start.6 = (f32[72,256]{1,0:T(8,128)S(1)}, f32[72,256]{1,0:T(8,128)S(1)}, u32[]{:S(2)}, u32[]{:S(2)}) collective-permute-start(f32[72,256]{1,0:T(8,128)S(1)} %slice_add_fusion.own), channel_id=1, source_target_pairs={{6,0},{4,2},{2,4},{0,6},{14,8},{12,10},{10,12},{8,14},{5,1},{7,3},... | collective-permute-start | bytes 221192 | tf_op jit(solution)/shard_map/ppermute | solution.py:431
  18.9 5.9 %collective-permute-start.5 = (f32[72,256]{1,0:T(8,128)S(1)}, f32[72,256]{1,0:T(8,128)S(1)}, u32[]{:S(2)}, u32[]{:S(2)}) collective-permute-start(f32[72,256]{1,0:T(8,128)S(1)} %slice_add_fusion.own), channel_id=1, source_target_pairs={{2,0},{0,2},{6,4},{4,6},{10,8},{8,10},{14,12},{12,14},{3,1},{1,3},... | collective-permute-start | bytes 221192 | tf_op jit(solution)/shard_map/ppermute | solution.py:431
  21.5 3.4 %collective-permute-start.12 = (f32[72,256]{1,0:T(8,128)S(1)}, f32[72,256]{1,0:T(8,128)S(1)}, u32[]{:S(2)}, u32[]{:S(2)}) collective-permute-start(f32[72,256]{1,0:T(8,128)S(1)} %collective-permute-done.8.refs_3_), channel_id=1, source_target_pairs={{0,1},{1,0},{2,3},{3,2},{4,5},{5,4},{6,7},{7,6},{8,9},{9,8},{10,11... | collective-permute-start | bytes 221192 | tf_op jit(solution)/shard_map/ppermute | solution.py:432
  24.3 1.3 %collective-permute-start.11 = (f32[72,256]{1,0:T(8,128)S(1)}, f32[72,256]{1,0:T(8,128)S(1)}, u32[]{:S(2)}, u32[]{:S(2)}) collective-permute-start(f32[72,256]{1,0:T(8,128)S(1)} %collective-permute-done.7.refs_2_), channel_id=1, source_target_pairs={{0,1},{1,0},{2,3},{3,2},{4,5},{5,4},{6,7},{7,6},{8,9},{9,8},{10,11... | collective-permute-start | bytes 221192 | tf_op jit(solution)/shard_map/ppermute | solution.py:432
  24.3 1.4 %collective-permute-start.10 = (f32[72,256]{1,0:T(8,128)S(1)}, f32[72,256]{1,0:T(8,128)S(1)}, u32[]{:S(2)}, u32[]{:S(2)}) collective-permute-start(f32[72,256]{1,0:T(8,128)S(1)} %collective-permute-done.6.refs_1_), channel_id=1, source_target_pairs={{0,1},{1,0},{2,3},{3,2},{4,5},{5,4},{6,7},{7,6},{8,9},{9,8},{10,11... | collective-permute-start | bytes 221192 | tf_op jit(solution)/shard_map/ppermute | solution.py:432
  24.8 1.3 %collective-permute-start.9 = (f32[72,256]{1,0:T(8,128)S(1)}, f32[72,256]{1,0:T(8,128)S(1)}, u32[]{:S(2)}, u32[]{:S(2)}) collective-permute-start(f32[72,256]{1,0:T(8,128)S(1)} %collective-permute-done.5.refs_0_), channel_id=1, source_target_pairs={{0,1},{1,0},{2,3},{3,2},{4,5},{5,4},{6,7},{7,6},{8,9},{9,8},{10,11... | collective-permute-start | bytes 221192 | tf_op jit(solution)/shard_map/ppermute | solution.py:432

commit v5 on v4

--- a/solution.py
+++ b/solution.py
@@ -70,48 +70,43 @@
     return (other_rest + link) * inv, link * inv
 
 
-def start_kernel(tracer_in, mix_in, cot_in, mask_in, surface_in, face, edge_b, edge_a, tracer, mix, surface, cot, mask, sems):
-    tracers, levels, rows, _ = tracer.shape
-    depth = lax.axis_index("depth")
+def edge_kernel(cot_in, mask_in, surface_in, tracer_in, mix_in, velocity_in, edge_b, edge_a, cot, mask, surface, sems):
+    levels, rows, _ = mask_in.shape
+    tracers = cot_in.shape[0] // levels
     odd = lax.rem(lax.axis_index("tile"), 2) == 1
-    moves = [(mix_in, mix), (tracer_in, tracer), (surface_in, surface), (mask_in, mask)]
-    moves += [(cot_in.at[:, :, 0:8], cot.at[0]), (cot_in.at[:, :, rows - 8 : rows], cot.at[1])]
-    copies = [pltpu.make_async_copy(src, dst, sems.at[i]) for i, (src, dst) in enumerate(moves)]
+    copies = []
+    for side, start in enumerate((0, rows - 8)):
+        part = pl.ds(start, 8)
+        moves = [(cot_in.at[:, part], cot), (mask_in.at[:, part], mask), (surface_in.at[part], surface)]
+        for src, dst in moves:
+            copies.append(pltpu.make_async_copy(src, dst.at[side], sems.at[len(copies)]))
     for copy in copies:
         copy.start()
-    copies[0].wait()
-    copies[1].wait()
-    _, ratio, rest = chain(mix, depth)
-    for tr in range(tracers):
-        num = tracer[tr, level(0, depth, levels)]
-        for j in range(1, levels):
-            num = tracer[tr, level(j, depth, levels)] + ratio[j - 1] * num
-        face[tr] = num
-    face[tracers] = rest
-    face[tracers + 1] = mix[levels - 1]
-    for copy in copies[2:]:
+    for copy in copies:
         copy.wait()
     for lev in range(levels):
-        first_wet = mask[lev, 0:1].astype(F32)
-        last_wet = mask[lev, rows - 1 : rows].astype(F32)
+        first_wet = mask[0, lev, 0:1].astype(F32)
+        last_wet = mask[1, lev, 7:8].astype(F32)
         for tr in range(tracers):
-            first = cot[0, tr, lev, 0:1] * first_wet
-            last = cot[1, tr, lev, 7:8] * last_wet
+            first = cot[0, tr * levels + lev, 0:1] * first_wet
+            last = cot[1, tr * levels + lev, 7:8] * last_wet
             at = lev * tracers + tr
             edge_a[at : at + 1] = jnp.where(odd, first, last)
             edge_b[at : at + 1] = jnp.where(odd, last, first)
     at = tracers * levels
     edge_a[at : at + 8] = jnp.zeros_like(edge_a[at : at + 8])
     edge_b[at : at + 8] = jnp.zeros_like(edge_b[at : at + 8])
-    edge_a[at : at + 1] = jnp.where(odd, surface[0:1], surface[rows - 1 : rows])
-    edge_b[at : at + 1] = jnp.where(odd, surface[rows - 1 : rows], surface[0:1])
-
-
-def interior_kernel(tracer, mix, cot, mask, velocity, surface, other, flux, nums, last, packed, lines, speed):
+    first, last = surface[0, 0:1], surface[1, 7:8]
+    edge_a[at : at + 1] = jnp.where(odd, first, last)
+    edge_b[at : at + 1] = jnp.where(odd, last, first)
+
+
+def interior_kernel(tracer, mix, cot, mask, velocity, surface, other, other_mix, flux, nums, last, packed, lines, speed):
     tracers, levels, rows, cols = tracer.shape
     depth = lax.axis_index("depth")
     inverse, ratio, rest = chain(mix, depth)
-    own_w, other_w = meet(rest, other[tracers], mix[levels - 1], other[tracers + 1], depth)
+    _, other_ratio, other_rest = chain(other_mix, 1 - depth)
+    own_w, other_w = meet(rest, other_rest, mix[levels - 1], other_mix[levels - 1], depth)
     right, left = lane_shifts(surface[...])
     down, up = row_shifts(surface[...], 0.0, 0.0)
     for lev in range(levels):
@@ -130,7 +125,10 @@
         held = [tracer[tr, level(0, depth, levels)]]
         for j in range(1, levels):
             held.append(tracer[tr, level(j, depth, levels)] + ratio[j - 1] * held[-1])
-        value = own_w * held[-1] + other_w * other[tr]
+        met = other[tr, level(0, 1 - depth, levels)]
+        for j in range(1, levels):
+            met = other[tr, level(j, 1 - depth, levels)] + other_ratio[j - 1] * met
+        value = own_w * held[-1] + other_w * met
         outs = [None] * levels
         for j in range(levels - 1, -1, -1):
             lev = level(j, depth, levels)
@@ -209,7 +207,7 @@
     send[2 * rows + 8 + tracers : 2 * rows + 8 + 2 * tracers] = delta[1, levels - 1]
 
 
-def solve_kernel(tiles, partners, flux, mix, nums, last, delta, other, other_last, swept, own, *refs):
+def solve_kernel(tiles, partners, flux, mix, nums, last, delta, other_mix, other_last, swept, own, *refs):
     steps = len(partners)
     got, swapped = refs[:steps], refs[steps : 2 * steps]
     adj_tracer_out, adj_velocity, adj_surface = refs[2 * steps : 2 * steps + 3]
@@ -220,7 +218,8 @@
 
     tracers = last.shape[0]
     inverse, ratio, rest = chain(mix, depth)
-    own_w, other_w = meet(rest, other[tracers], mix[levels - 1], other[tracers + 1], depth)
+    _, _, other_rest = chain(other_mix, 1 - depth)
+    own_w, other_w = meet(rest, other_rest, mix[levels - 1], other_mix[levels - 1], depth)
     row = lax.broadcasted_iota(jnp.int32, (rows, cols), 0)
     far = 2 * rows + 8
 
@@ -308,7 +307,7 @@
     norm, dot = sweep(lambda b: group(resid, b + 1))
 
     def advance(turn, carry):
-        norm, alpha, beta = carry
+        over_norm, inv, alpha, beta = carry
         step_own(alpha, beta)
 
         def fresh(b):
@@ -319,11 +318,15 @@
             keep(resid, b + 1, new)
             return new
 
-        norm_now, dot = sweep(fresh)
-        beta = norm_now / norm
-        return norm_now, norm_now / (dot - beta * norm_now / alpha), beta
-
-    _, alpha, beta = lax.fori_loop(0, ITERS - 1, advance, (norm, norm / dot, jnp.zeros_like(norm)))
+        norm, dot = sweep(fresh)
+        beta = norm * over_norm
+        divisor = dot - norm * (beta * inv)
+        over_norm = 1.0 / norm
+        return over_norm, divisor * over_norm, norm / divisor, beta
+
+    over_norm = 1.0 / norm
+    first = (over_norm, dot * over_norm, norm / dot, jnp.zeros_like(norm))
+    _, _, alpha, beta = lax.fori_loop(0, ITERS - 1, advance, first)
     step_own(alpha, beta)
 
     x = jnp.concatenate([sol[h, 1 : rows + 1] for h in range(parts)], axis=1)
@@ -371,13 +374,12 @@
 
 def partner_offsets(tiles):
     if tiles & (tiles - 1) == 0:
-        others = list(range(1, tiles))
+        others = sorted(range(1, tiles), key=lambda k: (bin(k).count("1"), k))
     else:
         others = list(range(tiles))
     if len(others) % 2 == 1:
         others = others[:1] + others
-    pairs = [(others[i], others[i + 1]) for i in range(0, len(others), 2)]
-    return [pair if i % 2 == 0 else pair[::-1] for i, pair in enumerate(pairs)]
+    return [(others[i], others[i + 1]) for i in range(0, len(others), 2)]
 
 
 def body(tracer_start, velocity, surface, mixing, land_mask, damping, tracer_cot, surface_cot):
@@ -387,34 +389,32 @@
     plane = (rows, cols)
     block = (tracers, levels) + plane
     edge = (tracers * levels + 8, cols)
-    face, edge_b, edge_a = call(
-        start_kernel,
-        [(tracers + 2,) + plane, edge, edge],
-        [tracer_start, mixing, tracer_cot, land_mask, surface],
+    edge_b, edge_a = call(
+        edge_kernel,
+        [edge, edge],
+        [tracer_cot.reshape(tracers * levels, rows, cols), land_mask, surface, tracer_start, mixing, velocity],
         scratch=[
-            pltpu.VMEM(block, F32),
-            pltpu.VMEM((levels,) + plane, F32),
-            pltpu.VMEM(plane, F32),
-            pltpu.VMEM((2, tracers, levels, 8, cols), F32),
-            pltpu.VMEM((levels,) + plane, jnp.int32),
+            pltpu.VMEM((2, tracers * levels, 8, cols), F32),
+            pltpu.VMEM((2, levels, 8, cols), jnp.int32),
+            pltpu.VMEM((2, 8, cols), F32),
             pltpu.SemaphoreType.DMA((6,)),
         ],
-        hbm_in=range(5),
+        hbm_in=range(6),
         vmem=56,
     )
     pairs_a = [(i, i + 1) for i in range(0, tiles - 1, 2)]
     pairs_b = [(i, i + 1) for i in range(1, tiles - 1, 2)]
-    other = lax.ppermute(face, "depth", swap)
+    other = lax.ppermute(tracer_start, "depth", swap)
+    other_mix = lax.ppermute(mixing, "depth", swap)
     edge_b = lax.ppermute(edge_b, "tile", pairs_b + [(b, a) for a, b in pairs_b])
     edge_a = lax.ppermute(edge_a, "tile", pairs_a + [(b, a) for a, b in pairs_a])
     planes = tracers * levels
     flux, nums, last, packed, lines = call(
         interior_kernel,
         [(2, levels) + plane, (levels - 1, tracers) + plane, (tracers,) + plane, (4, planes, cols), (4 * levels, cols)],
-        [tracer_start, mixing, tracer_cot, land_mask, velocity, surface, other],
+        [tracer_start, mixing, tracer_cot, land_mask, velocity, surface, other, other_mix],
         scratch=[pltpu.VMEM((2, levels) + plane, F32)],
     )
-    other_last = lax.ppermute(last, "depth", swap)
     flux, delta, part = call(
         column_kernel,
         [(2, levels) + plane, (2, levels, tracers, cols), (2 * rows + 8 + 2 * tracers, cols)],
@@ -431,9 +431,11 @@
         got.append(lax.ppermute(own, ("tile", "depth"), pairs))
     swapped = [lax.ppermute(piece, "depth", swap) for piece in got]
 
+    last_late, _ = lax.optimization_barrier((last, own))
+    other_last = lax.ppermute(last_late, "depth", swap)
     return solve_call(
         partners,
-        [flux, mixing, nums, last, delta, other, other_last, swept, own] + got + swapped,
+        [flux, mixing, nums, last, delta, other_mix, other_last, swept, own] + got + swapped,
         tiles,
     )
 

time: 29.4 us -> 29.4 us (level)
  starting transfers between devices: 14.9 us -> 16.3 us
  local copies, waits for them, and re-layouts: 0.97 us -> 0.04 us
  Pallas kernels: 7.06 us -> 6.68 us
    ppermute x4, waiting for transfers between devices: 3.5 us -> 2.38 us  [body(): got.append(lax.ppermute(own, ('tile', 'depth'), pairs))]
    unnamed x16, local copies, waits for them, and re-layouts: 0.97 us -> 0.04 us
    ppermute x4, starting transfers between devices: 0.57 us -> 1.48 us  [body(): swapped = [lax.ppermute(piece, 'depth', swap) for piece in got]]
    ppermute x1, waiting for transfers between devices: 0.01 us -> 0.65 us  [body(): lax.ppermute(edge_a, 'tile', pairs_a + [(b, a) for a, b in pairs_a])]
    ppermute x1, waiting for transfers between devices: 0.78 us -> 1.28 us  [body(): swept = lax.ppermute(part, 'depth', swap)]
    ppermute x1, starting transfers between devices: 5.37 us -> 5.78 us  [body(): lax.ppermute(edge_a, 'tile', pairs_a + [(b, a) for a, b in pairs_a])]
    pallas_call x4, Pallas kernels: 7.06 us -> 6.68 us  [call(): pl.pallas_call(kernel, out_shape=[jax.ShapeDtypeStruct(s, F32) for s in o...]
    ppermute x2 -> x3, starting transfers between devices: 1.01 us -> 0.82 us  [the longest x1 0.52 us: body(): other = lax.ppermute(tracer_start, 'depth', swap)]
  transfers between devices with their start and end apart: 13 -> 14, of which waited for: 6 -> 6; matrix products, arithmetic and copies ran while one was open for 0% -> 0% of each run, Pallas kernels for 5% -> 12%
where the time goes in v5:
time: 29.4 us; the launch traced here: 29.2 us
  starting transfers between devices  16.3 us (55%)
  Pallas kernels  6.68 us (23%)
  waiting for transfers between devices  5.46 us (19%)
  between operations  0.77 us (3%)
    ppermute x4, starting transfers between devices, body(): got.append(lax.ppermute(own, ('tile', 'depth'), pairs))  7.48 us
    pallas_call x4, Pallas kernels, call(): pl.pallas_call(kernel, out_shape=[jax.ShapeDtypeStruct(s, F32) for s in o...  6.68 us
    ppermute x1, starting transfers between devices, body(): lax.ppermute(edge_a, 'tile', pairs_a + [(b, a) for a, b in pairs_a])  5.78 us
    ppermute x4, waiting for transfers between devices, body(): got.append(lax.ppermute(own, ('tile', 'depth'), pairs))  2.38 us
    ppermute x4, starting transfers between devices, body(): swapped = [lax.ppermute(piece, 'depth', swap) for piece in got]  1.48 us
    ppermute x1, waiting for transfers between devices, body(): swept = lax.ppermute(part, 'depth', swap)  1.28 us
    ppermute x4, waiting for transfers between devices, body(): swapped = [lax.ppermute(piece, 'depth', swap) for piece in got]  1.15 us
    ppermute x1, starting transfers between devices, body(): lax.ppermute(edge_b, 'tile', pairs_b + [(b, a) for a, b in pairs_b])  0.66 us
  transfers between devices with their start and end apart: 14, of which 6 were waited for; matrix products, arithmetic and copies ran while one was open for 0% of the time, Pallas kernels for 12%

profile of v5, /device:TPU:0, one launch (start us, length us, event | category | flops | bytes accessed | tf_op | source)
XLA Modules:
  0.0 29.2 jit_solution(1544255464778059201)
XLA Ops:
  0.6 0.5 %collective-permute-start = (f32[8,4,32,256]{3,2,1,0:T(8,128)}, f32[8,4,32,256]{3,2,1,0:T(8,128)S(1)}, u32[]{:S(2)}, u32[]{:S(2)}) collective-permute-start(f32[8,4,32,256]{3,2,1,0:T(8,128)} %tracer_in.1), channel_id=1, source_target_pairs={{0,1},{1,0},{2,3},{3,2},{4,5},{5,4},{6,7},{7,6},{8,9},{9,8},{10,11... | collective-permute-start | bytes 3145736 | tf_op jit(solution)/shard_map/ppermute | solution.py:407
  1.1 0.1 collective-permute-start.1
  1.2 0.0 copy-start
  1.2 0.0 copy-start.1
  1.2 0.0 copy-start.2
  1.2 0.0 copy-start.3
  1.2 0.0 copy-start.4
  1.2 0.0 copy-start.5
  1.3 1.9 %shard_map.104 = (f32[40,256]{1,0:T(8,128)}, f32[40,256]{1,0:T(8,128)}) custom-call(f32[32,32,256]{2,1,0:T(8,128)} %bitcast.1, s32[4,32,256]{2,1,0:T(8,128)} %mask_in.1, f32[32,256]{1,0:T(8,128)} %surface_in.1, f32[8,4,32,256]{3,2,1,0:T(8,128)} %tracer_in.1, f32[4,32,256]{2,1,0:T(8,128)} %mix.3, f32[2,4,32,256]{3,2,1,0:T(8,128)} %velocity_in.1), custom_call_target="tpu_custom_call" | custom-call | flops 2000000 | bytes 2736128 | tf_op jit(solution)/shard_map/pallas_call | solution.py:22
  3.2 0.7 %collective-permute-start.2 = (f32[40,256]{1,0:T(8,128)}, f32[40,256]{1,0:T(8,128)S(1)}, u32[]{:S(2)}, u32[]{:S(2)}) collective-permute-start(f32[40,256]{1,0:T(8,128)} %get-tuple-element.17), channel_id=1, source_target_pairs={{2,4},{6,8},{10,12},{4,2},{8,6},{12,10},{3,5},{7,9},{11,13},{5,3},... | collective-permute-start | bytes 122888 | tf_op jit(solution)/shard_map/ppermute | solution.py:409
  3.9 0.0 copy-start.6
  3.9 0.0 copy-start.7
  3.9 5.8 %collective-permute-start.3 = (f32[40,256]{1,0:T(8,128)}, f32[40,256]{1,0:T(8,128)S(1)}, u32[]{:S(2)}, u32[]{:S(2)}) collective-permute-start(f32[40,256]{1,0:T(8,128)} %get-tuple-element.18), channel_id=1, source_target_pairs={{0,2},{4,6},{8,10},{12,14},{2,0},{6,4},{10,8},{14,12},{1,3},{5,7},... | collective-permute-start | bytes 122888 | tf_op jit(solution)/shard_map/ppermute | solution.py:410
  9.7 0.0 collective-permute-done.1.other_mix
  9.7 0.0 collective-permute-done.other
  9.7 0.0 copy-done
  9.7 0.0 copy-done.1
  9.7 0.0 copy-done.2
  9.7 0.0 copy-done.3
  9.7 0.0 copy-done.4
  9.7 0.0 copy-done.5
  9.7 1.5 %shard_map.103 = (f32[2,4,32,256]{3,2,1,0:T(8,128)S(1)}, f32[3,8,32,256]{3,2,1,0:T(8,128)S(1)}, f32[8,32,256]{2,1,0:T(8,128)S(1)}, f32[4,32,256]{2,1,0:T(8,128)S(1)}, f32[16,256]{1,0:T(8,128)S(1)}) custom-call(f32[8,4,32,256]{3,2,1,0:T(8,128)S(1)} %copy-done, f32[4,32,256]{2,1,0:T(8,128)S(1)} %copy-done.2, f32[8,4,32,256]{3,2,1,0:T(8,128)S(1)} %copy-done.1, ...), custom_call_target="tpu_custom_call" | custom-call | flops 2000000 | bytes 5292032 | tf_op jit(solution)/shard_map/pallas_call | solution.py:22
  11.2 0.0 collective-permute-done.2.edge_b
  11.2 0.6 %collective-permute-done.3.edge_a = f32[40,256]{1,0:T(8,128)S(1)} collective-permute-done((f32[40,256]{1,0:T(8,128)}, f32[40,256]{1,0:T(8,128)S(1)}, u32[]{:S(2)}, u32[]{:S(2)}) %collective-permute-start.3) | collective-permute-done | bytes 40992 | tf_op jit(solution)/shard_map/ppermute | solution.py:410
  11.9 0.0 copy-done.6
  11.9 0.0 copy-done.7
  11.9 0.1 shard_map.105
  12.0 0.1 collective-permute-start.4
  12.0 1.3 %collective-permute-done.4.swept = f32[88,256]{1,0:T(8,128)S(1)} collective-permute-done((f32[88,256]{1,0:T(8,128)S(1)}, f32[88,256]{1,0:T(8,128)S(1)}, u32[]{:S(2)}, u32[]{:S(2)}) %collective-permute-start.4) | collective-permute-done | bytes 90144 | tf_op jit(solution)/shard_map/ppermute | solution.py:423
  13.3 0.2 collective-permute-start.5
  13.6 4.0 %collective-permute-start.9 = (f32[72,256]{1,0:T(8,128)S(1)}, f32[72,256]{1,0:T(8,128)S(1)}, u32[]{:S(2)}, u32[]{:S(2)}) collective-permute-start(f32[72,256]{1,0:T(8,128)S(1)} %slice_add_fusion.own), channel_id=1, source_target_pairs={{12,0},{14,2},{8,4},{10,6},{4,8},{6,10},{0,12},{2,14},{15,1},{13,3... | collective-permute-start | bytes 221192 | tf_op jit(solution)/shard_map/ppermute | solution.py:431
  17.5 0.6 %collective-permute-start.8 = (f32[72,256]{1,0:T(8,128)S(1)}, f32[72,256]{1,0:T(8,128)S(1)}, u32[]{:S(2)}, u32[]{:S(2)}) collective-permute-start(f32[72,256]{1,0:T(8,128)S(1)} %slice_add_fusion.own), channel_id=1, source_target_pairs={{6,0},{4,2},{2,4},{0,6},{14,8},{12,10},{10,12},{8,14},{11,1},{9,3}... | collective-permute-start | bytes 221192 | tf_op jit(solution)/shard_map/ppermute | solution.py:431
  18.2 0.8 %collective-permute-start.7 = (f32[72,256]{1,0:T(8,128)S(1)}, f32[72,256]{1,0:T(8,128)S(1)}, u32[]{:S(2)}, u32[]{:S(2)}) collective-permute-start(f32[72,256]{1,0:T(8,128)S(1)} %slice_add_fusion.own), channel_id=1, source_target_pairs={{4,0},{6,2},{0,4},{2,6},{12,8},{14,10},{8,12},{10,14},{9,1},{11,3}... | collective-permute-start | bytes 221192 | tf_op jit(solution)/shard_map/ppermute | solution.py:431
  19.0 2.0 %collective-permute-start.6 = (f32[72,256]{1,0:T(8,128)S(1)}, f32[72,256]{1,0:T(8,128)S(1)}, u32[]{:S(2)}, u32[]{:S(2)}) collective-permute-start(f32[72,256]{1,0:T(8,128)S(1)} %slice_add_fusion.own), channel_id=1, source_target_pairs={{2,0},{0,2},{6,4},{4,6},{10,8},{8,10},{14,12},{12,14},{3,1},{1,3},... | collective-permute-start | bytes 221192 | tf_op jit(solution)/shard_map/ppermute | solution.py:431
  21.0 0.0 collective-permute-done.9.refs_3_
  21.0 0.0 collective-permute-start.13
  21.0 2.3 %collective-permute-done.8.refs_2_ = f32[72,256]{1,0:T(8,128)S(1)} collective-permute-done((f32[72,256]{1,0:T(8,128)S(1)}, f32[72,256]{1,0:T(8,128)S(1)}, u32[]{:S(2)}, u32[]{:S(2)}) %collective-permute-start.8) | collective-permute-done | bytes 73760 | tf_op jit(solution)/shard_map/ppermute | solution.py:431
  23.3 0.0 collective-permute-start.12
  23.3 0.0 collective-permute-done.7.refs_1_
  23.3 1.4 %collective-permute-start.11 = (f32[72,256]{1,0:T(8,128)S(1)}, f32[72,256]{1,0:T(8,128)S(1)}, u32[]{:S(2)}, u32[]{:S(2)}) collective-permute-start(f32[72,256]{1,0:T(8,128)S(1)} %collective-permute-done.7.refs_1_), channel_id=1, source_target_pairs={{0,1},{1,0},{2,3},{3,2},{4,5},{5,4},{6,7},{7,6},{8,9},{9,8},{10,11... | collective-permute-start | bytes 221192 | tf_op jit(solution)/shard_map/ppermute | solution.py:432
  24.7 0.1 collective-permute-done.6.refs_0_
  24.8 0.1 collective-permute-start.10
  24.9 0.0 collective-permute-done.13.refs_7_
  24.9 0.0 collective-permute-done.12.refs_6_
  24.9 0.7 %collective-permute-done.11.refs_5_ = f32[72,256]{1,0:T(8,128)S(1)} collective-permute-done((f32[72,256]{1,0:T(8,128)S(1)}, f32[72,256]{1,0:T(8,128)S(1)}, u32[]{:S(2)}, u32[]{:S(2)}) %collective-permute-start.11) | collective-permute-done | bytes 73760 | tf_op jit(solution)/shard_map/ppermute | solution.py:432
  25.6 0.5 %collective-permute-done.10.refs_4_ = f32[72,256]{1,0:T(8,128)S(1)} collective-permute-done((f32[72,256]{1,0:T(8,128)S(1)}, f32[72,256]{1,0:T(8,128)S(1)}, u32[]{:S(2)}, u32[]{:S(2)}) %collective-permute-start.10) | collective-permute-done | bytes 73760 | tf_op jit(solution)/shard_map/ppermute | solution.py:432
  26.0 0.0 collective-permute-done.5.other_last
  26.0 3.2 %shard_map.106 = (f32[8,4,32,256]{3,2,1,0:T(8,128)}, f32[2,4,32,256]{3,2,1,0:T(8,128)}, f32[32,256]{1,0:T(8,128)}) custom-call(f32[2,4,32,256]{3,2,1,0:T(8,128)S(1)} %get-tuple-element.19.flux, f32[4,32,256]{2,1,0:T(8,128)S(1)} %copy-done.2, f32[3,8,32,256]{3,2,1,0:T(8,128)S(1)} %get-tuple-element.20.nums, f32[8,32,256]{2,1,0:T(8,128)S(1)} %get-tuple-element.24.last, ...), custom_call_target="tpu_custom_call" | custom-call | flops 2000000 | bytes 3997696 | tf_op jit(solution)/shard_map/pallas_call | solution.py:22
  (1 shorter events, 0.0 us)
Async XLA Ops:
  0.6 9.0 %collective-permute-start = (f32[8,4,32,256]{3,2,1,0:T(8,128)}, f32[8,4,32,256]{3,2,1,0:T(8,128)S(1)}, u32[]{:S(2)}, u32[]{:S(2)}) collective-permute-start(f32[8,4,32,256]{3,2,1,0:T(8,128)} %tracer_in.1), channel_id=1, source_target_pairs={{0,1},{1,0},{2,3},{3,2},{4,5},{5,4},{6,7},{7,6},{8,9},{9,8},{10,11... | collective-permute-start | bytes 3145736 | tf_op jit(solution)/shard_map/ppermute | solution.py:407
  1.1 8.5 %collective-permute-start.1 = (f32[4,32,256]{2,1,0:T(8,128)}, f32[4,32,256]{2,1,0:T(8,128)S(1)}, u32[]{:S(2)}, u32[]{:S(2)}) collective-permute-start(f32[4,32,256]{2,1,0:T(8,128)} %mix.3), channel_id=1, source_target_pairs={{0,1},{1,0},{2,3},{3,2},{4,5},{5,4},{6,7},{7,6},{8,9},{9,8},{10,11... | collective-permute-start | bytes 393224 | tf_op jit(solution)/shard_map/ppermute | solution.py:408
  1.2 8.4 %copy-start = (f32[8,4,32,256]{3,2,1,0:T(8,128)S(1)}, f32[8,4,32,256]{3,2,1,0:T(8,128)}, u32[]{:S(2)}) copy-start(f32[8,4,32,256]{3,2,1,0:T(8,128)} %tracer_in.1) | copy-start | bytes 3145732
  1.2 8.4 %copy-start.1 = (f32[8,4,32,256]{3,2,1,0:T(8,128)S(1)}, f32[8,4,32,256]{3,2,1,0:T(8,128)}, u32[]{:S(2)}) copy-start(f32[8,4,32,256]{3,2,1,0:T(8,128)} %cot.1) | copy-start | bytes 3145732
  1.2 8.5 %copy-start.2 = (f32[4,32,256]{2,1,0:T(8,128)S(1)}, f32[4,32,256]{2,1,0:T(8,128)}, u32[]{:S(2)}) copy-start(f32[4,32,256]{2,1,0:T(8,128)} %mix.3) | copy-start | bytes 393220
  1.2 8.5 %copy-start.3 = (f32[2,4,32,256]{3,2,1,0:T(8,128)S(1)}, f32[2,4,32,256]{3,2,1,0:T(8,128)}, u32[]{:S(2)}) copy-start(f32[2,4,32,256]{3,2,1,0:T(8,128)} %velocity_in.1) | copy-start | bytes 786436
  1.2 8.5 %copy-start.4 = (s32[4,32,256]{2,1,0:T(8,128)S(1)}, s32[4,32,256]{2,1,0:T(8,128)}, u32[]{:S(2)}) copy-start(s32[4,32,256]{2,1,0:T(8,128)} %mask_in.1) | copy-start | bytes 393220
  1.2 8.5 %copy-start.5 = (f32[32,256]{1,0:T(8,128)S(1)}, f32[32,256]{1,0:T(8,128)}, u32[]{:S(2)}) copy-start(f32[32,256]{1,0:T(8,128)} %surface_in.1) | copy-start | bytes 98308
  3.2 8.0 %collective-permute-start.2 = (f32[40,256]{1,0:T(8,128)}, f32[40,256]{1,0:T(8,128)S(1)}, u32[]{:S(2)}, u32[]{:S(2)}) collective-permute-start(f32[40,256]{1,0:T(8,128)} %get-tuple-element.17), channel_id=1, source_target_pairs={{2,4},{6,8},{10,12},{4,2},{8,6},{12,10},{3,5},{7,9},{11,13},{5,3},... | collective-permute-start | bytes 122888 | tf_op jit(solution)/shard_map/ppermute | solution.py:409
  3.9 8.0 %copy-start.6 = (f32[32,256]{1,0:T(8,128)S(1)}, f32[32,256]{1,0:T(8,128)}, u32[]{:S(2)}) copy-start(f32[32,256]{1,0:T(8,128)} %surface_cot.1) | copy-start | bytes 98308
  3.9 8.0 %copy-start.7 = (f32[32,256]{1,0:T(8,128)S(1)}, f32[32,256]{1,0:T(8,128)}, u32[]{:S(2)}) copy-start(f32[32,256]{1,0:T(8,128)} %damping.1) | copy-start | bytes 98308
  3.9 8.0 %collective-permute-start.3 = (f32[40,256]{1,0:T(8,128)}, f32[40,256]{1,0:T(8,128)S(1)}, u32[]{:S(2)}, u32[]{:S(2)}) collective-permute-start(f32[40,256]{1,0:T(8,128)} %get-tuple-element.18), channel_id=1, source_target_pairs={{0,2},{4,6},{8,10},{12,14},{2,0},{6,4},{10,8},{14,12},{1,3},{5,7},... | collective-permute-start | bytes 122888 | tf_op jit(solution)/shard_map/ppermute | solution.py:410
  12.0 1.4 %collective-permute-start.4 = (f32[88,256]{1,0:T(8,128)S(1)}, f32[88,256]{1,0:T(8,128)S(1)}, u32[]{:S(2)}, u32[]{:S(2)}) collective-permute-start(f32[88,256]{1,0:T(8,128)S(1)} %get-tuple-element.23), channel_id=1, source_target_pairs={{0,1},{1,0},{2,3},{3,2},{4,5},{5,4},{6,7},{7,6},{8,9},{9,8},{10,11... | collective-permute-start | bytes 270344 | tf_op jit(solution)/shard_map/ppermute | solution.py:423
  13.3 12.7 %collective-permute-start.5 = (f32[8,32,256]{2,1,0:T(8,128)S(1)}, f32[8,32,256]{2,1,0:T(8,128)S(1)}, u32[]{:S(2)}, u32[]{:S(2)}) collective-permute-start(f32[8,32,256]{2,1,0:T(8,128)S(1)} %get-tuple-element.24.last), channel_id=1, source_target_pairs={{0,1},{1,0},{2,3},{3,2},{4,5},{5,4},{6,7},{7,6},{8,9},{9,8},{10,11... | collective-permute-start | bytes 786440 | tf_op jit(solution)/shard_map/ppermute | solution.py:435
  13.6 7.5 %collective-permute-start.9 = (f32[72,256]{1,0:T(8,128)S(1)}, f32[72,256]{1,0:T(8,128)S(1)}, u32[]{:S(2)}, u32[]{:S(2)}) collective-permute-start(f32[72,256]{1,0:T(8,128)S(1)} %slice_add_fusion.own), channel_id=1, source_target_pairs={{12,0},{14,2},{8,4},{10,6},{4,8},{6,10},{0,12},{2,14},{15,1},{13,3... | collective-permute-start | bytes 221192 | tf_op jit(solution)/shard_map/ppermute | solution.py:431
  17.5 5.8 %collective-permute-start.8 = (f32[72,256]{1,0:T(8,128)S(1)}, f32[72,256]{1,0:T(8,128)S(1)}, u32[]{:S(2)}, u32[]{:S(2)}) collective-permute-start(f32[72,256]{1,0:T(8,128)S(1)} %slice_add_fusion.own), channel_id=1, source_target_pairs={{6,0},{4,2},{2,4},{0,6},{14,8},{12,10},{10,12},{8,14},{11,1},{9,3}... | collective-permute-start | bytes 221192 | tf_op jit(solution)/shard_map/ppermute | solution.py:431
  18.2 5.1 %collective-permute-start.7 = (f32[72,256]{1,0:T(8,128)S(1)}, f32[72,256]{1,0:T(8,128)S(1)}, u32[]{:S(2)}, u32[]{:S(2)}) collective-permute-start(f32[72,256]{1,0:T(8,128)S(1)} %slice_add_fusion.own), channel_id=1, source_target_pairs={{4,0},{6,2},{0,4},{2,6},{12,8},{14,10},{8,12},{10,14},{9,1},{11,3}... | collective-permute-start | bytes 221192 | tf_op jit(solution)/shard_map/ppermute | solution.py:431
  19.0 5.8 %collective-permute-start.6 = (f32[72,256]{1,0:T(8,128)S(1)}, f32[72,256]{1,0:T(8,128)S(1)}, u32[]{:S(2)}, u32[]{:S(2)}) collective-permute-start(f32[72,256]{1,0:T(8,128)S(1)} %slice_add_fusion.own), channel_id=1, source_target_pairs={{2,0},{0,2},{6,4},{4,6},{10,8},{8,10},{14,12},{12,14},{3,1},{1,3},... | collective-permute-start | bytes 221192 | tf_op jit(solution)/shard_map/ppermute | solution.py:431
  21.0 3.9 %collective-permute-start.13 = (f32[72,256]{1,0:T(8,128)S(1)}, f32[72,256]{1,0:T(8,128)S(1)}, u32[]{:S(2)}, u32[]{:S(2)}) collective-permute-start(f32[72,256]{1,0:T(8,128)S(1)} %collective-permute-done.9.refs_3_), channel_id=1, source_target_pairs={{0,1},{1,0},{2,3},{3,2},{4,5},{5,4},{6,7},{7,6},{8,9},{9,8},{10,11... | collective-permute-start | bytes 221192 | tf_op jit(solution)/shard_map/ppermute | solution.py:432
  23.3 1.6 %collective-permute-start.12 = (f32[72,256]{1,0:T(8,128)S(1)}, f32[72,256]{1,0:T(8,128)S(1)}, u32[]{:S(2)}, u32[]{:S(2)}) collective-permute-start(f32[72,256]{1,0:T(8,128)S(1)} %collective-permute-done.8.refs_2_), channel_id=1, source_target_pairs={{0,1},{1,0},{2,3},{3,2},{4,5},{5,4},{6,7},{7,6},{8,9},{9,8},{10,11... | collective-permute-start | bytes 221192 | tf_op jit(solution)/shard_map/ppermute | solution.py:432
  23.3 2.3 %collective-permute-start.11 = (f32[72,256]{1,0:T(8,128)S(1)}, f32[72,256]{1,0:T(8,128)S(1)}, u32[]{:S(2)}, u32[]{:S(2)}) collective-permute-start(f32[72,256]{1,0:T(8,128)S(1)} %collective-permute-done.7.refs_1_), channel_id=1, source_target_pairs={{0,1},{1,0},{2,3},{3,2},{4,5},{5,4},{6,7},{7,6},{8,9},{9,8},{10,11... | collective-permute-start | bytes 221192 | tf_op jit(solution)/shard_map/ppermute | solution.py:432
  24.8 1.3 %collective-permute-start.10 = (f32[72,256]{1,0:T(8,128)S(1)}, f32[72,256]{1,0:T(8,128)S(1)}, u32[]{:S(2)}, u32[]{:S(2)}) collective-permute-start(f32[72,256]{1,0:T(8,128)S(1)} %collective-permute-done.6.refs_0_), channel_id=1, source_target_pairs={{0,1},{1,0},{2,3},{3,2},{4,5},{5,4},{6,7},{7,6},{8,9},{9,8},{10,11... | collective-permute-start | bytes 221192 | tf_op jit(solution)/shard_map/ppermute | solution.py:432

commit v6 on v5

--- a/solution.py
+++ b/solution.py
@@ -17,16 +17,18 @@
 HBM = pl.BlockSpec(memory_space=pltpu.HBM)
 
 
-def call(kernel, outs, args, scratch=(), flops=2_000_000, hbm_in=(), hbm_out=(), vmem=40):
+def call(kernel, outs, args, scratch=(), flops=2_000_000, hbm_in=(), hbm_out=(), near=False):
     nbytes = sum(a.size * 4 for a in args) + sum(4 * functools.reduce(lambda p, q: p * q, s) for s in outs)
+    if near:
+        args = [pltpu.with_memory_space_constraint(a, pltpu.HBM) for a in args]
     return pl.pallas_call(
         kernel,
-        out_shape=[jax.ShapeDtypeStruct(s, F32) for s in outs],
+        out_shape=[pltpu.VMEM(s, F32) if near else jax.ShapeDtypeStruct(s, F32) for s in outs],
         in_specs=[HBM if i in hbm_in else VMEM for i in range(len(args))],
         out_specs=[HBM if i in hbm_out else VMEM for i in range(len(outs))],
         scratch_shapes=list(scratch),
         cost_estimate=pl.CostEstimate(flops=flops, bytes_accessed=nbytes, transcendentals=0),
-        compiler_params=pltpu.CompilerParams(vmem_limit_bytes=int(vmem * 1024 * 1024)),
+        compiler_params=pltpu.CompilerParams(vmem_limit_bytes=40 * 1024 * 1024),
     )(*args)
 
 
@@ -400,7 +402,7 @@
             pltpu.SemaphoreType.DMA((6,)),
         ],
         hbm_in=range(6),
-        vmem=56,
+        near=True,
     )
     pairs_a = [(i, i + 1) for i in range(0, tiles - 1, 2)]
     pairs_b = [(i, i + 1) for i in range(1, tiles - 1, 2)]

time: 29.4 us -> 28.6 us (0.973)
  Pallas kernels: 6.68 us -> 6.05 us
    pallas_call x4, Pallas kernels: 6.68 us -> 6.05 us  [call(): pl.pallas_call(kernel, out_shape=[pltpu.VMEM(s, F32) if near else jax.Sha...]
  transfers between devices with their start and end apart: 14 -> 14, of which waited for: 6 -> 6; matrix products, arithmetic and copies ran while one was open for 0% -> 0% of each run, Pallas kernels for 12% -> 10%
where the time goes in v6:
time: 28.6 us; the launch traced here: 28.4 us
  starting transfers between devices  16.3 us (57%)
  Pallas kernels  6.05 us (21%)
  waiting for transfers between devices  5.25 us (18%)
  between operations  0.77 us (3%)
    ppermute x4, starting transfers between devices, body(): got.append(lax.ppermute(own, ('tile', 'depth'), pairs))  7.48 us
    pallas_call x4, Pallas kernels, call(): pl.pallas_call(kernel, out_shape=[pltpu.VMEM(s, F32) if near else jax.Sha...  6.05 us
    ppermute x1, starting transfers between devices, body(): lax.ppermute(edge_a, 'tile', pairs_a + [(b, a) for a, b in pairs_a])  5.78 us
    ppermute x4, waiting for transfers between devices, body(): got.append(lax.ppermute(own, ('tile', 'depth'), pairs))  2.38 us
    ppermute x4, starting transfers between devices, body(): swapped = [lax.ppermute(piece, 'depth', swap) for piece in got]  1.48 us
    ppermute x1, waiting for transfers between devices, body(): swept = lax.ppermute(part, 'depth', swap)  1.28 us
    ppermute x4, waiting for transfers between devices, body(): swapped = [lax.ppermute(piece, 'depth', swap) for piece in got]  1.15 us
    ppermute x1, starting transfers between devices, body(): lax.ppermute(edge_b, 'tile', pairs_b + [(b, a) for a, b in pairs_b])  0.66 us
  transfers between devices with their start and end apart: 14, of which 6 were waited for; matrix products, arithmetic and copies ran while one was open for 0% of the time, Pallas kernels for 10%

profile of v6, /device:TPU:0, one launch (start us, length us, event | category | flops | bytes accessed | tf_op | source)
XLA Modules:
  0.0 28.4 jit_solution(13237351569002705261)
XLA Ops:
  0.6 0.5 %collective-permute-start = (f32[8,4,32,256]{3,2,1,0:T(8,128)}, f32[8,4,32,256]{3,2,1,0:T(8,128)S(1)}, u32[]{:S(2)}, u32[]{:S(2)}) collective-permute-start(f32[8,4,32,256]{3,2,1,0:T(8,128)} %tracer_in.1), channel_id=1, source_target_pairs={{0,1},{1,0},{2,3},{3,2},{4,5},{5,4},{6,7},{7,6},{8,9},{9,8},{10,11... | collective-permute-start | bytes 3145736 | tf_op jit(solution)/shard_map/ppermute | solution.py:409
  1.1 0.1 collective-permute-start.1
  1.2 0.0 copy-start
  1.2 0.0 copy-start.1
  1.2 0.0 copy-start.2
  1.2 0.0 copy-start.3
  1.2 0.0 copy-start.4
  1.2 0.0 copy-start.5
  1.3 1.3 %shard_map.104 = (f32[40,256]{1,0:T(8,128)S(1)}, f32[40,256]{1,0:T(8,128)S(1)}) custom-call(f32[32,32,256]{2,1,0:T(8,128)} %bitcast.1, s32[4,32,256]{2,1,0:T(8,128)} %mask_in.1, f32[32,256]{1,0:T(8,128)} %surface_in.1, f32[8,4,32,256]{3,2,1,0:T(8,128)} %tracer_in.1, f32[4,32,256]{2,1,0:T(8,128)} %mix.3, f32[2,4,32,256]{3,2,1,0:T(8,128)} %velocity_in.1), custom_call_target="tpu_custom_call" | custom-call | flops 2000000 | bytes 2736128 | tf_op jit(solution)/shard_map/pallas_call | solution.py:24
  2.6 0.7 %collective-permute-start.2 = (f32[40,256]{1,0:T(8,128)S(1)}, f32[40,256]{1,0:T(8,128)S(1)}, u32[]{:S(2)}, u32[]{:S(2)}) collective-permute-start(f32[40,256]{1,0:T(8,128)S(1)} %get-tuple-element.17), channel_id=1, source_target_pairs={{2,4},{6,8},{10,12},{4,2},{8,6},{12,10},{3,5},{7,9},{11,13},{5,3},... | collective-permute-start | bytes 122888 | tf_op jit(solution)/shard_map/ppermute | solution.py:411
  3.2 0.0 copy-start.6
  3.2 0.0 copy-start.7
  3.3 5.8 %collective-permute-start.3 = (f32[40,256]{1,0:T(8,128)S(1)}, f32[40,256]{1,0:T(8,128)S(1)}, u32[]{:S(2)}, u32[]{:S(2)}) collective-permute-start(f32[40,256]{1,0:T(8,128)S(1)} %get-tuple-element.18), channel_id=1, source_target_pairs={{0,2},{4,6},{8,10},{12,14},{2,0},{6,4},{10,8},{14,12},{1,3},{5,7},... | collective-permute-start | bytes 122888 | tf_op jit(solution)/shard_map/ppermute | solution.py:412
  9.0 0.0 collective-permute-done.1.other_mix
  9.0 0.0 collective-permute-done.other
  9.0 0.0 copy-done
  9.0 0.0 copy-done.1
  9.1 0.0 copy-done.2
  9.1 0.0 copy-done.3
  9.1 0.0 copy-done.4
  9.1 0.0 copy-done.5
  9.1 1.5 %shard_map.103 = (f32[2,4,32,256]{3,2,1,0:T(8,128)S(1)}, f32[3,8,32,256]{3,2,1,0:T(8,128)S(1)}, f32[8,32,256]{2,1,0:T(8,128)S(1)}, f32[4,32,256]{2,1,0:T(8,128)S(1)}, f32[16,256]{1,0:T(8,128)S(1)}) custom-call(f32[8,4,32,256]{3,2,1,0:T(8,128)S(1)} %copy-done, f32[4,32,256]{2,1,0:T(8,128)S(1)} %copy-done.2, f32[8,4,32,256]{3,2,1,0:T(8,128)S(1)} %copy-done.1, ...), custom_call_target="tpu_custom_call" | custom-call | flops 2000000 | bytes 5292032 | tf_op jit(solution)/shard_map/pallas_call | solution.py:24
  10.6 0.0 collective-permute-done.2.edge_b
  10.6 0.4 %collective-permute-done.3.edge_a = f32[40,256]{1,0:T(8,128)S(1)} collective-permute-done((f32[40,256]{1,0:T(8,128)S(1)}, f32[40,256]{1,0:T(8,128)S(1)}, u32[]{:S(2)}, u32[]{:S(2)}) %collective-permute-start.3) | collective-permute-done | bytes 40992 | tf_op jit(solution)/shard_map/ppermute | solution.py:412
  11.0 0.0 copy-done.6
  11.0 0.0 copy-done.7
  11.0 0.1 shard_map.105
  11.1 0.1 collective-permute-start.4
  11.2 1.3 %collective-permute-done.4.swept = f32[88,256]{1,0:T(8,128)S(1)} collective-permute-done((f32[88,256]{1,0:T(8,128)S(1)}, f32[88,256]{1,0:T(8,128)S(1)}, u32[]{:S(2)}, u32[]{:S(2)}) %collective-permute-start.4) | collective-permute-done | bytes 90144 | tf_op jit(solution)/shard_map/ppermute | solution.py:425
  12.5 0.2 collective-permute-start.5
  12.7 4.0 %collective-permute-start.9 = (f32[72,256]{1,0:T(8,128)S(1)}, f32[72,256]{1,0:T(8,128)S(1)}, u32[]{:S(2)}, u32[]{:S(2)}) collective-permute-start(f32[72,256]{1,0:T(8,128)S(1)} %slice_add_fusion.own), channel_id=1, source_target_pairs={{12,0},{14,2},{8,4},{10,6},{4,8},{6,10},{0,12},{2,14},{15,1},{13,3... | collective-permute-start | bytes 221192 | tf_op jit(solution)/shard_map/ppermute | solution.py:433
  16.7 0.6 %collective-permute-start.8 = (f32[72,256]{1,0:T(8,128)S(1)}, f32[72,256]{1,0:T(8,128)S(1)}, u32[]{:S(2)}, u32[]{:S(2)}) collective-permute-start(f32[72,256]{1,0:T(8,128)S(1)} %slice_add_fusion.own), channel_id=1, source_target_pairs={{6,0},{4,2},{2,4},{0,6},{14,8},{12,10},{10,12},{8,14},{11,1},{9,3}... | collective-permute-start | bytes 221192 | tf_op jit(solution)/shard_map/ppermute | solution.py:433
  17.3 0.8 %collective-permute-start.7 = (f32[72,256]{1,0:T(8,128)S(1)}, f32[72,256]{1,0:T(8,128)S(1)}, u32[]{:S(2)}, u32[]{:S(2)}) collective-permute-start(f32[72,256]{1,0:T(8,128)S(1)} %slice_add_fusion.own), channel_id=1, source_target_pairs={{4,0},{6,2},{0,4},{2,6},{12,8},{14,10},{8,12},{10,14},{9,1},{11,3}... | collective-permute-start | bytes 221192 | tf_op jit(solution)/shard_map/ppermute | solution.py:433
  18.2 2.0 %collective-permute-start.6 = (f32[72,256]{1,0:T(8,128)S(1)}, f32[72,256]{1,0:T(8,128)S(1)}, u32[]{:S(2)}, u32[]{:S(2)}) collective-permute-start(f32[72,256]{1,0:T(8,128)S(1)} %slice_add_fusion.own), channel_id=1, source_target_pairs={{2,0},{0,2},{6,4},{4,6},{10,8},{8,10},{14,12},{12,14},{3,1},{1,3},... | collective-permute-start | bytes 221192 | tf_op jit(solution)/shard_map/ppermute | solution.py:433
  20.2 0.0 collective-permute-done.9.refs_3_
  20.2 0.0 collective-permute-start.13
  20.2 2.3 %collective-permute-done.8.refs_2_ = f32[72,256]{1,0:T(8,128)S(1)} collective-permute-done((f32[72,256]{1,0:T(8,128)S(1)}, f32[72,256]{1,0:T(8,128)S(1)}, u32[]{:S(2)}, u32[]{:S(2)}) %collective-permute-start.8) | collective-permute-done | bytes 73760 | tf_op jit(solution)/shard_map/ppermute | solution.py:433
  22.5 0.0 collective-permute-start.12
  22.5 0.0 collective-permute-done.7.refs_1_
  22.5 1.4 %collective-permute-start.11 = (f32[72,256]{1,0:T(8,128)S(1)}, f32[72,256]{1,0:T(8,128)S(1)}, u32[]{:S(2)}, u32[]{:S(2)}) collective-permute-start(f32[72,256]{1,0:T(8,128)S(1)} %collective-permute-done.7.refs_1_), channel_id=1, source_target_pairs={{0,1},{1,0},{2,3},{3,2},{4,5},{5,4},{6,7},{7,6},{8,9},{9,8},{10,11... | collective-permute-start | bytes 221192 | tf_op jit(solution)/shard_map/ppermute | solution.py:434
  23.8 0.1 collective-permute-done.6.refs_0_
  23.9 0.1 collective-permute-start.10
  24.1 0.0 collective-permute-done.13.refs_7_
  24.1 0.0 collective-permute-done.12.refs_6_
  24.1 0.7 %collective-permute-done.11.refs_5_ = f32[72,256]{1,0:T(8,128)S(1)} collective-permute-done((f32[72,256]{1,0:T(8,128)S(1)}, f32[72,256]{1,0:T(8,128)S(1)}, u32[]{:S(2)}, u32[]{:S(2)}) %collective-permute-start.11) | collective-permute-done | bytes 73760 | tf_op jit(solution)/shard_map/ppermute | solution.py:434
  24.7 0.5 %collective-permute-done.10.refs_4_ = f32[72,256]{1,0:T(8,128)S(1)} collective-permute-done((f32[72,256]{1,0:T(8,128)S(1)}, f32[72,256]{1,0:T(8,128)S(1)}, u32[]{:S(2)}, u32[]{:S(2)}) %collective-permute-start.10) | collective-permute-done | bytes 73760 | tf_op jit(solution)/shard_map/ppermute | solution.py:434
  25.2 0.0 collective-permute-done.5.other_last
  25.2 3.2 %shard_map.106 = (f32[8,4,32,256]{3,2,1,0:T(8,128)}, f32[2,4,32,256]{3,2,1,0:T(8,128)}, f32[32,256]{1,0:T(8,128)}) custom-call(f32[2,4,32,256]{3,2,1,0:T(8,128)S(1)} %get-tuple-element.19.flux, f32[4,32,256]{2,1,0:T(8,128)S(1)} %copy-done.2, f32[3,8,32,256]{3,2,1,0:T(8,128)S(1)} %get-tuple-element.20.nums, f32[8,32,256]{2,1,0:T(8,128)S(1)} %get-tuple-element.24.last, ...), custom_call_target="tpu_custom_call" | custom-call | flops 2000000 | bytes 3997696 | tf_op jit(solution)/shard_map/pallas_call | solution.py:24
  (1 shorter events, 0.0 us)
Async XLA Ops:
  0.6 8.4 %collective-permute-start = (f32[8,4,32,256]{3,2,1,0:T(8,128)}, f32[8,4,32,256]{3,2,1,0:T(8,128)S(1)}, u32[]{:S(2)}, u32[]{:S(2)}) collective-permute-start(f32[8,4,32,256]{3,2,1,0:T(8,128)} %tracer_in.1), channel_id=1, source_target_pairs={{0,1},{1,0},{2,3},{3,2},{4,5},{5,4},{6,7},{7,6},{8,9},{9,8},{10,11... | collective-permute-start | bytes 3145736 | tf_op jit(solution)/shard_map/ppermute | solution.py:409
  1.1 7.9 %collective-permute-start.1 = (f32[4,32,256]{2,1,0:T(8,128)}, f32[4,32,256]{2,1,0:T(8,128)S(1)}, u32[]{:S(2)}, u32[]{:S(2)}) collective-permute-start(f32[4,32,256]{2,1,0:T(8,128)} %mix.3), channel_id=1, source_target_pairs={{0,1},{1,0},{2,3},{3,2},{4,5},{5,4},{6,7},{7,6},{8,9},{9,8},{10,11... | collective-permute-start | bytes 393224 | tf_op jit(solution)/shard_map/ppermute | solution.py:410
  1.2 7.8 %copy-start = (f32[8,4,32,256]{3,2,1,0:T(8,128)S(1)}, f32[8,4,32,256]{3,2,1,0:T(8,128)}, u32[]{:S(2)}) copy-start(f32[8,4,32,256]{3,2,1,0:T(8,128)} %tracer_in.1) | copy-start | bytes 3145732
  1.2 7.8 %copy-start.1 = (f32[8,4,32,256]{3,2,1,0:T(8,128)S(1)}, f32[8,4,32,256]{3,2,1,0:T(8,128)}, u32[]{:S(2)}) copy-start(f32[8,4,32,256]{3,2,1,0:T(8,128)} %cot.1) | copy-start | bytes 3145732
  1.2 7.8 %copy-start.2 = (f32[4,32,256]{2,1,0:T(8,128)S(1)}, f32[4,32,256]{2,1,0:T(8,128)}, u32[]{:S(2)}) copy-start(f32[4,32,256]{2,1,0:T(8,128)} %mix.3) | copy-start | bytes 393220
  1.2 7.8 %copy-start.3 = (f32[2,4,32,256]{3,2,1,0:T(8,128)S(1)}, f32[2,4,32,256]{3,2,1,0:T(8,128)}, u32[]{:S(2)}) copy-start(f32[2,4,32,256]{3,2,1,0:T(8,128)} %velocity_in.1) | copy-start | bytes 786436
  1.2 7.8 %copy-start.4 = (s32[4,32,256]{2,1,0:T(8,128)S(1)}, s32[4,32,256]{2,1,0:T(8,128)}, u32[]{:S(2)}) copy-start(s32[4,32,256]{2,1,0:T(8,128)} %mask_in.1) | copy-start | bytes 393220
  1.2 7.8 %copy-start.5 = (f32[32,256]{1,0:T(8,128)S(1)}, f32[32,256]{1,0:T(8,128)}, u32[]{:S(2)}) copy-start(f32[32,256]{1,0:T(8,128)} %surface_in.1) | copy-start | bytes 98308
  2.6 8.0 %collective-permute-start.2 = (f32[40,256]{1,0:T(8,128)S(1)}, f32[40,256]{1,0:T(8,128)S(1)}, u32[]{:S(2)}, u32[]{:S(2)}) collective-permute-start(f32[40,256]{1,0:T(8,128)S(1)} %get-tuple-element.17), channel_id=1, source_target_pairs={{2,4},{6,8},{10,12},{4,2},{8,6},{12,10},{3,5},{7,9},{11,13},{5,3},... | collective-permute-start | bytes 122888 | tf_op jit(solution)/shard_map/ppermute | solution.py:411
  3.2 7.8 %copy-start.6 = (f32[32,256]{1,0:T(8,128)S(1)}, f32[32,256]{1,0:T(8,128)}, u32[]{:S(2)}) copy-start(f32[32,256]{1,0:T(8,128)} %surface_cot.1) | copy-start | bytes 98308
  3.2 7.8 %copy-start.7 = (f32[32,256]{1,0:T(8,128)S(1)}, f32[32,256]{1,0:T(8,128)}, u32[]{:S(2)}) copy-start(f32[32,256]{1,0:T(8,128)} %damping.1) | copy-start | bytes 98308
  3.3 7.8 %collective-permute-start.3 = (f32[40,256]{1,0:T(8,128)S(1)}, f32[40,256]{1,0:T(8,128)S(1)}, u32[]{:S(2)}, u32[]{:S(2)}) collective-permute-start(f32[40,256]{1,0:T(8,128)S(1)} %get-tuple-element.18), channel_id=1, source_target_pairs={{0,2},{4,6},{8,10},{12,14},{2,0},{6,4},{10,8},{14,12},{1,3},{5,7},... | collective-permute-start | bytes 122888 | tf_op jit(solution)/shard_map/ppermute | solution.py:412
  11.1 1.4 %collective-permute-start.4 = (f32[88,256]{1,0:T(8,128)S(1)}, f32[88,256]{1,0:T(8,128)S(1)}, u32[]{:S(2)}, u32[]{:S(2)}) collective-permute-start(f32[88,256]{1,0:T(8,128)S(1)} %get-tuple-element.23), channel_id=1, source_target_pairs={{0,1},{1,0},{2,3},{3,2},{4,5},{5,4},{6,7},{7,6},{8,9},{9,8},{10,11... | collective-permute-start | bytes 270344 | tf_op jit(solution)/shard_map/ppermute | solution.py:425
  12.5 12.7 %collective-permute-start.5 = (f32[8,32,256]{2,1,0:T(8,128)S(1)}, f32[8,32,256]{2,1,0:T(8,128)S(1)}, u32[]{:S(2)}, u32[]{:S(2)}) collective-permute-start(f32[8,32,256]{2,1,0:T(8,128)S(1)} %get-tuple-element.24.last), channel_id=1, source_target_pairs={{0,1},{1,0},{2,3},{3,2},{4,5},{5,4},{6,7},{7,6},{8,9},{9,8},{10,11... | collective-permute-start | bytes 786440 | tf_op jit(solution)/shard_map/ppermute | solution.py:437
  12.7 7.5 %collective-permute-start.9 = (f32[72,256]{1,0:T(8,128)S(1)}, f32[72,256]{1,0:T(8,128)S(1)}, u32[]{:S(2)}, u32[]{:S(2)}) collective-permute-start(f32[72,256]{1,0:T(8,128)S(1)} %slice_add_fusion.own), channel_id=1, source_target_pairs={{12,0},{14,2},{8,4},{10,6},{4,8},{6,10},{0,12},{2,14},{15,1},{13,3... | collective-permute-start | bytes 221192 | tf_op jit(solution)/shard_map/ppermute | solution.py:433
  16.7 5.8 %collective-permute-start.8 = (f32[72,256]{1,0:T(8,128)S(1)}, f32[72,256]{1,0:T(8,128)S(1)}, u32[]{:S(2)}, u32[]{:S(2)}) collective-permute-start(f32[72,256]{1,0:T(8,128)S(1)} %slice_add_fusion.own), channel_id=1, source_target_pairs={{6,0},{4,2},{2,4},{0,6},{14,8},{12,10},{10,12},{8,14},{11,1},{9,3}... | collective-permute-start | bytes 221192 | tf_op jit(solution)/shard_map/ppermute | solution.py:433
  17.3 5.1 %collective-permute-start.7 = (f32[72,256]{1,0:T(8,128)S(1)}, f32[72,256]{1,0:T(8,128)S(1)}, u32[]{:S(2)}, u32[]{:S(2)}) collective-permute-start(f32[72,256]{1,0:T(8,128)S(1)} %slice_add_fusion.own), channel_id=1, source_target_pairs={{4,0},{6,2},{0,4},{2,6},{12,8},{14,10},{8,12},{10,14},{9,1},{11,3}... | collective-permute-start | bytes 221192 | tf_op jit(solution)/shard_map/ppermute | solution.py:433
  18.2 5.8 %collective-permute-start.6 = (f32[72,256]{1,0:T(8,128)S(1)}, f32[72,256]{1,0:T(8,128)S(1)}, u32[]{:S(2)}, u32[]{:S(2)}) collective-permute-start(f32[72,256]{1,0:T(8,128)S(1)} %slice_add_fusion.own), channel_id=1, source_target_pairs={{2,0},{0,2},{6,4},{4,6},{10,8},{8,10},{14,12},{12,14},{3,1},{1,3},... | collective-permute-start | bytes 221192 | tf_op jit(solution)/shard_map/ppermute | solution.py:433
  20.2 3.9 %collective-permute-start.13 = (f32[72,256]{1,0:T(8,128)S(1)}, f32[72,256]{1,0:T(8,128)S(1)}, u32[]{:S(2)}, u32[]{:S(2)}) collective-permute-start(f32[72,256]{1,0:T(8,128)S(1)} %collective-permute-done.9.refs_3_), channel_id=1, source_target_pairs={{0,1},{1,0},{2,3},{3,2},{4,5},{5,4},{6,7},{7,6},{8,9},{9,8},{10,11... | collective-permute-start | bytes 221192 | tf_op jit(solution)/shard_map/ppermute | solution.py:434
  22.5 1.6 %collective-permute-start.12 = (f32[72,256]{1,0:T(8,128)S(1)}, f32[72,256]{1,0:T(8,128)S(1)}, u32[]{:S(2)}, u32[]{:S(2)}) collective-permute-start(f32[72,256]{1,0:T(8,128)S(1)} %collective-permute-done.8.refs_2_), channel_id=1, source_target_pairs={{0,1},{1,0},{2,3},{3,2},{4,5},{5,4},{6,7},{7,6},{8,9},{9,8},{10,11... | collective-permute-start | bytes 221192 | tf_op jit(solution)/shard_map/ppermute | solution.py:434
  22.5 2.3 %collective-permute-start.11 = (f32[72,256]{1,0:T(8,128)S(1)}, f32[72,256]{1,0:T(8,128)S(1)}, u32[]{:S(2)}, u32[]{:S(2)}) collective-permute-start(f32[72,256]{1,0:T(8,128)S(1)} %collective-permute-done.7.refs_1_), channel_id=1, source_target_pairs={{0,1},{1,0},{2,3},{3,2},{4,5},{5,4},{6,7},{7,6},{8,9},{9,8},{10,11... | collective-permute-start | bytes 221192 | tf_op jit(solution)/shard_map/ppermute | solution.py:434
  23.9 1.3 %collective-permute-start.10 = (f32[72,256]{1,0:T(8,128)S(1)}, f32[72,256]{1,0:T(8,128)S(1)}, u32[]{:S(2)}, u32[]{:S(2)}) collective-permute-start(f32[72,256]{1,0:T(8,128)S(1)} %collective-permute-done.6.refs_0_), channel_id=1, source_target_pairs={{0,1},{1,0},{2,3},{3,2},{4,5},{5,4},{6,7},{7,6},{8,9},{9,8},{10,11... | collective-permute-start | bytes 221192 | tf_op jit(solution)/shard_map/ppermute | solution.py:434

commit v7 on v6

--- a/solution.py
+++ b/solution.py
@@ -211,9 +211,11 @@
 
 def solve_kernel(tiles, partners, flux, mix, nums, last, delta, other_mix, other_last, swept, own, *refs):
     steps = len(partners)
-    got, swapped = refs[:steps], refs[steps : 2 * steps]
-    adj_tracer_out, adj_velocity, adj_surface = refs[2 * steps : 2 * steps + 3]
-    resid, image, moved, damp, firsts, finals, direc, sol, adj_tracer, sem = refs[2 * steps + 3 :]
+    got, rest = refs[:steps], refs[steps:]
+    swaps = sum(differ(pair) for pair in partners)
+    swapped, rest = iter(rest[:swaps]), rest[swaps:]
+    adj_tracer_out, adj_velocity, adj_surface = rest[:3]
+    resid, image, moved, damp, firsts, finals, direc, sol, adj_tracer, sem = rest[3:]
     levels, rows, cols = flux.shape[1:]
     me = lax.axis_index("tile")
     depth = lax.axis_index("depth")
@@ -254,7 +256,8 @@
     place(own, me)
     for step, (for_top, for_bottom) in enumerate(partners):
         place(got[step], partner(me, jnp.where(depth == 0, for_top, for_bottom), tiles))
-        place(swapped[step], partner(me, jnp.where(depth == 0, for_bottom, for_top), tiles))
+        if differ((for_top, for_bottom)):
+            place(next(swapped), partner(me, jnp.where(depth == 0, for_bottom, for_top), tiles))
 
     column = lax.broadcasted_iota(jnp.int32, (tiles, 128), 1)
 
@@ -374,6 +377,10 @@
     return (offset + tiles - tile) % tiles
 
 
+def differ(pair):
+    return pair[0] != pair[1]
+
+
 def partner_offsets(tiles):
     if tiles & (tiles - 1) == 0:
         others = sorted(range(1, tiles), key=lambda k: (bin(k).count("1"), k))
@@ -431,7 +438,7 @@
         pairs = [(2 * partner(t, for_top, tiles), 2 * t) for t in range(tiles)]
         pairs += [(2 * partner(t, for_bottom, tiles) + 1, 2 * t + 1) for t in range(tiles)]
         got.append(lax.ppermute(own, ("tile", "depth"), pairs))
-    swapped = [lax.ppermute(piece, "depth", swap) for piece in got]
+    swapped = [lax.ppermute(piece, "depth", swap) for piece, pair in zip(got, partners) if differ(pair)]
 
     last_late, _ = lax.optimization_barrier((last, own))
     other_last = lax.ppermute(last_late, "depth", swap)

time: 28.6 us -> 28.1 us (0.983)
  waiting for transfers between devices: 5.25 us -> 4.89 us
    ppermute x4 -> x3, waiting for transfers between devices: 1.15 us -> 0.79 us  [body(): lax.ppermute(piece, 'depth', swap)]
    ppermute x4 -> x3, starting transfers between devices: 1.48 us -> 1.36 us  [body(): lax.ppermute(piece, 'depth', swap)]
  transfers between devices with their start and end apart: 14 -> 13, of which waited for: 6 -> 5; matrix products, arithmetic and copies ran while one was open for 0% -> 0% of each run, Pallas kernels for 10% -> 10%
where the time goes in v7:
time: 28.1 us; the launch traced here: 27.9 us
  starting transfers between devices  16.2 us (58%)
  Pallas kernels  6.03 us (21%)
  waiting for transfers between devices  4.89 us (17%)
  between operations  0.77 us (3%)
    ppermute x4, starting transfers between devices, body(): got.append(lax.ppermute(own, ('tile', 'depth'), pairs))  7.48 us
    pallas_call x4, Pallas kernels, call(): pl.pallas_call(kernel, out_shape=[pltpu.VMEM(s, F32) if near else jax.Sha...  6.03 us
    ppermute x1, starting transfers between devices, body(): lax.ppermute(edge_a, 'tile', pairs_a + [(b, a) for a, b in pairs_a])  5.78 us
    ppermute x4, waiting for transfers between devices, body(): got.append(lax.ppermute(own, ('tile', 'depth'), pairs))  2.38 us
    ppermute x3, starting transfers between devices, body(): lax.ppermute(piece, 'depth', swap)  1.36 us
    ppermute x1, waiting for transfers between devices, body(): swept = lax.ppermute(part, 'depth', swap)  1.28 us
    ppermute x3, waiting for transfers between devices, body(): lax.ppermute(piece, 'depth', swap)  0.79 us
    ppermute x1, starting transfers between devices, body(): lax.ppermute(edge_b, 'tile', pairs_b + [(b, a) for a, b in pairs_b])  0.66 us
  transfers between devices with their start and end apart: 13, of which 5 were waited for; matrix products, arithmetic and copies ran while one was open for 0% of the time, Pallas kernels for 10%

profile of v7, /device:TPU:0, one launch (start us, length us, event | category | flops | bytes accessed | tf_op | source)
XLA Modules:
  0.0 27.9 jit_solution(17526058524889236398)
XLA Ops:
  0.6 0.5 %collective-permute-start = (f32[8,4,32,256]{3,2,1,0:T(8,128)}, f32[8,4,32,256]{3,2,1,0:T(8,128)S(1)}, u32[]{:S(2)}, u32[]{:S(2)}) collective-permute-start(f32[8,4,32,256]{3,2,1,0:T(8,128)} %tracer_in.1), channel_id=1, source_target_pairs={{0,1},{1,0},{2,3},{3,2},{4,5},{5,4},{6,7},{7,6},{8,9},{9,8},{10,11... | collective-permute-start | bytes 3145736 | tf_op jit(solution)/shard_map/ppermute | solution.py:416
  1.1 0.1 collective-permute-start.1
  1.2 0.0 copy-start
  1.2 0.0 copy-start.1
  1.2 0.0 copy-start.2
  1.2 0.0 copy-start.3
  1.2 0.0 copy-start.4
  1.2 0.0 copy-start.5
  1.3 1.3 %shard_map.104 = (f32[40,256]{1,0:T(8,128)S(1)}, f32[40,256]{1,0:T(8,128)S(1)}) custom-call(f32[32,32,256]{2,1,0:T(8,128)} %bitcast.1, s32[4,32,256]{2,1,0:T(8,128)} %mask_in.1, f32[32,256]{1,0:T(8,128)} %surface_in.1, f32[8,4,32,256]{3,2,1,0:T(8,128)} %tracer_in.1, f32[4,32,256]{2,1,0:T(8,128)} %mix.3, f32[2,4,32,256]{3,2,1,0:T(8,128)} %velocity_in.1), custom_call_target="tpu_custom_call" | custom-call | flops 2000000 | bytes 2736128 | tf_op jit(solution)/shard_map/pallas_call | solution.py:24
  2.6 0.7 %collective-permute-start.2 = (f32[40,256]{1,0:T(8,128)S(1)}, f32[40,256]{1,0:T(8,128)S(1)}, u32[]{:S(2)}, u32[]{:S(2)}) collective-permute-start(f32[40,256]{1,0:T(8,128)S(1)} %get-tuple-element.17), channel_id=1, source_target_pairs={{2,4},{6,8},{10,12},{4,2},{8,6},{12,10},{3,5},{7,9},{11,13},{5,3},... | collective-permute-start | bytes 122888 | tf_op jit(solution)/shard_map/ppermute | solution.py:418
  3.2 0.0 copy-start.6
  3.2 0.0 copy-start.7
  3.3 5.8 %collective-permute-start.3 = (f32[40,256]{1,0:T(8,128)S(1)}, f32[40,256]{1,0:T(8,128)S(1)}, u32[]{:S(2)}, u32[]{:S(2)}) collective-permute-start(f32[40,256]{1,0:T(8,128)S(1)} %get-tuple-element.18), channel_id=1, source_target_pairs={{0,2},{4,6},{8,10},{12,14},{2,0},{6,4},{10,8},{14,12},{1,3},{5,7},... | collective-permute-start | bytes 122888 | tf_op jit(solution)/shard_map/ppermute | solution.py:419
  9.0 0.0 collective-permute-done.1.other_mix
  9.0 0.0 collective-permute-done.other
  9.0 0.0 copy-done
  9.0 0.0 copy-done.1
  9.1 0.0 copy-done.2
  9.1 0.0 copy-done.3
  9.1 0.0 copy-done.4
  9.1 0.0 copy-done.5
  9.1 1.5 %shard_map.103 = (f32[2,4,32,256]{3,2,1,0:T(8,128)S(1)}, f32[3,8,32,256]{3,2,1,0:T(8,128)S(1)}, f32[8,32,256]{2,1,0:T(8,128)S(1)}, f32[4,32,256]{2,1,0:T(8,128)S(1)}, f32[16,256]{1,0:T(8,128)S(1)}) custom-call(f32[8,4,32,256]{3,2,1,0:T(8,128)S(1)} %copy-done, f32[4,32,256]{2,1,0:T(8,128)S(1)} %copy-done.2, f32[8,4,32,256]{3,2,1,0:T(8,128)S(1)} %copy-done.1, ...), custom_call_target="tpu_custom_call" | custom-call | flops 2000000 | bytes 5292032 | tf_op jit(solution)/shard_map/pallas_call | solution.py:24
  10.6 0.0 collective-permute-done.2.edge_b
  10.6 0.4 %collective-permute-done.3.edge_a = f32[40,256]{1,0:T(8,128)S(1)} collective-permute-done((f32[40,256]{1,0:T(8,128)S(1)}, f32[40,256]{1,0:T(8,128)S(1)}, u32[]{:S(2)}, u32[]{:S(2)}) %collective-permute-start.3) | collective-permute-done | bytes 40992 | tf_op jit(solution)/shard_map/ppermute | solution.py:419
  11.0 0.0 copy-done.6
  11.0 0.0 copy-done.7
  11.0 0.1 shard_map.105
  11.1 0.1 collective-permute-start.4
  11.2 1.3 %collective-permute-done.4.swept = f32[88,256]{1,0:T(8,128)S(1)} collective-permute-done((f32[88,256]{1,0:T(8,128)S(1)}, f32[88,256]{1,0:T(8,128)S(1)}, u32[]{:S(2)}, u32[]{:S(2)}) %collective-permute-start.4) | collective-permute-done | bytes 90144 | tf_op jit(solution)/shard_map/ppermute | solution.py:432
  12.5 0.2 collective-permute-start.5
  12.7 4.0 %collective-permute-start.9 = (f32[72,256]{1,0:T(8,128)S(1)}, f32[72,256]{1,0:T(8,128)S(1)}, u32[]{:S(2)}, u32[]{:S(2)}) collective-permute-start(f32[72,256]{1,0:T(8,128)S(1)} %slice_add_fusion.own), channel_id=1, source_target_pairs={{12,0},{14,2},{8,4},{10,6},{4,8},{6,10},{0,12},{2,14},{15,1},{13,3... | collective-permute-start | bytes 221192 | tf_op jit(solution)/shard_map/ppermute | solution.py:440
  16.7 0.6 %collective-permute-start.8 = (f32[72,256]{1,0:T(8,128)S(1)}, f32[72,256]{1,0:T(8,128)S(1)}, u32[]{:S(2)}, u32[]{:S(2)}) collective-permute-start(f32[72,256]{1,0:T(8,128)S(1)} %slice_add_fusion.own), channel_id=1, source_target_pairs={{6,0},{4,2},{2,4},{0,6},{14,8},{12,10},{10,12},{8,14},{11,1},{9,3}... | collective-permute-start | bytes 221192 | tf_op jit(solution)/shard_map/ppermute | solution.py:440
  17.3 0.8 %collective-permute-start.7 = (f32[72,256]{1,0:T(8,128)S(1)}, f32[72,256]{1,0:T(8,128)S(1)}, u32[]{:S(2)}, u32[]{:S(2)}) collective-permute-start(f32[72,256]{1,0:T(8,128)S(1)} %slice_add_fusion.own), channel_id=1, source_target_pairs={{4,0},{6,2},{0,4},{2,6},{12,8},{14,10},{8,12},{10,14},{9,1},{11,3}... | collective-permute-start | bytes 221192 | tf_op jit(solution)/shard_map/ppermute | solution.py:440
  18.2 2.0 %collective-permute-start.6 = (f32[72,256]{1,0:T(8,128)S(1)}, f32[72,256]{1,0:T(8,128)S(1)}, u32[]{:S(2)}, u32[]{:S(2)}) collective-permute-start(f32[72,256]{1,0:T(8,128)S(1)} %slice_add_fusion.own), channel_id=1, source_target_pairs={{2,0},{0,2},{6,4},{4,6},{10,8},{8,10},{14,12},{12,14},{3,1},{1,3},... | collective-permute-start | bytes 221192 | tf_op jit(solution)/shard_map/ppermute | solution.py:440
  20.2 0.0 collective-permute-done.9.refs_3_
  20.2 0.0 collective-permute-start.12
  20.2 2.3 %collective-permute-done.8.refs_2_ = f32[72,256]{1,0:T(8,128)S(1)} collective-permute-done((f32[72,256]{1,0:T(8,128)S(1)}, f32[72,256]{1,0:T(8,128)S(1)}, u32[]{:S(2)}, u32[]{:S(2)}) %collective-permute-start.8) | collective-permute-done | bytes 73760 | tf_op jit(solution)/shard_map/ppermute | solution.py:440
  22.5 0.0 collective-permute-start.11
  22.5 0.0 collective-permute-done.7.refs_1_
  22.5 1.4 %collective-permute-start.10 = (f32[72,256]{1,0:T(8,128)S(1)}, f32[72,256]{1,0:T(8,128)S(1)}, u32[]{:S(2)}, u32[]{:S(2)}) collective-permute-start(f32[72,256]{1,0:T(8,128)S(1)} %collective-permute-done.7.refs_1_), channel_id=1, source_target_pairs={{0,1},{1,0},{2,3},{3,2},{4,5},{5,4},{6,7},{7,6},{8,9},{9,8},{10,11... | collective-permute-start | bytes 221192 | tf_op jit(solution)/shard_map/ppermute | solution.py:441
  23.8 0.1 collective-permute-done.6.refs_0_
  23.9 0.0 collective-permute-done.12.refs_6_
  23.9 0.0 collective-permute-done.11.refs_5_
  23.9 0.8 %collective-permute-done.10.refs_4_ = f32[72,256]{1,0:T(8,128)S(1)} collective-permute-done((f32[72,256]{1,0:T(8,128)S(1)}, f32[72,256]{1,0:T(8,128)S(1)}, u32[]{:S(2)}, u32[]{:S(2)}) %collective-permute-start.10) | collective-permute-done | bytes 73760 | tf_op jit(solution)/shard_map/ppermute | solution.py:441
  24.7 0.0 collective-permute-done.5.other_last
  24.7 3.2 %shard_map.106 = (f32[8,4,32,256]{3,2,1,0:T(8,128)}, f32[2,4,32,256]{3,2,1,0:T(8,128)}, f32[32,256]{1,0:T(8,128)}) custom-call(f32[2,4,32,256]{3,2,1,0:T(8,128)S(1)} %get-tuple-element.19.flux, f32[4,32,256]{2,1,0:T(8,128)S(1)} %copy-done.2, f32[3,8,32,256]{3,2,1,0:T(8,128)S(1)} %get-tuple-element.20.nums, f32[8,32,256]{2,1,0:T(8,128)S(1)} %get-tuple-element.24.last, ...), custom_call_target="tpu_custom_call" | custom-call | flops 2000000 | bytes 3923968 | tf_op jit(solution)/shard_map/pallas_call | solution.py:24
  (1 shorter events, 0.0 us)
Async XLA Ops:
  0.6 8.4 %collective-permute-start = (f32[8,4,32,256]{3,2,1,0:T(8,128)}, f32[8,4,32,256]{3,2,1,0:T(8,128)S(1)}, u32[]{:S(2)}, u32[]{:S(2)}) collective-permute-start(f32[8,4,32,256]{3,2,1,0:T(8,128)} %tracer_in.1), channel_id=1, source_target_pairs={{0,1},{1,0},{2,3},{3,2},{4,5},{5,4},{6,7},{7,6},{8,9},{9,8},{10,11... | collective-permute-start | bytes 3145736 | tf_op jit(solution)/shard_map/ppermute | solution.py:416
  1.1 7.9 %collective-permute-start.1 = (f32[4,32,256]{2,1,0:T(8,128)}, f32[4,32,256]{2,1,0:T(8,128)S(1)}, u32[]{:S(2)}, u32[]{:S(2)}) collective-permute-start(f32[4,32,256]{2,1,0:T(8,128)} %mix.3), channel_id=1, source_target_pairs={{0,1},{1,0},{2,3},{3,2},{4,5},{5,4},{6,7},{7,6},{8,9},{9,8},{10,11... | collective-permute-start | bytes 393224 | tf_op jit(solution)/shard_map/ppermute | solution.py:417
  1.2 7.8 %copy-start = (f32[8,4,32,256]{3,2,1,0:T(8,128)S(1)}, f32[8,4,32,256]{3,2,1,0:T(8,128)}, u32[]{:S(2)}) copy-start(f32[8,4,32,256]{3,2,1,0:T(8,128)} %tracer_in.1) | copy-start | bytes 3145732
  1.2 7.8 %copy-start.1 = (f32[8,4,32,256]{3,2,1,0:T(8,128)S(1)}, f32[8,4,32,256]{3,2,1,0:T(8,128)}, u32[]{:S(2)}) copy-start(f32[8,4,32,256]{3,2,1,0:T(8,128)} %cot.1) | copy-start | bytes 3145732
  1.2 7.8 %copy-start.2 = (f32[4,32,256]{2,1,0:T(8,128)S(1)}, f32[4,32,256]{2,1,0:T(8,128)}, u32[]{:S(2)}) copy-start(f32[4,32,256]{2,1,0:T(8,128)} %mix.3) | copy-start | bytes 393220
  1.2 7.8 %copy-start.3 = (f32[2,4,32,256]{3,2,1,0:T(8,128)S(1)}, f32[2,4,32,256]{3,2,1,0:T(8,128)}, u32[]{:S(2)}) copy-start(f32[2,4,32,256]{3,2,1,0:T(8,128)} %velocity_in.1) | copy-start | bytes 786436
  1.2 7.8 %copy-start.4 = (s32[4,32,256]{2,1,0:T(8,128)S(1)}, s32[4,32,256]{2,1,0:T(8,128)}, u32[]{:S(2)}) copy-start(s32[4,32,256]{2,1,0:T(8,128)} %mask_in.1) | copy-start | bytes 393220
  1.2 7.8 %copy-start.5 = (f32[32,256]{1,0:T(8,128)S(1)}, f32[32,256]{1,0:T(8,128)}, u32[]{:S(2)}) copy-start(f32[32,256]{1,0:T(8,128)} %surface_in.1) | copy-start | bytes 98308
  2.6 8.0 %collective-permute-start.2 = (f32[40,256]{1,0:T(8,128)S(1)}, f32[40,256]{1,0:T(8,128)S(1)}, u32[]{:S(2)}, u32[]{:S(2)}) collective-permute-start(f32[40,256]{1,0:T(8,128)S(1)} %get-tuple-element.17), channel_id=1, source_target_pairs={{2,4},{6,8},{10,12},{4,2},{8,6},{12,10},{3,5},{7,9},{11,13},{5,3},... | collective-permute-start | bytes 122888 | tf_op jit(solution)/shard_map/ppermute | solution.py:418
  3.2 7.8 %copy-start.6 = (f32[32,256]{1,0:T(8,128)S(1)}, f32[32,256]{1,0:T(8,128)}, u32[]{:S(2)}) copy-start(f32[32,256]{1,0:T(8,128)} %surface_cot.1) | copy-start | bytes 98308
  3.2 7.8 %copy-start.7 = (f32[32,256]{1,0:T(8,128)S(1)}, f32[32,256]{1,0:T(8,128)}, u32[]{:S(2)}) copy-start(f32[32,256]{1,0:T(8,128)} %damping.1) | copy-start | bytes 98308
  3.3 7.8 %collective-permute-start.3 = (f32[40,256]{1,0:T(8,128)S(1)}, f32[40,256]{1,0:T(8,128)S(1)}, u32[]{:S(2)}, u32[]{:S(2)}) collective-permute-start(f32[40,256]{1,0:T(8,128)S(1)} %get-tuple-element.18), channel_id=1, source_target_pairs={{0,2},{4,6},{8,10},{12,14},{2,0},{6,4},{10,8},{14,12},{1,3},{5,7},... | collective-permute-start | bytes 122888 | tf_op jit(solution)/shard_map/ppermute | solution.py:419
  11.1 1.4 %collective-permute-start.4 = (f32[88,256]{1,0:T(8,128)S(1)}, f32[88,256]{1,0:T(8,128)S(1)}, u32[]{:S(2)}, u32[]{:S(2)}) collective-permute-start(f32[88,256]{1,0:T(8,128)S(1)} %get-tuple-element.23), channel_id=1, source_target_pairs={{0,1},{1,0},{2,3},{3,2},{4,5},{5,4},{6,7},{7,6},{8,9},{9,8},{10,11... | collective-permute-start | bytes 270344 | tf_op jit(solution)/shard_map/ppermute | solution.py:432
  12.5 12.2 %collective-permute-start.5 = (f32[8,32,256]{2,1,0:T(8,128)S(1)}, f32[8,32,256]{2,1,0:T(8,128)S(1)}, u32[]{:S(2)}, u32[]{:S(2)}) collective-permute-start(f32[8,32,256]{2,1,0:T(8,128)S(1)} %get-tuple-element.24.last), channel_id=1, source_target_pairs={{0,1},{1,0},{2,3},{3,2},{4,5},{5,4},{6,7},{7,6},{8,9},{9,8},{10,11... | collective-permute-start | bytes 786440 | tf_op jit(solution)/shard_map/ppermute | solution.py:444
  12.7 7.5 %collective-permute-start.9 = (f32[72,256]{1,0:T(8,128)S(1)}, f32[72,256]{1,0:T(8,128)S(1)}, u32[]{:S(2)}, u32[]{:S(2)}) collective-permute-start(f32[72,256]{1,0:T(8,128)S(1)} %slice_add_fusion.own), channel_id=1, source_target_pairs={{12,0},{14,2},{8,4},{10,6},{4,8},{6,10},{0,12},{2,14},{15,1},{13,3... | collective-permute-start | bytes 221192 | tf_op jit(solution)/shard_map/ppermute | solution.py:440
  16.7 5.8 %collective-permute-start.8 = (f32[72,256]{1,0:T(8,128)S(1)}, f32[72,256]{1,0:T(8,128)S(1)}, u32[]{:S(2)}, u32[]{:S(2)}) collective-permute-start(f32[72,256]{1,0:T(8,128)S(1)} %slice_add_fusion.own), channel_id=1, source_target_pairs={{6,0},{4,2},{2,4},{0,6},{14,8},{12,10},{10,12},{8,14},{11,1},{9,3}... | collective-permute-start | bytes 221192 | tf_op jit(solution)/shard_map/ppermute | solution.py:440
  17.3 5.1 %collective-permute-start.7 = (f32[72,256]{1,0:T(8,128)S(1)}, f32[72,256]{1,0:T(8,128)S(1)}, u32[]{:S(2)}, u32[]{:S(2)}) collective-permute-start(f32[72,256]{1,0:T(8,128)S(1)} %slice_add_fusion.own), channel_id=1, source_target_pairs={{4,0},{6,2},{0,4},{2,6},{12,8},{14,10},{8,12},{10,14},{9,1},{11,3}... | collective-permute-start | bytes 221192 | tf_op jit(solution)/shard_map/ppermute | solution.py:440
  18.2 5.8 %collective-permute-start.6 = (f32[72,256]{1,0:T(8,128)S(1)}, f32[72,256]{1,0:T(8,128)S(1)}, u32[]{:S(2)}, u32[]{:S(2)}) collective-permute-start(f32[72,256]{1,0:T(8,128)S(1)} %slice_add_fusion.own), channel_id=1, source_target_pairs={{2,0},{0,2},{6,4},{4,6},{10,8},{8,10},{14,12},{12,14},{3,1},{1,3},... | collective-permute-start | bytes 221192 | tf_op jit(solution)/shard_map/ppermute | solution.py:440
  20.2 3.7 %collective-permute-start.12 = (f32[72,256]{1,0:T(8,128)S(1)}, f32[72,256]{1,0:T(8,128)S(1)}, u32[]{:S(2)}, u32[]{:S(2)}) collective-permute-start(f32[72,256]{1,0:T(8,128)S(1)} %collective-permute-done.9.refs_3_), channel_id=1, source_target_pairs={{0,1},{1,0},{2,3},{3,2},{4,5},{5,4},{6,7},{7,6},{8,9},{9,8},{10,11... | collective-permute-start | bytes 221192 | tf_op jit(solution)/shard_map/ppermute | solution.py:441
  22.5 1.5 %collective-permute-start.11 = (f32[72,256]{1,0:T(8,128)S(1)}, f32[72,256]{1,0:T(8,128)S(1)}, u32[]{:S(2)}, u32[]{:S(2)}) collective-permute-start(f32[72,256]{1,0:T(8,128)S(1)} %collective-permute-done.8.refs_2_), channel_id=1, source_target_pairs={{0,1},{1,0},{2,3},{3,2},{4,5},{5,4},{6,7},{7,6},{8,9},{9,8},{10,11... | collective-permute-start | bytes 221192 | tf_op jit(solution)/shard_map/ppermute | solution.py:441
  22.5 2.3 %collective-permute-start.10 = (f32[72,256]{1,0:T(8,128)S(1)}, f32[72,256]{1,0:T(8,128)S(1)}, u32[]{:S(2)}, u32[]{:S(2)}) collective-permute-start(f32[72,256]{1,0:T(8,128)S(1)} %collective-permute-done.7.refs_1_), channel_id=1, source_target_pairs={{0,1},{1,0},{2,3},{3,2},{4,5},{5,4},{6,7},{7,6},{8,9},{9,8},{10,11... | collective-permute-start | bytes 221192 | tf_op jit(solution)/shard_map/ppermute | solution.py:441

commit v8 on v7

--- a/solution.py
+++ b/solution.py
@@ -165,7 +165,6 @@
     depth = lax.axis_index("depth")
     odd = lax.rem(lax.axis_index("tile"), 2) == 1
     row = lax.broadcasted_iota(jnp.int32, (rows, cols), 0)
-    kind = lax.broadcasted_iota(jnp.int32, (8, cols), 0)
 
     def halo(at, size):
         from_a, from_b = edge_a[pl.ds(at, size)], edge_b[pl.ds(at, size)]
@@ -188,9 +187,21 @@
     down, up = row_shifts(col_y, 0.0, 0.0)
     top = depth == 0
     source = GRAVITY * (right - left + down - up)
-    send[0:rows] = source + jnp.where(top, surface_cot[...], 0.0)
-    send[rows : rows + 8] = jnp.where(kind == 0, col_y[0:1], jnp.where(kind == 1, col_y[rows - 1 : rows], 0.0))
-    send[rows + 8 : 2 * rows + 8] = jnp.where(top, damping[...], 0.0)
+    source = source + jnp.where(top, surface_cot[...], 0.0)
+    weight = jnp.where(top, damping[...], 0.0)
+    parts = cols // 128
+    for h in range(parts):
+        lane = slice(128 * h, 128 * (h + 1))
+        send[h * rows : (h + 1) * rows] = source[:, lane]
+        send[(parts + h) * rows : (parts + h + 1) * rows] = weight[:, lane]
+    at = 2 * parts * rows
+    kind = lax.broadcasted_iota(jnp.int32, (8, 128), 0)
+    ends = jnp.zeros((8, 128), F32)
+    for h in range(parts):
+        lane = slice(128 * h, 128 * (h + 1))
+        ends = jnp.where(kind == h, col_y[0:1, lane], ends)
+        ends = jnp.where(kind == parts + h, col_y[rows - 1 : rows, lane], ends)
+    send[at : at + 8] = ends
 
     low_s, high_s = halo(levels * tracers, 8)
     low_s, high_s = ADVECT * GRAVITY * low_s[0:1], ADVECT * GRAVITY * high_s[0:1]
@@ -205,8 +216,11 @@
             final = final + lines[3 * levels + j - 1 : 3 * levels + j] * delta[1, j - 1]
         delta[0, j] = first
         delta[1, j] = final
-    send[2 * rows + 8 : 2 * rows + 8 + tracers] = delta[0, levels - 1]
-    send[2 * rows + 8 + tracers : 2 * rows + 8 + 2 * tracers] = delta[1, levels - 1]
+    at = 2 * parts * rows + 8
+    for side in range(2):
+        for h in range(parts):
+            send[at : at + tracers] = delta[side, levels - 1, :, 128 * h : 128 * (h + 1)]
+            at += tracers
 
 
 def solve_kernel(tiles, partners, flux, mix, nums, last, delta, other_mix, other_last, swept, own, *refs):
@@ -225,15 +239,19 @@
     _, _, other_rest = chain(other_mix, 1 - depth)
     own_w, other_w = meet(rest, other_rest, mix[levels - 1], other_mix[levels - 1], depth)
     row = lax.broadcasted_iota(jnp.int32, (rows, cols), 0)
-    far = 2 * rows + 8
+    parts = cols // 128
+    far = 2 * parts * rows + 8
 
     def with_rows(block, first, final):
         return block + (jnp.where(row == 0, first, 0.0) + jnp.where(row == rows - 1, final, 0.0))
 
     for tr in range(tracers):
         num = with_rows(last[tr], delta[0, levels - 1, tr : tr + 1], delta[1, levels - 1, tr : tr + 1])
-        at = far + tr
-        other_num = with_rows(other_last[tr], swept[at : at + 1], swept[at + tracers : at + tracers + 1])
+        first, final = [
+            jnp.concatenate([swept[at + h * tracers : at + h * tracers + 1] for h in range(parts)], axis=1)
+            for at in (far + tr, far + parts * tracers + tr)
+        ]
+        other_num = with_rows(other_last[tr], first, final)
         value = own_w * num + other_w * other_num
         adj_tracer[tr, level(levels - 1, depth, levels)] = value
         for j in range(levels - 2, -1, -1):
@@ -243,15 +261,14 @@
     copy_out = pltpu.make_async_copy(adj_tracer, adj_tracer_out, sem)
     copy_out.start()
 
-    parts = cols // 128
-    lanes = [slice(128 * h, 128 * (h + 1)) for h in range(parts)]
+    ends = 2 * parts * rows
 
     def place(ref, tile):
-        for h, lane in enumerate(lanes):
-            resid[h, pl.ds(tiles + tile, rows, stride=tiles)] = ref[0:rows, lane]
-            damp[h, pl.ds(tile, rows, stride=tiles)] = 4.0 + ref[rows + 8 : 2 * rows + 8, lane]
-            firsts[h, pl.ds(tile, 1)] = ref[rows : rows + 1, lane]
-            finals[h, pl.ds(tile, 1)] = ref[rows + 1 : rows + 2, lane]
+        for h in range(parts):
+            resid[h, pl.ds(tiles + tile, rows, stride=tiles)] = ref[h * rows : (h + 1) * rows]
+            damp[h, pl.ds(tile, rows, stride=tiles)] = 4.0 + ref[(parts + h) * rows : (parts + h + 1) * rows]
+            firsts[h, pl.ds(tile, 1)] = ref[ends + h : ends + h + 1]
+            finals[h, pl.ds(tile, 1)] = ref[ends + parts + h : ends + parts + h + 1]
 
     place(own, me)
     for step, (for_top, for_bottom) in enumerate(partners):
@@ -417,7 +434,8 @@
     other_mix = lax.ppermute(mixing, "depth", swap)
     edge_b = lax.ppermute(edge_b, "tile", pairs_b + [(b, a) for a, b in pairs_b])
     edge_a = lax.ppermute(edge_a, "tile", pairs_a + [(b, a) for a, b in pairs_a])
-    planes = tracers * levels
+    planes, parts = tracers * levels, cols // 128
+    share = 2 * parts * rows + 8
     flux, nums, last, packed, lines = call(
         interior_kernel,
         [(2, levels) + plane, (levels - 1, tracers) + plane, (tracers,) + plane, (4, planes, cols), (4 * levels, cols)],
@@ -426,11 +444,11 @@
     )
     flux, delta, part = call(
         column_kernel,
-        [(2, levels) + plane, (2, levels, tracers, cols), (2 * rows + 8 + 2 * tracers, cols)],
+        [(2, levels) + plane, (2, levels, tracers, cols), (share + 2 * parts * tracers, 128)],
         [flux, packed, lines, edge_b, edge_a, surface_cot, damping],
     )
     swept = lax.ppermute(part, "depth", swap)
-    own = part[: 2 * rows + 8] + swept[: 2 * rows + 8]
+    own = part[:share] + swept[:share]
 
     partners = partner_offsets(tiles)
     got = []

time: 28.1 us -> 27.7 us (0.986)
  starting transfers between devices: 16.2 us -> 15.5 us
    ppermute x3, starting transfers between devices: 1.36 us -> 0.73 us  [body(): lax.ppermute(piece, 'depth', swap)]
    ppermute x4, waiting for transfers between devices: 2.38 us -> 2.73 us  [body(): got.append(lax.ppermute(own, ('tile', 'depth'), pairs))]
  transfers between devices with their start and end apart: 13 -> 13, of which waited for: 5 -> 6; matrix products, arithmetic and copies ran while one was open for 0% -> 0% of each run, Pallas kernels for 10% -> 10%
where the time goes in v8:
time: 27.7 us; the launch traced here: 27.5 us
  starting transfers between devices  15.5 us (56%)
  Pallas kernels  6.04 us (22%)
  waiting for transfers between devices  5.16 us (19%)
  between operations  0.77 us (3%)
    ppermute x4, starting transfers between devices, body(): got.append(lax.ppermute(own, ('tile', 'depth'), pairs))  7.48 us
    pallas_call x4, Pallas kernels, call(): pl.pallas_call(kernel, out_shape=[pltpu.VMEM(s, F32) if near else jax.Sha...  6.04 us
    ppermute x1, starting transfers between devices, body(): lax.ppermute(edge_a, 'tile', pairs_a + [(b, a) for a, b in pairs_a])  5.78 us
    ppermute x4, waiting for transfers between devices, body(): got.append(lax.ppermute(own, ('tile', 'depth'), pairs))  2.73 us
    ppermute x1, waiting for transfers between devices, body(): swept = lax.ppermute(part, 'depth', swap)  1.27 us
    ppermute x3, starting transfers between devices, body(): lax.ppermute(piece, 'depth', swap)  0.73 us
    ppermute x3, waiting for transfers between devices, body(): lax.ppermute(piece, 'depth', swap)  0.71 us
    ppermute x1, starting transfers between devices, body(): lax.ppermute(edge_b, 'tile', pairs_b + [(b, a) for a, b in pairs_b])  0.66 us
  transfers between devices with their start and end apart: 13, of which 6 were waited for; matrix products, arithmetic and copies ran while one was open for 0% of the time, Pallas kernels for 10%

profile of v8, /device:TPU:0, one launch (start us, length us, event | category | flops | bytes accessed | tf_op | source)
XLA Modules:
  0.0 27.5 jit_solution(7422384654788927320)
XLA Ops:
  0.6 0.5 %collective-permute-start = (f32[8,4,32,256]{3,2,1,0:T(8,128)}, f32[8,4,32,256]{3,2,1,0:T(8,128)S(1)}, u32[]{:S(2)}, u32[]{:S(2)}) collective-permute-start(f32[8,4,32,256]{3,2,1,0:T(8,128)} %tracer_in.1), channel_id=1, source_target_pairs={{0,1},{1,0},{2,3},{3,2},{4,5},{5,4},{6,7},{7,6},{8,9},{9,8},{10,11... | collective-permute-start | bytes 3145736 | tf_op jit(solution)/shard_map/ppermute | solution.py:433
  1.1 0.1 collective-permute-start.1
  1.2 0.0 copy-start
  1.2 0.0 copy-start.1
  1.2 0.0 copy-start.2
  1.2 0.0 copy-start.3
  1.2 0.0 copy-start.4
  1.2 0.0 copy-start.5
  1.3 1.3 %shard_map.104 = (f32[40,256]{1,0:T(8,128)S(1)}, f32[40,256]{1,0:T(8,128)S(1)}) custom-call(f32[32,32,256]{2,1,0:T(8,128)} %bitcast.1, s32[4,32,256]{2,1,0:T(8,128)} %mask_in.1, f32[32,256]{1,0:T(8,128)} %surface_in.1, f32[8,4,32,256]{3,2,1,0:T(8,128)} %tracer_in.1, f32[4,32,256]{2,1,0:T(8,128)} %mix.3, f32[2,4,32,256]{3,2,1,0:T(8,128)} %velocity_in.1), custom_call_target="tpu_custom_call" | custom-call | flops 2000000 | bytes 2736128 | tf_op jit(solution)/shard_map/pallas_call | solution.py:24
  2.6 0.7 %collective-permute-start.2 = (f32[40,256]{1,0:T(8,128)S(1)}, f32[40,256]{1,0:T(8,128)S(1)}, u32[]{:S(2)}, u32[]{:S(2)}) collective-permute-start(f32[40,256]{1,0:T(8,128)S(1)} %get-tuple-element.17), channel_id=1, source_target_pairs={{2,4},{6,8},{10,12},{4,2},{8,6},{12,10},{3,5},{7,9},{11,13},{5,3},... | collective-permute-start | bytes 122888 | tf_op jit(solution)/shard_map/ppermute | solution.py:435
  3.2 0.0 copy-start.6
  3.2 0.0 copy-start.7
  3.3 5.8 %collective-permute-start.3 = (f32[40,256]{1,0:T(8,128)S(1)}, f32[40,256]{1,0:T(8,128)S(1)}, u32[]{:S(2)}, u32[]{:S(2)}) collective-permute-start(f32[40,256]{1,0:T(8,128)S(1)} %get-tuple-element.18), channel_id=1, source_target_pairs={{0,2},{4,6},{8,10},{12,14},{2,0},{6,4},{10,8},{14,12},{1,3},{5,7},... | collective-permute-start | bytes 122888 | tf_op jit(solution)/shard_map/ppermute | solution.py:436
  9.0 0.0 collective-permute-done.1.other_mix
  9.0 0.0 collective-permute-done.other
  9.0 0.0 copy-done
  9.0 0.0 copy-done.1
  9.1 0.0 copy-done.2
  9.1 0.0 copy-done.3
  9.1 0.0 copy-done.4
  9.1 0.0 copy-done.5
  9.1 1.5 %shard_map.103 = (f32[2,4,32,256]{3,2,1,0:T(8,128)S(1)}, f32[3,8,32,256]{3,2,1,0:T(8,128)S(1)}, f32[8,32,256]{2,1,0:T(8,128)S(1)}, f32[4,32,256]{2,1,0:T(8,128)S(1)}, f32[16,256]{1,0:T(8,128)S(1)}) custom-call(f32[8,4,32,256]{3,2,1,0:T(8,128)S(1)} %copy-done, f32[4,32,256]{2,1,0:T(8,128)S(1)} %copy-done.2, f32[8,4,32,256]{3,2,1,0:T(8,128)S(1)} %copy-done.1, ...), custom_call_target="tpu_custom_call" | custom-call | flops 2000000 | bytes 5292032 | tf_op jit(solution)/shard_map/pallas_call | solution.py:24
  10.6 0.0 collective-permute-done.2.edge_b
  10.6 0.4 %collective-permute-done.3.edge_a = f32[40,256]{1,0:T(8,128)S(1)} collective-permute-done((f32[40,256]{1,0:T(8,128)S(1)}, f32[40,256]{1,0:T(8,128)S(1)}, u32[]{:S(2)}, u32[]{:S(2)}) %collective-permute-start.3) | collective-permute-done | bytes 40992 | tf_op jit(solution)/shard_map/ppermute | solution.py:436
  11.0 0.0 copy-done.6
  11.0 0.0 copy-done.7
  11.0 0.1 shard_map.105
  11.1 0.1 collective-permute-start.4
  11.2 1.3 %collective-permute-done.4.swept = f32[168,128]{1,0:T(8,128)S(1)} collective-permute-done((f32[168,128]{1,0:T(8,128)S(1)}, f32[168,128]{1,0:T(8,128)S(1)}, u32[]{:S(2)}, u32[]{:S(2)}) %collective-permute-start.4) | collective-permute-done | bytes 86048 | tf_op jit(solution)/shard_map/ppermute | solution.py:450
  12.5 0.2 collective-permute-start.5
  12.7 4.0 %collective-permute-start.9 = (f32[136,128]{1,0:T(8,128)S(1)}, f32[136,128]{1,0:T(8,128)S(1)}, u32[]{:S(2)}, u32[]{:S(2)}) collective-permute-start(f32[136,128]{1,0:T(8,128)S(1)} %slice_add_fusion.own), channel_id=1, source_target_pairs={{12,0},{14,2},{8,4},{10,6},{4,8},{6,10},{0,12},{2,14},{15,1},{13,3... | collective-permute-start | bytes 208904 | tf_op jit(solution)/shard_map/ppermute | solution.py:458
  16.7 0.6 %collective-permute-start.8 = (f32[136,128]{1,0:T(8,128)S(1)}, f32[136,128]{1,0:T(8,128)S(1)}, u32[]{:S(2)}, u32[]{:S(2)}) collective-permute-start(f32[136,128]{1,0:T(8,128)S(1)} %slice_add_fusion.own), channel_id=1, source_target_pairs={{6,0},{4,2},{2,4},{0,6},{14,8},{12,10},{10,12},{8,14},{11,1},{9,3}... | collective-permute-start | bytes 208904 | tf_op jit(solution)/shard_map/ppermute | solution.py:458
  17.3 0.8 %collective-permute-start.7 = (f32[136,128]{1,0:T(8,128)S(1)}, f32[136,128]{1,0:T(8,128)S(1)}, u32[]{:S(2)}, u32[]{:S(2)}) collective-permute-start(f32[136,128]{1,0:T(8,128)S(1)} %slice_add_fusion.own), channel_id=1, source_target_pairs={{4,0},{6,2},{0,4},{2,6},{12,8},{14,10},{8,12},{10,14},{9,1},{11,3}... | collective-permute-start | bytes 208904 | tf_op jit(solution)/shard_map/ppermute | solution.py:458
  18.2 2.0 %collective-permute-start.6 = (f32[136,128]{1,0:T(8,128)S(1)}, f32[136,128]{1,0:T(8,128)S(1)}, u32[]{:S(2)}, u32[]{:S(2)}) collective-permute-start(f32[136,128]{1,0:T(8,128)S(1)} %slice_add_fusion.own), channel_id=1, source_target_pairs={{2,0},{0,2},{6,4},{4,6},{10,8},{8,10},{14,12},{12,14},{3,1},{1,3},... | collective-permute-start | bytes 208904 | tf_op jit(solution)/shard_map/ppermute | solution.py:458
  20.2 0.0 collective-permute-done.9.refs_3_
  20.2 0.0 collective-permute-start.12
  20.2 2.5 %collective-permute-done.8.refs_2_ = f32[136,128]{1,0:T(8,128)S(1)} collective-permute-done((f32[136,128]{1,0:T(8,128)S(1)}, f32[136,128]{1,0:T(8,128)S(1)}, u32[]{:S(2)}, u32[]{:S(2)}) %collective-permute-start.8) | collective-permute-done | bytes 69664 | tf_op jit(solution)/shard_map/ppermute | solution.py:458
  22.7 0.0 collective-permute-start.11
  22.7 0.0 collective-permute-done.7.refs_1_
  22.7 0.7 %collective-permute-start.10 = (f32[136,128]{1,0:T(8,128)S(1)}, f32[136,128]{1,0:T(8,128)S(1)}, u32[]{:S(2)}, u32[]{:S(2)}) collective-permute-start(f32[136,128]{1,0:T(8,128)S(1)} %collective-permute-done.7.refs_1_), channel_id=1, source_target_pairs={{0,1},{1,0},{2,3},{3,2},{4,5},{5,4},{6,7},{7,6},{8,9},{9,8},{10,11... | collective-permute-start | bytes 208904 | tf_op jit(solution)/shard_map/ppermute | solution.py:459
  23.5 0.2 collective-permute-done.6.refs_0_
  23.7 0.0 collective-permute-done.12.refs_6_
  23.7 0.3 %collective-permute-done.11.refs_5_ = f32[136,128]{1,0:T(8,128)S(1)} collective-permute-done((f32[136,128]{1,0:T(8,128)S(1)}, f32[136,128]{1,0:T(8,128)S(1)}, u32[]{:S(2)}, u32[]{:S(2)}) %collective-permute-start.11) | collective-permute-done | bytes 69664 | tf_op jit(solution)/shard_map/ppermute | solution.py:459
  24.0 0.4 %collective-permute-done.10.refs_4_ = f32[136,128]{1,0:T(8,128)S(1)} collective-permute-done((f32[136,128]{1,0:T(8,128)S(1)}, f32[136,128]{1,0:T(8,128)S(1)}, u32[]{:S(2)}, u32[]{:S(2)}) %collective-permute-start.10) | collective-permute-done | bytes 69664 | tf_op jit(solution)/shard_map/ppermute | solution.py:459
  24.4 0.0 collective-permute-done.5.other_last
  24.4 3.2 %shard_map.106 = (f32[8,4,32,256]{3,2,1,0:T(8,128)}, f32[2,4,32,256]{3,2,1,0:T(8,128)}, f32[32,256]{1,0:T(8,128)}) custom-call(f32[2,4,32,256]{3,2,1,0:T(8,128)S(1)} %get-tuple-element.19.flux, f32[4,32,256]{2,1,0:T(8,128)S(1)} %copy-done.2, f32[3,8,32,256]{3,2,1,0:T(8,128)S(1)} %get-tuple-element.20.nums, f32[8,32,256]{2,1,0:T(8,128)S(1)} %get-tuple-element.24.last, ...), custom_call_target="tpu_custom_call" | custom-call | flops 2000000 | bytes 3887104 | tf_op jit(solution)/shard_map/pallas_call | solution.py:24
  (1 shorter events, 0.0 us)
Async XLA Ops:
  0.6 8.4 %collective-permute-start = (f32[8,4,32,256]{3,2,1,0:T(8,128)}, f32[8,4,32,256]{3,2,1,0:T(8,128)S(1)}, u32[]{:S(2)}, u32[]{:S(2)}) collective-permute-start(f32[8,4,32,256]{3,2,1,0:T(8,128)} %tracer_in.1), channel_id=1, source_target_pairs={{0,1},{1,0},{2,3},{3,2},{4,5},{5,4},{6,7},{7,6},{8,9},{9,8},{10,11... | collective-permute-start | bytes 3145736 | tf_op jit(solution)/shard_map/ppermute | solution.py:433
  1.1 7.9 %collective-permute-start.1 = (f32[4,32,256]{2,1,0:T(8,128)}, f32[4,32,256]{2,1,0:T(8,128)S(1)}, u32[]{:S(2)}, u32[]{:S(2)}) collective-permute-start(f32[4,32,256]{2,1,0:T(8,128)} %mix.3), channel_id=1, source_target_pairs={{0,1},{1,0},{2,3},{3,2},{4,5},{5,4},{6,7},{7,6},{8,9},{9,8},{10,11... | collective-permute-start | bytes 393224 | tf_op jit(solution)/shard_map/ppermute | solution.py:434
  1.2 7.8 %copy-start = (f32[8,4,32,256]{3,2,1,0:T(8,128)S(1)}, f32[8,4,32,256]{3,2,1,0:T(8,128)}, u32[]{:S(2)}) copy-start(f32[8,4,32,256]{3,2,1,0:T(8,128)} %tracer_in.1) | copy-start | bytes 3145732
  1.2 7.8 %copy-start.1 = (f32[8,4,32,256]{3,2,1,0:T(8,128)S(1)}, f32[8,4,32,256]{3,2,1,0:T(8,128)}, u32[]{:S(2)}) copy-start(f32[8,4,32,256]{3,2,1,0:T(8,128)} %cot.1) | copy-start | bytes 3145732
  1.2 7.8 %copy-start.2 = (f32[4,32,256]{2,1,0:T(8,128)S(1)}, f32[4,32,256]{2,1,0:T(8,128)}, u32[]{:S(2)}) copy-start(f32[4,32,256]{2,1,0:T(8,128)} %mix.3) | copy-start | bytes 393220
  1.2 7.8 %copy-start.3 = (f32[2,4,32,256]{3,2,1,0:T(8,128)S(1)}, f32[2,4,32,256]{3,2,1,0:T(8,128)}, u32[]{:S(2)}) copy-start(f32[2,4,32,256]{3,2,1,0:T(8,128)} %velocity_in.1) | copy-start | bytes 786436
  1.2 7.8 %copy-start.4 = (s32[4,32,256]{2,1,0:T(8,128)S(1)}, s32[4,32,256]{2,1,0:T(8,128)}, u32[]{:S(2)}) copy-start(s32[4,32,256]{2,1,0:T(8,128)} %mask_in.1) | copy-start | bytes 393220
  1.2 7.8 %copy-start.5 = (f32[32,256]{1,0:T(8,128)S(1)}, f32[32,256]{1,0:T(8,128)}, u32[]{:S(2)}) copy-start(f32[32,256]{1,0:T(8,128)} %surface_in.1) | copy-start | bytes 98308
  2.6 8.0 %collective-permute-start.2 = (f32[40,256]{1,0:T(8,128)S(1)}, f32[40,256]{1,0:T(8,128)S(1)}, u32[]{:S(2)}, u32[]{:S(2)}) collective-permute-start(f32[40,256]{1,0:T(8,128)S(1)} %get-tuple-element.17), channel_id=1, source_target_pairs={{2,4},{6,8},{10,12},{4,2},{8,6},{12,10},{3,5},{7,9},{11,13},{5,3},... | collective-permute-start | bytes 122888 | tf_op jit(solution)/shard_map/ppermute | solution.py:435
  3.2 7.8 %copy-start.6 = (f32[32,256]{1,0:T(8,128)S(1)}, f32[32,256]{1,0:T(8,128)}, u32[]{:S(2)}) copy-start(f32[32,256]{1,0:T(8,128)} %surface_cot.1) | copy-start | bytes 98308
  3.2 7.8 %copy-start.7 = (f32[32,256]{1,0:T(8,128)S(1)}, f32[32,256]{1,0:T(8,128)}, u32[]{:S(2)}) copy-start(f32[32,256]{1,0:T(8,128)} %damping.1) | copy-start | bytes 98308
  3.3 7.8 %collective-permute-start.3 = (f32[40,256]{1,0:T(8,128)S(1)}, f32[40,256]{1,0:T(8,128)S(1)}, u32[]{:S(2)}, u32[]{:S(2)}) collective-permute-start(f32[40,256]{1,0:T(8,128)S(1)} %get-tuple-element.18), channel_id=1, source_target_pairs={{0,2},{4,6},{8,10},{12,14},{2,0},{6,4},{10,8},{14,12},{1,3},{5,7},... | collective-permute-start | bytes 122888 | tf_op jit(solution)/shard_map/ppermute | solution.py:436
  11.1 1.3 %collective-permute-start.4 = (f32[168,128]{1,0:T(8,128)S(1)}, f32[168,128]{1,0:T(8,128)S(1)}, u32[]{:S(2)}, u32[]{:S(2)}) collective-permute-start(f32[168,128]{1,0:T(8,128)S(1)} %get-tuple-element.23), channel_id=1, source_target_pairs={{0,1},{1,0},{2,3},{3,2},{4,5},{5,4},{6,7},{7,6},{8,9},{9,8},{10,11... | collective-permute-start | bytes 258056 | tf_op jit(solution)/shard_map/ppermute | solution.py:450
  12.5 11.9 %collective-permute-start.5 = (f32[8,32,256]{2,1,0:T(8,128)S(1)}, f32[8,32,256]{2,1,0:T(8,128)S(1)}, u32[]{:S(2)}, u32[]{:S(2)}) collective-permute-start(f32[8,32,256]{2,1,0:T(8,128)S(1)} %get-tuple-element.24.last), channel_id=1, source_target_pairs={{0,1},{1,0},{2,3},{3,2},{4,5},{5,4},{6,7},{7,6},{8,9},{9,8},{10,11... | collective-permute-start | bytes 786440 | tf_op jit(solution)/shard_map/ppermute | solution.py:462
  12.7 7.5 %collective-permute-start.9 = (f32[136,128]{1,0:T(8,128)S(1)}, f32[136,128]{1,0:T(8,128)S(1)}, u32[]{:S(2)}, u32[]{:S(2)}) collective-permute-start(f32[136,128]{1,0:T(8,128)S(1)} %slice_add_fusion.own), channel_id=1, source_target_pairs={{12,0},{14,2},{8,4},{10,6},{4,8},{6,10},{0,12},{2,14},{15,1},{13,3... | collective-permute-start | bytes 208904 | tf_op jit(solution)/shard_map/ppermute | solution.py:458
  16.7 6.0 %collective-permute-start.8 = (f32[136,128]{1,0:T(8,128)S(1)}, f32[136,128]{1,0:T(8,128)S(1)}, u32[]{:S(2)}, u32[]{:S(2)}) collective-permute-start(f32[136,128]{1,0:T(8,128)S(1)} %slice_add_fusion.own), channel_id=1, source_target_pairs={{6,0},{4,2},{2,4},{0,6},{14,8},{12,10},{10,12},{8,14},{11,1},{9,3}... | collective-permute-start | bytes 208904 | tf_op jit(solution)/shard_map/ppermute | solution.py:458
  17.3 5.4 %collective-permute-start.7 = (f32[136,128]{1,0:T(8,128)S(1)}, f32[136,128]{1,0:T(8,128)S(1)}, u32[]{:S(2)}, u32[]{:S(2)}) collective-permute-start(f32[136,128]{1,0:T(8,128)S(1)} %slice_add_fusion.own), channel_id=1, source_target_pairs={{4,0},{6,2},{0,4},{2,6},{12,8},{14,10},{8,12},{10,14},{9,1},{11,3}... | collective-permute-start | bytes 208904 | tf_op jit(solution)/shard_map/ppermute | solution.py:458
  18.2 5.5 %collective-permute-start.6 = (f32[136,128]{1,0:T(8,128)S(1)}, f32[136,128]{1,0:T(8,128)S(1)}, u32[]{:S(2)}, u32[]{:S(2)}) collective-permute-start(f32[136,128]{1,0:T(8,128)S(1)} %slice_add_fusion.own), channel_id=1, source_target_pairs={{2,0},{0,2},{6,4},{4,6},{10,8},{8,10},{14,12},{12,14},{3,1},{1,3},... | collective-permute-start | bytes 208904 | tf_op jit(solution)/shard_map/ppermute | solution.py:458
  20.2 3.5 %collective-permute-start.12 = (f32[136,128]{1,0:T(8,128)S(1)}, f32[136,128]{1,0:T(8,128)S(1)}, u32[]{:S(2)}, u32[]{:S(2)}) collective-permute-start(f32[136,128]{1,0:T(8,128)S(1)} %collective-permute-done.9.refs_3_), channel_id=1, source_target_pairs={{0,1},{1,0},{2,3},{3,2},{4,5},{5,4},{6,7},{7,6},{8,9},{9,8},{10,11... | collective-permute-start | bytes 208904 | tf_op jit(solution)/shard_map/ppermute | solution.py:459
  22.7 1.3 %collective-permute-start.11 = (f32[136,128]{1,0:T(8,128)S(1)}, f32[136,128]{1,0:T(8,128)S(1)}, u32[]{:S(2)}, u32[]{:S(2)}) collective-permute-start(f32[136,128]{1,0:T(8,128)S(1)} %collective-permute-done.8.refs_2_), channel_id=1, source_target_pairs={{0,1},{1,0},{2,3},{3,2},{4,5},{5,4},{6,7},{7,6},{8,9},{9,8},{10,11... | collective-permute-start | bytes 208904 | tf_op jit(solution)/shard_map/ppermute | solution.py:459
  22.7 1.6 %collective-permute-start.10 = (f32[136,128]{1,0:T(8,128)S(1)}, f32[136,128]{1,0:T(8,128)S(1)}, u32[]{:S(2)}, u32[]{:S(2)}) collective-permute-start(f32[136,128]{1,0:T(8,128)S(1)} %collective-permute-done.7.refs_1_), channel_id=1, source_target_pairs={{0,1},{1,0},{2,3},{3,2},{4,5},{5,4},{6,7},{7,6},{8,9},{9,8},{10,11... | collective-permute-start | bytes 208904 | tf_op jit(solution)/shard_map/ppermute | solution.py:459

commit v9 on v8

--- a/solution.py
+++ b/solution.py
@@ -458,8 +458,7 @@
         got.append(lax.ppermute(own, ("tile", "depth"), pairs))
     swapped = [lax.ppermute(piece, "depth", swap) for piece, pair in zip(got, partners) if differ(pair)]
 
-    last_late, _ = lax.optimization_barrier((last, own))
-    other_last = lax.ppermute(last_late, "depth", swap)
+    other_last = lax.ppermute(last, "depth", swap)
     return solve_call(
         partners,
         [flux, mixing, nums, last, delta, other_mix, other_last, swept, own] + got + swapped,

time: 27.7 us -> 27.6 us (level)
  waiting for transfers between devices: 5.16 us -> 4.31 us
  starting transfers between devices: 15.5 us -> 16.2 us
    ppermute x1, waiting for transfers between devices: 1.27 us -> 0.77 us  [body(): swept = lax.ppermute(part, 'depth', swap)]
    ppermute x4, waiting for transfers between devices: 2.73 us -> 2.34 us  [body(): got.append(lax.ppermute(own, ('tile', 'depth'), pairs))]
    ppermute x3, starting transfers between devices: 0.73 us -> 1.09 us  [body(): lax.ppermute(piece, 'depth', swap)]
  transfers between devices with their start and end apart: 13 -> 13, of which waited for: 6 -> 5; matrix products, arithmetic and copies ran while one was open for 0% -> 0% of each run, Pallas kernels for 10% -> 10%
where the time goes in v9:
time: 27.6 us; the launch traced here: 27.4 us
  starting transfers between devices  16.2 us (59%)
  Pallas kernels  6.03 us (22%)
  waiting for transfers between devices  4.31 us (16%)
  between operations  0.77 us (3%)
    ppermute x4, starting transfers between devices, body(): got.append(lax.ppermute(own, ('tile', 'depth'), pairs))  7.54 us
    pallas_call x4, Pallas kernels, call(): pl.pallas_call(kernel, out_shape=[pltpu.VMEM(s, F32) if near else jax.Sha...  6.03 us
    ppermute x1, starting transfers between devices, body(): lax.ppermute(edge_a, 'tile', pairs_a + [(b, a) for a, b in pairs_a])  5.78 us
    ppermute x4, waiting for transfers between devices, body(): got.append(lax.ppermute(own, ('tile', 'depth'), pairs))  2.34 us
    ppermute x3, starting transfers between devices, body(): lax.ppermute(piece, 'depth', swap)  1.09 us
    ppermute x1, waiting for transfers between devices, body(): swept = lax.ppermute(part, 'depth', swap)  0.77 us
    ppermute x3, waiting for transfers between devices, body(): lax.ppermute(piece, 'depth', swap)  0.75 us
    ppermute x1, starting transfers between devices, body(): lax.ppermute(edge_b, 'tile', pairs_b + [(b, a) for a, b in pairs_b])  0.66 us
  transfers between devices with their start and end apart: 13, of which 5 were waited for; matrix products, arithmetic and copies ran while one was open for 0% of the time, Pallas kernels for 10%

profile of v9, /device:TPU:0, one launch (start us, length us, event | category | flops | bytes accessed | tf_op | source)
XLA Modules:
  0.0 27.4 jit_solution(4276912618641717592)
XLA Ops:
  0.6 0.5 %collective-permute-start = (f32[8,4,32,256]{3,2,1,0:T(8,128)}, f32[8,4,32,256]{3,2,1,0:T(8,128)S(1)}, u32[]{:S(2)}, u32[]{:S(2)}) collective-permute-start(f32[8,4,32,256]{3,2,1,0:T(8,128)} %tracer_in.1), channel_id=1, source_target_pairs={{0,1},{1,0},{2,3},{3,2},{4,5},{5,4},{6,7},{7,6},{8,9},{9,8},{10,11... | collective-permute-start | bytes 3145736 | tf_op jit(solution)/shard_map/ppermute | solution.py:433
  1.1 0.1 collective-permute-start.1
  1.2 0.0 copy-start
  1.2 0.0 copy-start.1
  1.2 0.0 copy-start.2
  1.2 0.0 copy-start.3
  1.2 0.0 copy-start.4
  1.2 0.0 copy-start.5
  1.3 1.3 %shard_map.104 = (f32[40,256]{1,0:T(8,128)S(1)}, f32[40,256]{1,0:T(8,128)S(1)}) custom-call(f32[32,32,256]{2,1,0:T(8,128)} %bitcast.1, s32[4,32,256]{2,1,0:T(8,128)} %mask_in.1, f32[32,256]{1,0:T(8,128)} %surface_in.1, f32[8,4,32,256]{3,2,1,0:T(8,128)} %tracer_in.1, f32[4,32,256]{2,1,0:T(8,128)} %mix.3, f32[2,4,32,256]{3,2,1,0:T(8,128)} %velocity_in.1), custom_call_target="tpu_custom_call" | custom-call | flops 2000000 | bytes 2736128 | tf_op jit(solution)/shard_map/pallas_call | solution.py:24
  2.6 0.7 %collective-permute-start.2 = (f32[40,256]{1,0:T(8,128)S(1)}, f32[40,256]{1,0:T(8,128)S(1)}, u32[]{:S(2)}, u32[]{:S(2)}) collective-permute-start(f32[40,256]{1,0:T(8,128)S(1)} %get-tuple-element.16), channel_id=1, source_target_pairs={{2,4},{6,8},{10,12},{4,2},{8,6},{12,10},{3,5},{7,9},{11,13},{5,3},... | collective-permute-start | bytes 122888 | tf_op jit(solution)/shard_map/ppermute | solution.py:435
  3.2 0.0 copy-start.6
  3.2 0.0 copy-start.7
  3.3 5.8 %collective-permute-start.3 = (f32[40,256]{1,0:T(8,128)S(1)}, f32[40,256]{1,0:T(8,128)S(1)}, u32[]{:S(2)}, u32[]{:S(2)}) collective-permute-start(f32[40,256]{1,0:T(8,128)S(1)} %get-tuple-element.17), channel_id=1, source_target_pairs={{0,2},{4,6},{8,10},{12,14},{2,0},{6,4},{10,8},{14,12},{1,3},{5,7},... | collective-permute-start | bytes 122888 | tf_op jit(solution)/shard_map/ppermute | solution.py:436
  9.0 0.0 collective-permute-done.1.other_mix
  9.0 0.0 collective-permute-done.other
  9.0 0.0 copy-done
  9.0 0.0 copy-done.1
  9.1 0.0 copy-done.2
  9.1 0.0 copy-done.3
  9.1 0.0 copy-done.4
  9.1 0.0 copy-done.5
  9.1 1.5 %shard_map.103 = (f32[2,4,32,256]{3,2,1,0:T(8,128)S(1)}, f32[3,8,32,256]{3,2,1,0:T(8,128)S(1)}, f32[8,32,256]{2,1,0:T(8,128)S(1)}, f32[4,32,256]{2,1,0:T(8,128)S(1)}, f32[16,256]{1,0:T(8,128)S(1)}) custom-call(f32[8,4,32,256]{3,2,1,0:T(8,128)S(1)} %copy-done, f32[4,32,256]{2,1,0:T(8,128)S(1)} %copy-done.2, f32[8,4,32,256]{3,2,1,0:T(8,128)S(1)} %copy-done.1, ...), custom_call_target="tpu_custom_call" | custom-call | flops 2000000 | bytes 5292032 | tf_op jit(solution)/shard_map/pallas_call | solution.py:24
  10.6 0.0 collective-permute-done.2.edge_b
  10.6 0.4 %collective-permute-done.3.edge_a = f32[40,256]{1,0:T(8,128)S(1)} collective-permute-done((f32[40,256]{1,0:T(8,128)S(1)}, f32[40,256]{1,0:T(8,128)S(1)}, u32[]{:S(2)}, u32[]{:S(2)}) %collective-permute-start.3) | collective-permute-done | bytes 40992 | tf_op jit(solution)/shard_map/ppermute | solution.py:436
  11.0 0.0 copy-done.6
  11.0 0.0 copy-done.7
  11.0 0.1 shard_map.105
  11.1 0.1 collective-permute-start.5
  11.2 0.5 %collective-permute-start.4 = (f32[8,32,256]{2,1,0:T(8,128)S(1)}, f32[8,32,256]{2,1,0:T(8,128)S(1)}, u32[]{:S(2)}, u32[]{:S(2)}) collective-permute-start(f32[8,32,256]{2,1,0:T(8,128)S(1)} %get-tuple-element.20.last), channel_id=1, source_target_pairs={{0,1},{1,0},{2,3},{3,2},{4,5},{5,4},{6,7},{7,6},{8,9},{9,8},{10,11... | collective-permute-start | bytes 786440 | tf_op jit(solution)/shard_map/ppermute | solution.py:461
  11.7 0.8 %collective-permute-done.5.swept = f32[168,128]{1,0:T(8,128)S(1)} collective-permute-done((f32[168,128]{1,0:T(8,128)S(1)}, f32[168,128]{1,0:T(8,128)S(1)}, u32[]{:S(2)}, u32[]{:S(2)}) %collective-permute-start.5) | collective-permute-done | bytes 86048 | tf_op jit(solution)/shard_map/ppermute | solution.py:450
  12.5 4.1 %collective-permute-start.9 = (f32[136,128]{1,0:T(8,128)S(1)}, f32[136,128]{1,0:T(8,128)S(1)}, u32[]{:S(2)}, u32[]{:S(2)}) collective-permute-start(f32[136,128]{1,0:T(8,128)S(1)} %slice_add_fusion.own), channel_id=1, source_target_pairs={{12,0},{14,2},{8,4},{10,6},{4,8},{6,10},{0,12},{2,14},{15,1},{13,3... | collective-permute-start | bytes 208904 | tf_op jit(solution)/shard_map/ppermute | solution.py:458
  16.5 0.6 %collective-permute-start.8 = (f32[136,128]{1,0:T(8,128)S(1)}, f32[136,128]{1,0:T(8,128)S(1)}, u32[]{:S(2)}, u32[]{:S(2)}) collective-permute-start(f32[136,128]{1,0:T(8,128)S(1)} %slice_add_fusion.own), channel_id=1, source_target_pairs={{6,0},{4,2},{2,4},{0,6},{14,8},{12,10},{10,12},{8,14},{11,1},{9,3}... | collective-permute-start | bytes 208904 | tf_op jit(solution)/shard_map/ppermute | solution.py:458
  17.2 0.8 %collective-permute-start.7 = (f32[136,128]{1,0:T(8,128)S(1)}, f32[136,128]{1,0:T(8,128)S(1)}, u32[]{:S(2)}, u32[]{:S(2)}) collective-permute-start(f32[136,128]{1,0:T(8,128)S(1)} %slice_add_fusion.own), channel_id=1, source_target_pairs={{4,0},{6,2},{0,4},{2,6},{12,8},{14,10},{8,12},{10,14},{9,1},{11,3}... | collective-permute-start | bytes 208904 | tf_op jit(solution)/shard_map/ppermute | solution.py:458
  18.0 2.0 %collective-permute-start.6 = (f32[136,128]{1,0:T(8,128)S(1)}, f32[136,128]{1,0:T(8,128)S(1)}, u32[]{:S(2)}, u32[]{:S(2)}) collective-permute-start(f32[136,128]{1,0:T(8,128)S(1)} %slice_add_fusion.own), channel_id=1, source_target_pairs={{2,0},{0,2},{6,4},{4,6},{10,8},{8,10},{14,12},{12,14},{3,1},{1,3},... | collective-permute-start | bytes 208904 | tf_op jit(solution)/shard_map/ppermute | solution.py:458
  20.0 0.0 collective-permute-done.9.refs_3_
  20.0 0.0 collective-permute-start.12
  20.0 2.2 %collective-permute-done.8.refs_2_ = f32[136,128]{1,0:T(8,128)S(1)} collective-permute-done((f32[136,128]{1,0:T(8,128)S(1)}, f32[136,128]{1,0:T(8,128)S(1)}, u32[]{:S(2)}, u32[]{:S(2)}) %collective-permute-start.8) | collective-permute-done | bytes 69664 | tf_op jit(solution)/shard_map/ppermute | solution.py:458
  22.2 0.0 collective-permute-start.11
  22.2 0.0 collective-permute-done.7.refs_1_
  22.2 1.1 %collective-permute-start.10 = (f32[136,128]{1,0:T(8,128)S(1)}, f32[136,128]{1,0:T(8,128)S(1)}, u32[]{:S(2)}, u32[]{:S(2)}) collective-permute-start(f32[136,128]{1,0:T(8,128)S(1)} %collective-permute-done.7.refs_1_), channel_id=1, source_target_pairs={{0,1},{1,0},{2,3},{3,2},{4,5},{5,4},{6,7},{7,6},{8,9},{9,8},{10,11... | collective-permute-start | bytes 208904 | tf_op jit(solution)/shard_map/ppermute | solution.py:459
  23.3 0.2 collective-permute-done.6.refs_0_
  23.5 0.0 collective-permute-done.12.refs_6_
  23.5 0.0 collective-permute-done.11.refs_5_
  23.5 0.7 %collective-permute-done.10.refs_4_ = f32[136,128]{1,0:T(8,128)S(1)} collective-permute-done((f32[136,128]{1,0:T(8,128)S(1)}, f32[136,128]{1,0:T(8,128)S(1)}, u32[]{:S(2)}, u32[]{:S(2)}) %collective-permute-start.10) | collective-permute-done | bytes 69664 | tf_op jit(solution)/shard_map/ppermute | solution.py:459
  24.2 0.0 collective-permute-done.4.other_last
  24.2 3.2 %shard_map.106 = (f32[8,4,32,256]{3,2,1,0:T(8,128)}, f32[2,4,32,256]{3,2,1,0:T(8,128)}, f32[32,256]{1,0:T(8,128)}) custom-call(f32[2,4,32,256]{3,2,1,0:T(8,128)S(1)} %get-tuple-element.18.flux, f32[4,32,256]{2,1,0:T(8,128)S(1)} %copy-done.2, f32[3,8,32,256]{3,2,1,0:T(8,128)S(1)} %get-tuple-element.19.nums, f32[8,32,256]{2,1,0:T(8,128)S(1)} %get-tuple-element.20.last, ...), custom_call_target="tpu_custom_call" | custom-call | flops 2000000 | bytes 3887104 | tf_op jit(solution)/shard_map/pallas_call | solution.py:24
  (1 shorter events, 0.0 us)
Async XLA Ops:
  0.6 8.4 %collective-permute-start = (f32[8,4,32,256]{3,2,1,0:T(8,128)}, f32[8,4,32,256]{3,2,1,0:T(8,128)S(1)}, u32[]{:S(2)}, u32[]{:S(2)}) collective-permute-start(f32[8,4,32,256]{3,2,1,0:T(8,128)} %tracer_in.1), channel_id=1, source_target_pairs={{0,1},{1,0},{2,3},{3,2},{4,5},{5,4},{6,7},{7,6},{8,9},{9,8},{10,11... | collective-permute-start | bytes 3145736 | tf_op jit(solution)/shard_map/ppermute | solution.py:433
  1.1 7.9 %collective-permute-start.1 = (f32[4,32,256]{2,1,0:T(8,128)}, f32[4,32,256]{2,1,0:T(8,128)S(1)}, u32[]{:S(2)}, u32[]{:S(2)}) collective-permute-start(f32[4,32,256]{2,1,0:T(8,128)} %mix.3), channel_id=1, source_target_pairs={{0,1},{1,0},{2,3},{3,2},{4,5},{5,4},{6,7},{7,6},{8,9},{9,8},{10,11... | collective-permute-start | bytes 393224 | tf_op jit(solution)/shard_map/ppermute | solution.py:434
  1.2 7.8 %copy-start = (f32[8,4,32,256]{3,2,1,0:T(8,128)S(1)}, f32[8,4,32,256]{3,2,1,0:T(8,128)}, u32[]{:S(2)}) copy-start(f32[8,4,32,256]{3,2,1,0:T(8,128)} %tracer_in.1) | copy-start | bytes 3145732
  1.2 7.8 %copy-start.1 = (f32[8,4,32,256]{3,2,1,0:T(8,128)S(1)}, f32[8,4,32,256]{3,2,1,0:T(8,128)}, u32[]{:S(2)}) copy-start(f32[8,4,32,256]{3,2,1,0:T(8,128)} %cot.1) | copy-start | bytes 3145732
  1.2 7.8 %copy-start.2 = (f32[4,32,256]{2,1,0:T(8,128)S(1)}, f32[4,32,256]{2,1,0:T(8,128)}, u32[]{:S(2)}) copy-start(f32[4,32,256]{2,1,0:T(8,128)} %mix.3) | copy-start | bytes 393220
  1.2 7.8 %copy-start.3 = (f32[2,4,32,256]{3,2,1,0:T(8,128)S(1)}, f32[2,4,32,256]{3,2,1,0:T(8,128)}, u32[]{:S(2)}) copy-start(f32[2,4,32,256]{3,2,1,0:T(8,128)} %velocity_in.1) | copy-start | bytes 786436
  1.2 7.8 %copy-start.4 = (s32[4,32,256]{2,1,0:T(8,128)S(1)}, s32[4,32,256]{2,1,0:T(8,128)}, u32[]{:S(2)}) copy-start(s32[4,32,256]{2,1,0:T(8,128)} %mask_in.1) | copy-start | bytes 393220
  1.2 7.8 %copy-start.5 = (f32[32,256]{1,0:T(8,128)S(1)}, f32[32,256]{1,0:T(8,128)}, u32[]{:S(2)}) copy-start(f32[32,256]{1,0:T(8,128)} %surface_in.1) | copy-start | bytes 98308
  2.6 8.0 %collective-permute-start.2 = (f32[40,256]{1,0:T(8,128)S(1)}, f32[40,256]{1,0:T(8,128)S(1)}, u32[]{:S(2)}, u32[]{:S(2)}) collective-permute-start(f32[40,256]{1,0:T(8,128)S(1)} %get-tuple-element.16), channel_id=1, source_target_pairs={{2,4},{6,8},{10,12},{4,2},{8,6},{12,10},{3,5},{7,9},{11,13},{5,3},... | collective-permute-start | bytes 122888 | tf_op jit(solution)/shard_map/ppermute | solution.py:435
  3.2 7.8 %copy-start.6 = (f32[32,256]{1,0:T(8,128)S(1)}, f32[32,256]{1,0:T(8,128)}, u32[]{:S(2)}) copy-start(f32[32,256]{1,0:T(8,128)} %surface_cot.1) | copy-start | bytes 98308
  3.2 7.8 %copy-start.7 = (f32[32,256]{1,0:T(8,128)S(1)}, f32[32,256]{1,0:T(8,128)}, u32[]{:S(2)}) copy-start(f32[32,256]{1,0:T(8,128)} %damping.1) | copy-start | bytes 98308
  3.3 7.8 %collective-permute-start.3 = (f32[40,256]{1,0:T(8,128)S(1)}, f32[40,256]{1,0:T(8,128)S(1)}, u32[]{:S(2)}, u32[]{:S(2)}) collective-permute-start(f32[40,256]{1,0:T(8,128)S(1)} %get-tuple-element.17), channel_id=1, source_target_pairs={{0,2},{4,6},{8,10},{12,14},{2,0},{6,4},{10,8},{14,12},{1,3},{5,7},... | collective-permute-start | bytes 122888 | tf_op jit(solution)/shard_map/ppermute | solution.py:436
  11.1 1.3 %collective-permute-start.5 = (f32[168,128]{1,0:T(8,128)S(1)}, f32[168,128]{1,0:T(8,128)S(1)}, u32[]{:S(2)}, u32[]{:S(2)}) collective-permute-start(f32[168,128]{1,0:T(8,128)S(1)} %get-tuple-element.22), channel_id=1, source_target_pairs={{0,1},{1,0},{2,3},{3,2},{4,5},{5,4},{6,7},{7,6},{8,9},{9,8},{10,11... | collective-permute-start | bytes 258056 | tf_op jit(solution)/shard_map/ppermute | solution.py:450
  11.2 13.0 %collective-permute-start.4 = (f32[8,32,256]{2,1,0:T(8,128)S(1)}, f32[8,32,256]{2,1,0:T(8,128)S(1)}, u32[]{:S(2)}, u32[]{:S(2)}) collective-permute-start(f32[8,32,256]{2,1,0:T(8,128)S(1)} %get-tuple-element.20.last), channel_id=1, source_target_pairs={{0,1},{1,0},{2,3},{3,2},{4,5},{5,4},{6,7},{7,6},{8,9},{9,8},{10,11... | collective-permute-start | bytes 786440 | tf_op jit(solution)/shard_map/ppermute | solution.py:461
  12.5 7.5 %collective-permute-start.9 = (f32[136,128]{1,0:T(8,128)S(1)}, f32[136,128]{1,0:T(8,128)S(1)}, u32[]{:S(2)}, u32[]{:S(2)}) collective-permute-start(f32[136,128]{1,0:T(8,128)S(1)} %slice_add_fusion.own), channel_id=1, source_target_pairs={{12,0},{14,2},{8,4},{10,6},{4,8},{6,10},{0,12},{2,14},{15,1},{13,3... | collective-permute-start | bytes 208904 | tf_op jit(solution)/shard_map/ppermute | solution.py:458
  16.5 5.7 %collective-permute-start.8 = (f32[136,128]{1,0:T(8,128)S(1)}, f32[136,128]{1,0:T(8,128)S(1)}, u32[]{:S(2)}, u32[]{:S(2)}) collective-permute-start(f32[136,128]{1,0:T(8,128)S(1)} %slice_add_fusion.own), channel_id=1, source_target_pairs={{6,0},{4,2},{2,4},{0,6},{14,8},{12,10},{10,12},{8,14},{11,1},{9,3}... | collective-permute-start | bytes 208904 | tf_op jit(solution)/shard_map/ppermute | solution.py:458
  17.2 5.1 %collective-permute-start.7 = (f32[136,128]{1,0:T(8,128)S(1)}, f32[136,128]{1,0:T(8,128)S(1)}, u32[]{:S(2)}, u32[]{:S(2)}) collective-permute-start(f32[136,128]{1,0:T(8,128)S(1)} %slice_add_fusion.own), channel_id=1, source_target_pairs={{4,0},{6,2},{0,4},{2,6},{12,8},{14,10},{8,12},{10,14},{9,1},{11,3}... | collective-permute-start | bytes 208904 | tf_op jit(solution)/shard_map/ppermute | solution.py:458
  18.0 5.5 %collective-permute-start.6 = (f32[136,128]{1,0:T(8,128)S(1)}, f32[136,128]{1,0:T(8,128)S(1)}, u32[]{:S(2)}, u32[]{:S(2)}) collective-permute-start(f32[136,128]{1,0:T(8,128)S(1)} %slice_add_fusion.own), channel_id=1, source_target_pairs={{2,0},{0,2},{6,4},{4,6},{10,8},{8,10},{14,12},{12,14},{3,1},{1,3},... | collective-permute-start | bytes 208904 | tf_op jit(solution)/shard_map/ppermute | solution.py:458
  20.0 3.4 %collective-permute-start.12 = (f32[136,128]{1,0:T(8,128)S(1)}, f32[136,128]{1,0:T(8,128)S(1)}, u32[]{:S(2)}, u32[]{:S(2)}) collective-permute-start(f32[136,128]{1,0:T(8,128)S(1)} %collective-permute-done.9.refs_3_), channel_id=1, source_target_pairs={{0,1},{1,0},{2,3},{3,2},{4,5},{5,4},{6,7},{7,6},{8,9},{9,8},{10,11... | collective-permute-start | bytes 208904 | tf_op jit(solution)/shard_map/ppermute | solution.py:459
  22.2 1.3 %collective-permute-start.11 = (f32[136,128]{1,0:T(8,128)S(1)}, f32[136,128]{1,0:T(8,128)S(1)}, u32[]{:S(2)}, u32[]{:S(2)}) collective-permute-start(f32[136,128]{1,0:T(8,128)S(1)} %collective-permute-done.8.refs_2_), channel_id=1, source_target_pairs={{0,1},{1,0},{2,3},{3,2},{4,5},{5,4},{6,7},{7,6},{8,9},{9,8},{10,11... | collective-permute-start | bytes 208904 | tf_op jit(solution)/shard_map/ppermute | solution.py:459
  22.2 2.0 %collective-permute-start.10 = (f32[136,128]{1,0:T(8,128)S(1)}, f32[136,128]{1,0:T(8,128)S(1)}, u32[]{:S(2)}, u32[]{:S(2)}) collective-permute-start(f32[136,128]{1,0:T(8,128)S(1)} %collective-permute-done.7.refs_1_), channel_id=1, source_target_pairs={{0,1},{1,0},{2,3},{3,2},{4,5},{5,4},{6,7},{7,6},{8,9},{9,8},{10,11... | collective-permute-start | bytes 208904 | tf_op jit(solution)/shard_map/ppermute | solution.py:459
